TPU v7x, 32 devices: a whole 2x2x4 slice. The times are simulated.
32 devices in a mesh: groups: 2 (over x), gx: 16 (over z, y, core).
Axes of the slice: x: 2, y: 2, z: 4, core: 2. Of those that a mesh axis runs over, the one named last changes fastest.
Arguments:
- points: float32 [3, 131072], P(None, ('groups', 'gx')), parts along dimension 1, may hold values from 0 to 32
- noise_var: float32 [131072], P(('groups', 'gx')), parts along dimension 0, may hold values from 0.3 to 3
- probes: float32 [16, 131072], P(None, ('groups', 'gx')), parts along dimension 1, may hold values from -6 to 6
- pair_list: int32 [128, 2], P(('groups', 'gx')), parts along dimension 0, may hold values from 0 to 31, as said below
- counts: int32 [32], P(('groups', 'gx')), parts along dimension 0, may hold values from 2 to 4, as said below
Outputs:
- solution: float32 [16, 131072], P(None, ('groups', 'gx')), parts along dimension 1
- residual: float32 [16, 131072], P(None, ('groups', 'gx')), parts along dimension 1
There are 2 independent parts, one for each index of `groups`. A program takes and returns all parts, laid end to end along the dimension named above; each array names one. Nothing has to cross between parts.
Inputs may be any that keep to these rules, and one draw needn't show every extreme that they name: `pair_list`: rows k * 4 to (k + 1) * 4 - 1 belong to device k of gx: the owner is one of its blocks k * 2 to (k + 1) * 2 - 1 and the partner is owner + d with 0 <= d <= 1; the live rows of a device are distinct. `counts`: the live rows lead each device's rows.
All inputs are finite; a program needn't handle non-finite values.
Results may differ from a plain program's by a relative error of at most 0.0043.
Values may be sent and summed in bfloat16 or wider, within the bound.
No kernel may reach another device: no remote copies, remote signals or barrier semaphores. Data moves between devices by JAX's collectives and lax.ppermute only.
A program may use at most 256 MiB of HBM per device.

v0:
```python
import functools

import jax
import jax.numpy as jnp
from jax import lax
from jax.experimental import pallas as pl
from jax.experimental.pallas import tpu as pltpu
from jax.sharding import PartitionSpec as P

BLK = 2048
STRIP = 256
STRIPS = BLK // STRIP
SUB = 128
SUBS = BLK // SUB
OFF_W = 768
OFF_SUBS = OFF_W // SUB
DIAG_W = 512
N_PROBES = 16
N_FEATURES = 64
UNROLL = 2
MIB = 1 << 20

VMEM = pl.BlockSpec(memory_space=pltpu.VMEM)
SMEM = pl.BlockSpec(memory_space=pltpu.SMEM)

f32 = jnp.float32
bf16 = jnp.bfloat16

T_START, T_END, T_EXTRA, T_LIVE = 0, 1, 2, 3


def nt(left, right):
    return lax.dot_general(left, right, (((1,), (1,)), ((), ())), preferred_element_type=f32)


def nn(left, right):
    return jnp.dot(left, right, preferred_element_type=f32)


def split2(value):
    high = value.astype(bf16)
    low = (value - high.astype(f32)).astype(bf16)
    return jnp.concatenate([high, low], axis=0)


def halves(value):
    n = value.shape[0] // 2
    return value[:n] + value[n:]


def split3(value):
    high = value.astype(bf16).astype(f32)
    rest = value - high
    mid = rest.astype(bf16).astype(f32)
    return high, mid, rest - mid


def at(index, size):
    return pl.ds(pl.multiple_of(index * size, size), size)


def one_hot(marked, place):
    parts = []
    for h in range(2):
        hit = jnp.broadcast_to(marked[:, h * SUB : (h + 1) * SUB], (STRIP, SUB)) == place
        parts.append(jnp.where(hit, jnp.ones((STRIP, SUB), bf16), jnp.zeros((STRIP, SUB), bf16)))
    return jnp.concatenate(parts, axis=1)


def places():
    return lax.broadcasted_iota(jnp.int32, (STRIP, SUB), 0).astype(f32).astype(bf16)


def marks(rank, g):
    group = lax.shift_right_logical(rank, 8)
    within = jnp.bitwise_and(rank, STRIP - 1)
    return jnp.where(group == g, within, -1).astype(f32).astype(bf16)


def turned(value):
    shape = (STRIP, STRIP)
    same = lax.broadcasted_iota(jnp.int32, shape, 0) == lax.broadcasted_iota(jnp.int32, shape, 1)
    return nt(jnp.where(same, 1.0, 0.0).astype(bf16), value).astype(bf16)


def fill_ranks(y_row, rank_ref, key_ref, before_ref):
    low = jnp.min(y_row, axis=1, keepdims=True)
    high = jnp.max(y_row, axis=1, keepdims=True)
    scale = 255.0 / jnp.maximum(high - low, 1e-6)
    key_ref[...] = jnp.clip(jnp.floor((y_row - low) * scale), 0.0, 255.0)
    shape = (STRIP, STRIP)
    first = lax.broadcasted_iota(jnp.int32, shape, 0)
    second = lax.broadcasted_iota(jnp.int32, shape, 1)
    upper = jnp.where(first < second, 1.0, 0.0).astype(bf16)
    lower = jnp.where(second < first, 1.0, 0.0).astype(bf16)
    ones = jnp.ones((STRIP, SUB), bf16)
    value = places()
    before_ref[...] = jnp.zeros((STRIP, SUB), f32)

    def count(j, carry):
        before_ref[...] += nn(one_hot(key_ref[:, at(j, STRIP)].astype(bf16), value), ones)
        return carry

    lax.fori_loop(0, STRIPS, count, 0, unroll=2)
    total = before_ref[...]
    coarse = jnp.floor(total * (1.0 / 16.0)) * 16.0
    before_ref[...] = nn(lower, coarse.astype(bf16)) + nn(lower, (total - coarse).astype(bf16))

    def place(j, carry):
        hit = one_hot(key_ref[:, at(j, STRIP)].astype(bf16), value)
        before = before_ref[...]
        ahead = nn(hit, upper) + jnp.concatenate([before, before], axis=1)
        rank = jnp.sum(hit.astype(f32) * ahead, axis=0, keepdims=True)
        rank_ref[:, at(j, STRIP)] = rank.astype(jnp.int32)
        before_ref[...] = before + nn(hit, ones)
        return carry

    lax.fori_loop(0, STRIPS, place, 0)


def plan(row_side, col_side, live, diag):
    y_row = row_side[17:18, :]
    y_col = col_side[17:18, :]
    strips = jnp.concatenate([y_row[:, i * STRIP : (i + 1) * STRIP] for i in range(STRIPS)], axis=0)
    low = jnp.min(strips, axis=1, keepdims=True) - 1.0
    high = jnp.max(strips, axis=1, keepdims=True) + 1.0
    groups = jnp.concatenate([y_col[:, j * SUB : (j + 1) * SUB] for j in range(SUBS)], axis=0)
    own = lax.broadcasted_iota(jnp.int32, (SUBS, SUB), 0) == lax.broadcasted_iota(jnp.int32, (SUBS, SUB), 1)

    def across(value):
        return jnp.sum(jnp.where(own, value, 0.0), axis=0, keepdims=True)

    group_low = across(jnp.min(groups, axis=1, keepdims=True))
    group_high = across(jnp.max(groups, axis=1, keepdims=True))
    lane = lax.broadcasted_iota(jnp.int32, (STRIPS, SUB), 1)
    place = lane.astype(f32)
    reached = (group_low < high) & (group_high > low) & (lane < SUBS)
    end = jnp.max(jnp.where(reached, place + 1.0, 0.0), axis=1, keepdims=True)
    if diag:
        start = lax.broadcasted_iota(jnp.int32, (STRIPS, 1), 0).astype(f32) * 2.0 + (DIAG_W // SUB - OFF_SUBS)
    else:
        first = jnp.min(jnp.where(reached, place, float(SUBS)), axis=1, keepdims=True)
        start = jnp.minimum(first, float(SUBS - OFF_SUBS))
    extra = jnp.sum(jnp.maximum(end - (start + OFF_SUBS), 0.0), axis=0, keepdims=True)
    alive = live.astype(f32)
    table = jnp.where(lane == T_START, start, jnp.where(lane == T_END, end, extra))
    return jnp.where(lane == T_LIVE, alive, table).astype(jnp.int32)


def row_id(width):
    return lax.broadcasted_iota(jnp.int32, (8, width), 0)


def features(offset, left):
    first, second, third = split3(offset)
    norm = jnp.sum(offset * offset, axis=0, keepdims=True)
    n1, n2, n3 = split3(norm)
    ids = row_id(offset.shape[1])
    own, other = (0, 3) if left else (3, 0)
    norms = jnp.where(ids == own, n1, jnp.where(ids == own + 1, n2, jnp.where(ids == own + 2, n3, 0.0)))
    norms = jnp.where((ids >= other) & (ids < other + 3), 1.0, norms)
    if left:
        first, second, third = -2.0 * first, -2.0 * second, -2.0 * third
        parts = [first, first, first, second, second, third]
    else:
        parts = [first, second, third, first, second, first]
    return jnp.concatenate(parts + [norms, jnp.zeros_like(norms)], axis=0), norm


def sort_kernel(
    pts_hbm, nv_hbm, pr_hbm, pair_hbm, count, side, first, lhs, rank, pr_ref, flags, tab,
    pts_ref, nv_ref, pair, plan_ref, key_ref, before_ref, data_ref, rows_ref, sems
):
    copies = [
        pltpu.make_async_copy(src, dst, sems.at[k])
        for k, (src, dst) in enumerate(
            ((pts_hbm, pts_ref), (nv_hbm, nv_ref), (pr_hbm, pr_ref), (pair_hbm, pair))
        )
    ]
    for copy in copies:
        copy.start()
    for copy in copies:
        copy.wait()
    for local in range(2):
        for ahead in range(2):
            flags[2 * local + ahead] = live_flag(pair, count, local, ahead)
    position = lax.shift_right_logical(pair[0, 0], 1)
    flags[4] = jnp.bitwise_and(position, 1)
    flags[5] = jnp.where(position > 0, 1, 0)

    def block(blk, carry):
        cols = at(blk, BLK)
        fill_ranks(pts_ref[1:2, cols], rank.at[blk], key_ref, before_ref)
        aux = jnp.concatenate(
            [pts_ref[0:3, cols] * 2.0, nv_ref[:, cols], jnp.zeros((4, BLK), f32)], axis=0
        )
        data_ref[...] = jnp.concatenate(
            [*split3(pr_ref[:, cols]), *split3(aux), jnp.zeros((8, BLK), f32)], axis=0
        ).astype(bf16)
        centre = 0.5 * (jnp.min(aux, axis=1, keepdims=True) + jnp.max(aux, axis=1, keepdims=True))
        centre = jnp.concatenate([jnp.zeros((4, 1), f32), centre[0:3], jnp.zeros((1, 1), f32)], axis=0)
        place = places()

        def strip(g, carry):
            marked = marks(rank[blk], g)
            got = None
            for c in range(STRIPS):
                here = slice(c * STRIP, (c + 1) * STRIP)
                part = nt(data_ref[:, here], one_hot(marked[:, here], place))
                got = part if got is None else got + part
            side[blk, 0:16, at(g, STRIP)] = (got[0:16] + got[16:32]) + got[32:48]
            side[blk, 16:24, at(g, STRIP)] = ((got[48:56] + got[56:64]) + got[64:72]) + centre
            return carry

        lax.fori_loop(0, STRIPS, strip, 0)
        rows, _ = features(offset_of(side.at[blk], side.at[blk]), True)
        rows_ref[...] = rows.astype(bf16)

        def turn(c, carry):
            lhs[blk, at(c, STRIP), :] = turned(rows_ref[:, at(c, STRIP)])
            return carry

        lax.fori_loop(0, STRIPS, turn, 0, unroll=2)
        return carry

    lax.fori_loop(0, 2, block, 0)
    first[...] = side[0]
    plan_ref[0:8, :] = plan(side.at[0], side.at[0], flags[0], True)
    plan_ref[8:16, :] = plan(side.at[0], side.at[1], flags[1], False)
    plan_ref[16:24, :] = plan(side.at[1], side.at[1], flags[2], True)
    pltpu.sync_copy(plan_ref, tab)


def offset_of(side_ref, centre_ref):
    centre = jnp.concatenate([centre_ref[20:23, 0:1], jnp.zeros((5, 1), f32)], axis=0)
    return jnp.where(row_id(BLK) < 3, side_ref[16:24, :] - centre, 0.0)


def live_flag(pair_ref, count_ref, local, ahead):
    flag = jnp.int32(0)
    for s in range(pair_ref.shape[1]):
        owner = pair_ref[0, s]
        match = (
            (jnp.int32(s) < count_ref[0])
            & (jnp.bitwise_and(owner, 1) == local)
            & (pair_ref[1, s] - owner == ahead)
        )
        flag = jnp.where(match, jnp.int32(1), flag)
    return flag


def kernel_values(squared):
    squared = jnp.maximum(squared, 1e-30)
    t = jnp.maximum(1.0 - squared * lax.rsqrt(squared), 0.0)
    t2 = t * t
    return ((t2 * t2) * (1.25 - t)).astype(bf16)


def tile_by_difference(row_side, row_at, col_side, col_at):
    squared = None
    for axis in range(16, 19):
        mine = jnp.broadcast_to(row_side[axis : axis + 1, pl.ds(row_at, SUB)], (SUB, SUB)).T
        diff = mine - col_side[axis : axis + 1, pl.ds(col_at, SUB)]
        part = diff * diff
        squared = part if squared is None else squared + part
    return kernel_values(squared)


def fast_strip(k_ref, i, lhs, rhs, start, width):
    for h in range(width // STRIP):
        right = rhs[:, pl.ds(pl.multiple_of(start + h * STRIP, SUB), STRIP)]
        for g in range(STRIP // SUB):
            left = lhs[pl.ds(pl.multiple_of(i * STRIP + g * SUB, SUB), SUB), :]
            k_ref[i, g * SUB : (g + 1) * SUB, h * STRIP : (h + 1) * STRIP] = kernel_values(nn(left, right))


def slow_build(k_ref, row_side, col_side, first_group, groups):
    def strip(i, carry):
        def tile(j, carry):
            for g in range(STRIP // SUB):
                at = pl.multiple_of(i * STRIP + g * SUB, SUB)
                col_at = pl.multiple_of(jnp.minimum(first_group(i) + j, SUBS - 1) * SUB, SUB)
                k_ref[i, g * SUB : (g + 1) * SUB, pl.ds(pl.multiple_of(j * SUB, SUB), SUB)] = (
                    tile_by_difference(row_side, at, col_side, col_at)
                )
            return carry

        return lax.fori_loop(0, groups, tile, carry)

    lax.fori_loop(0, STRIPS, strip, 0)


def right_features(rhs, row_side, col_side):
    offset = offset_of(col_side, row_side)
    rows, norm = features(offset, False)
    rhs[...] = rows.astype(bf16)
    offset = offset_of(row_side, row_side)
    return jnp.maximum(jnp.max(norm), jnp.max(jnp.sum(offset * offset, axis=0, keepdims=True))) <= 100.0


def off_pair(k_ref, tab_ref, base, lhs, rhs, row_side, col_side, v_row, v_col, acc_row, acc_col):
    near = right_features(rhs, row_side, col_side)

    @pl.when(near)
    def _():
        def strip(i, carry):
            start = pl.multiple_of(tab_ref[base + i, T_START] * SUB, SUB)
            fast_strip(k_ref, i, lhs, rhs, start, OFF_W)
            owner_strip(k_ref, i, start, v_col, acc_row)
            partner_strip(k_ref, i, start, v_row, acc_col)
            return carry

        lax.fori_loop(0, STRIPS, strip, 0, unroll=UNROLL)

    @pl.when(jnp.logical_not(near))
    def _():
        slow_build(k_ref, row_side, col_side, lambda i: tab_ref[base + i, T_START], OFF_SUBS)
        off_products(k_ref, tab_ref, base, v_row, v_col, acc_row, acc_col)

    return near, lhs, rhs


def diag_pair(k_ref, lhs, rhs, side, v, acc):
    near = right_features(rhs, side, side)

    @pl.when(near)
    def _():
        def strip(i, carry):
            fast_strip(k_ref, i, lhs, rhs, i * STRIP, DIAG_W)
            diag_strip(k_ref, i, v, acc, DIAG_W)
            return carry

        lax.fori_loop(0, STRIPS - 1, strip, 0)
        fast_strip(k_ref, STRIPS - 1, lhs, rhs, (STRIPS - 1) * STRIP, STRIP)
        diag_strip(k_ref, STRIPS - 1, v, acc, STRIP)

    @pl.when(jnp.logical_not(near))
    def _():
        slow_build(k_ref, side, side, lambda i: 2 * i, DIAG_W // SUB)
        diag_products(k_ref, v, acc)


def owner_strip(k_ref, i, start, v_col, acc_row):
    acc_row[:, at(i, STRIP)] += halves(nt(v_col[:, pl.ds(start, OFF_W)], k_ref[i]))


def partner_strip(k_ref, i, start, v_row, acc_col):
    acc_col[:, pl.ds(start, OFF_W)] += halves(nn(v_row[:, at(i, STRIP)], k_ref[i]))


def off_products(k_ref, tab_ref, base, v_row, v_col, acc_row, acc_col):
    def strip(i, carry):
        start = pl.multiple_of(tab_ref[base + i, T_START] * SUB, SUB)
        if acc_row is not None:
            owner_strip(k_ref, i, start, v_col, acc_row)
        if acc_col is not None:
            partner_strip(k_ref, i, start, v_row, acc_col)
        return carry

    lax.fori_loop(0, STRIPS, strip, 0, unroll=UNROLL)


def diag_strip(k_ref, i, v_ref, acc_ref, width):
    start = pl.multiple_of(i * STRIP, STRIP)
    acc_ref[:, at(i, STRIP)] += halves(nt(v_ref[:, pl.ds(start, width)], k_ref[i, :, :width]))
    if width > STRIP:
        acc_ref[:, at(i + 1, STRIP)] += halves(nn(v_ref[:, at(i, STRIP)], k_ref[i, :, STRIP:width]))


def diag_products(k_ref, v_ref, acc_ref):
    def strip(i, carry):
        diag_strip(k_ref, i, v_ref, acc_ref, DIAG_W)
        return carry

    lax.fori_loop(0, STRIPS - 1, strip, 0, unroll=UNROLL)
    diag_strip(k_ref, STRIPS - 1, v_ref, acc_ref, STRIP)


def extra_tiles(
    tab_ref, base, row_side, col_side, tile_ref, v_row, v_col, acc_row, acc_col, kept=None, fill=None
):
    @pl.when(tab_ref[base, T_EXTRA] > 0)
    def _():
        def strip(i, carry):
            here = pl.ds(pl.multiple_of(i * STRIP, STRIP), STRIP)
            first = tab_ref[base + i, T_START] + OFF_SUBS

            def tile(j, carry):
                col_at = pl.multiple_of(j * SUB, SUB)
                there = pl.ds(col_at, SUB)

                def by_difference():
                    for g in range(STRIP // SUB):
                        row_at = pl.multiple_of(i * STRIP + g * SUB, SUB)
                        tile_ref[g * SUB : (g + 1) * SUB, :] = tile_by_difference(row_side, row_at, col_side, col_at)

                if kept is None:
                    by_difference()
                elif fill is None:
                    pl.when(j > first)(by_difference)

                    @pl.when(j == first)
                    def _():
                        tile_ref[...] = kept[i]
                else:
                    near, lhs, rhs = fill
                    pl.when(jnp.logical_not(near))(by_difference)

                    @pl.when(near)
                    def _():
                        tile_ref[...] = kernel_values(nn(lhs[here, :], rhs[:, there]))

                    @pl.when(j == first)
                    def _():
                        kept[i] = tile_ref[...]

                if acc_row is not None:
                    acc_row[:, here] += halves(nt(v_col[:, there], tile_ref[...]))
                if acc_col is not None:
                    acc_col[:, there] += halves(nn(v_row[:, here], tile_ref[...]))
                return carry

            return lax.fori_loop(first, tab_ref[base + i, T_END], tile, carry)

        lax.fori_loop(0, STRIPS, strip, 0)


TILE = pltpu.VMEM((STRIP, SUB), bf16)
SPLIT = pltpu.VMEM((2 * N_PROBES, BLK), bf16)
SPLITS = pltpu.VMEM((2, 2 * N_PROBES, BLK), bf16)
FIELD = (N_PROBES, BLK)
FIELDS = (2, N_PROBES, BLK)


def call(body, outs, ins, out_specs, scratch, flops, name, limit=12):
    def run(*args):
        return pl.pallas_call(
            body,
            out_shape=outs,
            in_specs=ins,
            out_specs=out_specs,
            scratch_shapes=scratch,
            compiler_params=pltpu.CompilerParams(vmem_limit_bytes=limit * MIB),
            cost_estimate=pl.CostEstimate(flops=flops, bytes_accessed=MIB, transcendentals=0),
            name=name,
        )(*args)

    return run


def diag_build_kernel(tab, side, lhs, kd, acc, tile, v, rhs):
    def block(blk, carry):
        acc[blk] = jnp.zeros(FIELD, f32)
        base = 2 * STRIPS * blk

        @pl.when(tab[base, T_LIVE] > 0)
        def _():
            v[...] = split2(side[blk, 0:16, :])
            diag_pair(kd.at[blk], lhs.at[blk], rhs, side.at[blk], v, acc.at[blk])
            extra_tiles(tab, base, side.at[blk], side.at[blk], tile, v, v, acc.at[blk], acc.at[blk])

        return carry

    lax.fori_loop(0, 2, block, 0)


def halo_build_kernel(
    flags, side, lhs, got_a, got_b, acc_in, k12, x12, tab, acc, back, halo, plan_ref, tile, v1, v2, rhs, sem
):
    halo[...] = jnp.where(flags[4] == 0, got_a[...], got_b[...])
    plan_ref[...] = plan(side.at[1], halo, flags[3], False)
    copy = pltpu.make_async_copy(plan_ref, tab, sem.at[0])
    copy.start()
    acc[...] = acc_in[...]
    back[...] = jnp.zeros(FIELD, f32)
    copy.wait()

    @pl.when(flags[3] > 0)
    def _():
        v1[...] = split2(side[1, 0:16, :])
        v2[...] = split2(halo[0:16, :])
        fill = off_pair(k12, tab, 0, lhs.at[1], rhs, side.at[1], halo, v1, v2, acc.at[1], back)
        extra_tiles(tab, 0, side.at[1], halo, tile, v1, v2, acc.at[1], back, x12, fill)


def own_build_kernel(tab, side, lhs, acc_in, k01, x01, acc, tile, v, rhs):
    acc[...] = acc_in[...]

    @pl.when(tab[STRIPS, T_LIVE] > 0)
    def _():
        v[0] = split2(side[0, 0:16, :])
        v[1] = split2(side[1, 0:16, :])
        args = side.at[0], side.at[1]
        ends = v.at[0], v.at[1], acc.at[0], acc.at[1]
        fill = off_pair(k01, tab, STRIPS, lhs.at[0], rhs, *args, *ends)
        extra_tiles(tab, STRIPS, *args, tile, *ends, x01, fill)


def own_apply_kernel(tab, kd, k01, x01, side, w, acc, tile, v):
    def block(blk, carry):
        acc[blk] = jnp.zeros(FIELD, f32)
        v[blk] = split2(w[blk])
        base = 2 * STRIPS * blk

        @pl.when(tab[base, T_LIVE] > 0)
        def _():
            diag_products(kd.at[blk], v.at[blk], acc.at[blk])
            extra_tiles(
                tab, base, side.at[blk], side.at[blk], tile, v.at[blk], v.at[blk], acc.at[blk], acc.at[blk]
            )

        return carry

    lax.fori_loop(0, 2, block, 0)

    @pl.when(tab[STRIPS, T_LIVE] > 0)
    def _():
        ends = v.at[0], v.at[1], acc.at[0], acc.at[1]
        off_products(k01, tab, STRIPS, *ends)
        extra_tiles(tab, STRIPS, side.at[0], side.at[1], tile, *ends, x01)


def from_left(flags, got_a, got_b):
    arrived = jnp.where(flags[4] == 0, got_b[...], got_a[...])
    return jnp.where(flags[5] > 0, arrived, 0.0)


def inner(left, right):
    return jnp.sum(left * right, axis=1, keepdims=True)


def halo_product(tab, k12, x12, side, halo, halo_w, tile, v2, acc):
    @pl.when(tab[0, T_LIVE] > 0)
    def _():
        v2[...] = split2(halo_w)
        off_products(k12, tab, 0, None, v2, acc, None)
        extra_tiles(tab, 0, side.at[1], halo, tile, None, v2, acc, None, x12)


def finish_kernel(
    level, flags, tab, k12, x12, side, halo, got_a, got_b, acc_in, w, mom_in, new, send_a, send_b, mom,
    tile, v1, v2, acc, back
):
    acc[...] = acc_in[1]
    if level > 1:
        halo_w = jnp.where(flags[4] == 0, got_a[...], got_b[...])
        halo_product(tab, k12, x12, side, halo, halo_w, tile, v2, acc)
    before0 = w[0, 0:16, :]
    before1 = w[1, 0:16, :]
    next1 = side[1, 19:20, :] * before1 + acc[...]
    new[1] = next1
    back[...] = jnp.zeros(FIELD, f32)

    @pl.when(tab[0, T_LIVE] > 0)
    def _():
        v1[...] = split2(next1)
        off_products(k12, tab, 0, v1, None, None, back)
        extra_tiles(tab, 0, side.at[1], halo, tile, v1, None, None, back, x12)

    next0 = side[0, 19:20, :] * before0 + (acc_in[0] + from_left(flags, got_a, got_b))
    new[0] = next0
    send_a[...] = jnp.where(flags[4] == 0, back[...], next0)
    send_b[...] = jnp.where(flags[4] == 0, next0, back[...])
    lane = lax.broadcasted_iota(jnp.int32, (N_PROBES, SUB), 1)
    cross = inner(before0, next0) + inner(before1, next1)
    own = inner(next0, next0) + inner(next1, next1)
    total = jnp.where(lane == 2 * level - 1, cross, jnp.where(lane == 2 * level, own, 0.0))
    if level == 1:
        total = jnp.where(lane == 0, inner(before0, before0) + inner(before1, before1), total)
    else:
        total = total + mom_in[...]
    mom[...] = total


def moment_kernel(flags, side, acc, got_a, got_b, w, mom_in, mom):
    lane = lax.broadcasted_iota(jnp.int32, (N_PROBES, SUB), 1)
    one = w[0]
    two = w[1]
    arrived = from_left(flags, got_a, got_b)
    cross = inner(one, side[0, 19:20, :] * one + (acc[0] + 2.0 * arrived))
    cross = cross + inner(two, side[1, 19:20, :] * two + acc[1])
    mom[...] = mom_in[...] + jnp.where(lane == 5, cross, 0.0)


def last_kernel(flags, tab, k12, x12, side, halo, got_a, got_b, acc, w, new, tile, v2):
    new[1] = side[1, 19:20, :] * w[1] + acc[1]
    new[0] = side[0, 19:20, :] * w[0] + (acc[0] + from_left(flags, got_a, got_b))
    halo_w = jnp.where(flags[4] == 0, got_a[...], got_b[...])
    halo_product(tab, k12, x12, side, halo, halo_w, tile, v2, new.at[1])


def unsort(rank, fields, store):
    def block(blk, carry):
        stacked = jnp.concatenate([split2(field[blk]) for field in fields], axis=0)
        place = places()

        def strip(c, carry):
            piece = rank[blk, :, at(c, STRIP)]
            got = None
            for g in range(STRIPS):
                part = nn(stacked[:, g * STRIP : (g + 1) * STRIP], one_hot(marks(piece, g), place))
                got = part if got is None else got + part
            size = 2 * N_PROBES
            store(blk, at(blk * STRIPS + c, STRIP), [halves(got[size * k : size * (k + 1)]) for k in range(len(fields))])
            return carry

        lax.fori_loop(0, STRIPS, strip, 0)
        return carry

    lax.fori_loop(0, 2, block, 0)


def unsort_kernel(rank, wa, wb, wc, out):
    def store(blk, cols, values):
        for k, value in enumerate(values):
            out[16 * k : 16 * (k + 1), cols] = value

    unsort(rank, (wa, wb, wc), store)


def steps_kernel(mom, out, sound):
    lane = lax.broadcasted_iota(jnp.int32, (N_PROBES, SUB), 1)
    mu = [jnp.sum(jnp.where(lane == k, mom[...], 0.0), axis=1, keepdims=True) for k in range(6)]
    fine = []

    def form(left, right, shift):
        total, size = None, None
        for i, a in enumerate(left):
            for j, b in enumerate(right):
                part = (a * b) * mu[i + j + shift]
                total = part if total is None else total + part
                size = jnp.abs(part) if size is None else size + jnp.abs(part)
        fine.append(size <= 4000.0 * total)
        return total

    one = jnp.ones((N_PROBES, 1), f32)
    d = [one]
    r = [one]
    s = []
    rr = mu[0]
    for it in range(3):
        step = rr / form(d, d, 1)
        moved = [step * v for v in d]
        s = [a + b for a, b in zip(s + [0.0] * (len(d) - len(s)), moved)]
        r = [r[0]] + [(r[i] if i < len(r) else 0.0) - moved[i - 1] for i in range(1, len(moved) + 1)]
        if it < 2:
            new = form(r, r, 0)
            ratio = new / rr
            d = [r[i] + (ratio * d[i] if i < len(d) else 0.0) for i in range(len(r))]
            rr = new
    norms = [jnp.sqrt(mu[0]), jnp.sqrt(mu[2]), jnp.sqrt(mu[4])]
    norms.append(mu[5] / norms[2])
    size = sum(jnp.abs(a) * b for a, b in zip(r, norms))
    fine.append(size <= 200.0 * jnp.sqrt(rr))
    all_fine = fine[0]
    for other in fine[1:]:
        all_fine = all_fine & other
    sound[0] = jnp.min(jnp.where(all_fine, 1.0, 0.0)).astype(jnp.int32)
    table = jnp.zeros((N_PROBES, SUB), f32)
    for k, value in enumerate(s + r):
        table = jnp.where(lane == k, value, table)
    out[...] = table


def combine_kernel(steps, probes, u, sol, res):
    c = [steps[:, k : k + 1] for k in range(7)]

    def part(b, carry):
        here = at(b, 512)
        w = [probes[:, here], u[0:16, here], u[16:32, here], u[32:48, here]]
        sol[:, here] = (c[0] * w[0] + c[1] * w[1]) + c[2] * w[2]
        res[:, here] = ((c[3] * w[0] + c[4] * w[1]) + c[5] * w[2]) + c[6] * w[3]
        return carry

    lax.fori_loop(0, 2 * BLK // 512, part, 0)


def plain_product_kernel(flags, side, halo, got_a, got_b, d, acc, back, v, v2):
    acc[...] = jnp.zeros(FIELDS, f32)
    back[...] = jnp.zeros(FIELD, f32)
    v[...] = d[...].astype(bf16)
    v2[...] = jnp.where(flags[4] == 0, got_a[...], got_b[...]).astype(bf16)

    def pair(row_side, col_side, v_row, v_col, acc_row, acc_col):
        def row(i, carry):
            def col(j, carry):
                rows, cols = at(i, SUB), at(j, SUB)
                tile = tile_by_difference(
                    row_side, pl.multiple_of(i * SUB, SUB), col_side, pl.multiple_of(j * SUB, SUB)
                )
                acc_row[:, rows] += nt(v_col[:, cols], tile)
                if acc_col is not None:
                    acc_col[:, cols] += nn(v_row[:, rows], tile)
                return carry

            return lax.fori_loop(0, SUBS, col, carry)

        lax.fori_loop(0, SUBS, row, 0)

    def block(blk, carry):
        @pl.when(flags[2 * blk] > 0)
        def _():
            pair(side.at[blk], side.at[blk], None, v.at[blk], acc.at[blk], None)

        return carry

    lax.fori_loop(0, 2, block, 0)

    @pl.when(flags[1] > 0)
    def _():
        pair(side.at[0], side.at[1], v.at[0], v.at[1], acc.at[0], acc.at[1])

    @pl.when(flags[3] > 0)
    def _():
        pair(side.at[1], halo, v.at[1], v2, acc.at[1], back)


def plain_image_kernel(flags, side, acc, got_a, got_b, d, image, part):
    image[0] = side[0, 19:20, :] * d[0] + (acc[0] + from_left(flags, got_a, got_b))
    image[1] = side[1, 19:20, :] * d[1] + acc[1]
    part[...] = jnp.broadcast_to(inner(d[0], image[0]) + inner(d[1], image[1]), (N_PROBES, SUB))


def plain_step_kernel(norm, curvature, x, r, d, image, x_new, r_new, part):
    step = norm[:, 0:1] / curvature[:, 0:1]
    for b in range(2):
        x_new[b] = x[b] + step * d[b]
        r_new[b] = r[b] - step * image[b]
    part[...] = jnp.broadcast_to(inner(r_new[0], r_new[0]) + inner(r_new[1], r_new[1]), (N_PROBES, SUB))


def plain_turn_kernel(norm, new, r, d, d_new):
    ratio = new[:, 0:1] / norm[:, 0:1]
    for b in range(2):
        d_new[b] = r[b] + ratio * d[b]


def plain_start_kernel(side, x, r, part):
    x[...] = jnp.zeros(FIELDS, f32)
    r[0] = side[0, 0:16, :]
    r[1] = side[1, 0:16, :]
    part[...] = jnp.broadcast_to(inner(r[0], r[0]) + inner(r[1], r[1]), (N_PROBES, SUB))


def plain_end_kernel(rank, x, r, sol, res):
    def store(blk, cols, values):
        sol[:, cols], res[:, cols] = values

    unsort(rank, (x, r), store)


def plain_steps(flags, side, halo, rank, shape):
    fields = jax.ShapeDtypeStruct(FIELDS, f32)
    field = jax.ShapeDtypeStruct(FIELD, f32)
    sums = jax.ShapeDtypeStruct((N_PROBES, SUB), f32)

    def small(body, outs, ins, scratch=()):
        return call(body, outs, ins, (VMEM,) * len(outs), list(scratch), 10**7, "plain")

    x, r, part = small(plain_start_kernel, (fields, fields, sums), [VMEM])(side)

    def step(_, state):
        x, r, d, norm = state
        got = swapped_both(d[0], d[0])
        acc, back = small(
            plain_product_kernel,
            (fields, field),
            [SMEM] + [VMEM] * 5,
            (pltpu.VMEM(FIELDS, bf16), pltpu.VMEM(FIELD, bf16)),
        )(flags, side, halo, *got, d)
        got = swapped_both(back, back)
        image, part = small(plain_image_kernel, (fields, sums), [SMEM] + [VMEM] * 5)(flags, side, acc, *got, d)
        curvature = sum_over(part, "gx")
        x, r, part = small(plain_step_kernel, (fields, fields, sums), [VMEM] * 6)(norm, curvature, x, r, d, image)
        new = sum_over(part, "gx")
        (d,) = small(plain_turn_kernel, (fields,), [VMEM] * 4)(norm, new, r, d)
        return x, r, d, new

    x, r, _, _ = lax.fori_loop(0, 3, step, (x, r, r, sum_over(part, "gx")))
    out = jax.ShapeDtypeStruct(shape, f32)
    return small(plain_end_kernel, (out, out), [VMEM] * 3)(rank, x, r)


def swapped_both(to_a, to_b):
    count = lax.axis_size("gx")
    a = lax.ppermute(to_a, "gx", [(k, k ^ 1) for k in range(count)])
    ends = [(0, 0), (count - 1, count - 1)]
    b = lax.ppermute(to_b, "gx", ends + [(k, ((k + 1) ^ 1) - 1) for k in range(1, count - 1)])
    return a, b


def sum_over(value, axis):
    count = lax.axis_size(axis)
    if count & (count - 1):
        return lax.psum(value, axis)
    step = 1
    while step < count:
        radix = min(4, count // step)
        parts = [value] + [
            lax.ppermute(value, axis, [(k, k ^ (m * step)) for k in range(count)]) for m in range(1, radix)
        ]
        while len(parts) > 1:
            parts = [parts[m] + parts[m + 1] for m in range(0, len(parts), 2)]
        value = parts[0]
        step *= radix
    return value


def on_device(points, noise_var, probes, pair_list, counts):
    noise = noise_var.reshape(1, -1)
    field = pltpu.VMEM(FIELD, f32)
    fields = pltpu.VMEM(FIELDS, f32)
    one_side = pltpu.VMEM((24, BLK), f32)
    right = pltpu.VMEM((N_FEATURES, BLK), bf16)
    table = pltpu.SMEM((STRIPS, SUB), jnp.int32)
    moments = pltpu.VMEM((N_PROBES, SUB), f32)
    off = pltpu.VMEM((STRIPS, STRIP, OFF_W), bf16)
    outside = pltpu.VMEM((STRIPS, STRIP, SUB), bf16)
    far_space = pl.BlockSpec(memory_space=pltpu.HBM)
    shape = probes.shape

    side, first, lhs, rank, probes, flags, tab = call(
        sort_kernel,
        (
            pltpu.VMEM((2, 24, BLK), f32),
            one_side,
            pltpu.VMEM((2, BLK, N_FEATURES), bf16),
            pltpu.VMEM((2, 1, BLK), jnp.int32),
            pltpu.VMEM(shape, f32),
            pltpu.SMEM((6,), jnp.int32),
            pltpu.SMEM((3 * STRIPS, SUB), jnp.int32),
        ),
        [far_space] * 4 + [SMEM],
        (VMEM,) * 5 + (SMEM,) * 2,
        [
            pltpu.VMEM(points.shape, f32),
            pltpu.VMEM(noise.shape, f32),
            pltpu.SMEM(pair_list.shape[::-1], jnp.int32),
            pltpu.VMEM((3 * STRIPS, SUB), jnp.int32),
            pltpu.VMEM((1, BLK), f32),
            pltpu.VMEM((STRIP, SUB), f32),
            pltpu.VMEM((80, BLK), bf16),
            right,
            pltpu.SemaphoreType.DMA((4,)),
        ],
        10**9,
        "sort_blocks",
    )(*[pltpu.with_memory_space_constraint(x, pltpu.HBM) for x in (points, noise, probes, pair_list.T)], counts)

    halos = swapped_both(first, first)
    kd, acc = call(
        diag_build_kernel,
        (pltpu.VMEM((2, STRIPS, STRIP, DIAG_W), bf16), fields),
        [SMEM] + [VMEM] * 2,
        (VMEM,) * 2,
        [TILE, SPLIT, right],
        3 * 10**9,
        "diag_build",
    )(tab, side, lhs)
    k12, x12, tab12, acc, back, halo = call(
        halo_build_kernel,
        (off, outside, table, fields, field, one_side),
        [SMEM] + [VMEM] * 5,
        (VMEM, VMEM, SMEM, VMEM, VMEM, VMEM),
        [pltpu.VMEM((STRIPS, SUB), jnp.int32), TILE, SPLIT, SPLIT, right, pltpu.SemaphoreType.DMA((1,))],
        3 * 10**9,
        "halo_build",
    )(flags, side, lhs, *halos, acc)
    got = swapped_both(back, back)
    k01, x01, acc = call(
        own_build_kernel,
        (off, outside, fields),
        [SMEM] + [VMEM] * 3,
        (VMEM,) * 3,
        [TILE, SPLITS, right],
        5 * 10**9,
        "own_build",
    )(tab, side, lhs, acc)

    w = side
    mom = jnp.zeros((N_PROBES, SUB), f32)
    kept = []
    for level in (1, 2):
        w, send_a, send_b, mom = call(
            functools.partial(finish_kernel, level),
            (fields, field, field, moments),
            [SMEM] * 2 + [VMEM] * 9,
            (VMEM,) * 4,
            [TILE, SPLIT, SPLIT, pltpu.VMEM(FIELD, f32), pltpu.VMEM(FIELD, f32)],
            10**9,
            "finish",
        )(flags, tab12, k12, x12, side, halo, *got, acc, w, mom)
        kept.append(w)
        got = swapped_both(send_a, send_b)
        (acc,) = call(
            own_apply_kernel,
            (fields,),
            [SMEM] + [VMEM] * 5,
            (VMEM,),
            [TILE, SPLITS],
            2 * 10**9,
            "own_apply",
        )(tab, kd, k01, x01, side, w)
    mom = call(moment_kernel, moments, [SMEM] + [VMEM] * 6, VMEM, [], 10**7, "moment")(
        flags, side, acc, *got, w, mom
    )
    total = sum_over(mom, "gx")
    kept.append(
        call(last_kernel, fields, [SMEM] * 2 + [VMEM] * 8, VMEM, [TILE, SPLIT], 10**9, "last")(
            flags, tab12, k12, x12, side, halo, *got, acc, w
        )
    )
    given = call(
        unsort_kernel,
        pltpu.VMEM((3 * N_PROBES, 2 * BLK), f32),
        [VMEM] * 4,
        VMEM,
        [],
        4 * 96 * BLK * BLK,
        "unsort",
    )(rank, *kept)
    steps, sound = call(
        steps_kernel,
        (moments, pltpu.SMEM((1,), jnp.int32)),
        [VMEM],
        (VMEM, SMEM),
        [],
        10**6,
        "steps",
    )(total)

    def from_basis():
        out = jax.ShapeDtypeStruct(shape, f32)
        return tuple(
            call(combine_kernel, (out, out), [VMEM] * 3, (VMEM, VMEM), [], 10**6, "combine")(steps, probes, given)
        )

    def from_start():
        return tuple(plain_steps(flags, side, halo, rank, shape))

    return lax.cond(sound[0] > 0, from_basis, from_start)


def solution(mesh):
    placed = (
        P(None, ("groups", "gx")),
        P(("groups", "gx")),
        P(None, ("groups", "gx")),
        P(("groups", "gx"), None),
        P(("groups", "gx")),
    )
    return jax.shard_map(
        on_device,
        mesh=mesh,
        in_specs=placed,
        out_specs=(P(None, ("groups", "gx")), P(None, ("groups", "gx"))),
        check_vma=False,
    )
```

profile of v0, /device:TPU:0, one launch (start us, length us, event | category | flops | bytes accessed | tf_op | source)
XLA Modules:
  0.0 80.9 jit_solution(3878179778484515061)
XLA Ops:
  1.3 18.0 %sort_blocks.1 = (f32[2,24,2048]{2,1,0:T(8,128)S(1)}, f32[24,2048]{1,0:T(8,128)S(1)}, bf16[2,2048,64]{2,1,0:T(8,128)(2,1)S(1)}, s32[2,1,2048]{2,1,0:T(1,128)S(1)...) custom-call(f32[3,4096]{1,0:T(4,128)} %pts_hbm.1, f32[1,4096]{1,0:T(1,128)} %bitcast.7, ...), custom_call_target="tpu_custom_call" | custom-call | flops 1000000000 | bytes 1048576 | tf_op jit(solution)/shard_map/sort_blocks/pallas_call | solution.py:437
  19.2 0.5 collective-permute-start.22
  19.8 0.7 collective-permute-start.23
  20.4 7.4 %diag_build.1 = (bf16[2,8,256,512]{3,2,1,0:T(8,128)(2,1)S(1)}, f32[2,16,2048]{2,1,0:T(8,128)S(1)}) custom-call(s32[24,128]{1,0:T(8,128)S(4)} %get-tuple-element.106.tab, f32[2,24,2048]{2,1,0:T(8,128)S(1)} %get-tuple-element.105.side.w, bf16[2,2048,64]{2,1,0:T(8,128)(2,1)S(1)} %get-tuple-element.107.lhs), custom_call_target="tpu_custom_call" | custom-call | flops 3000000000 | bytes 1048576 | tf_op jit(solution)/shard_map/diag_build/pallas_call | solution.py:437
  27.9 5.2 %halo_build.1 = (bf16[8,256,768]{2,1,0:T(8,128)(2,1)S(1)}, bf16[8,256,128]{2,1,0:T(8,128)(2,1)S(1)}, s32[8,128]{1,0:T(8,128)S(4)}, f32[2,16,2048]{2,1,0:T(8,128)...) custom-call(s32[6]{0:T(128)S(4)} %get-tuple-element.104.flags, f32[2,24,2048]{2,1,0:T(8,128)S(1)} %get-tuple-element.105.side.w, ...), custom_call_target="tpu_custom_call" | custom-call | flops 3000000000 | bytes 1048576 | tf_op jit(solution)/shard_map/halo_build/pallas_call | solution.py:437
  33.1 4.0 %collective-permute-start.24 = (f32[16,2048]{1,0:T(8,128)S(1)}, f32[16,2048]{1,0:T(8,128)S(1)}, u32[]{:S(2)}, u32[]{:S(2)}) collective-permute-start(f32[16,2048]{1,0:T(8,128)S(1)} %get-tuple-element.118), channel_id=1, source_target_pairs={{0,1},{1,0},{2,3},{3,2},{4,5},{5,4},{6,7},{7,6},{8,9},{9,8},{10,11... | collective-permute-start | bytes 393224 | tf_op jit(solution)/shard_map/ppermute | solution.py:786
  37.1 0.7 collective-permute-start.25
  37.7 4.7 %own_build.1 = (bf16[8,256,768]{2,1,0:T(8,128)(2,1)S(1)}, bf16[8,256,128]{2,1,0:T(8,128)(2,1)S(1)}, f32[2,16,2048]{2,1,0:T(8,128)S(1)}) custom-call(s32[24,128]{1,0:T(8,128)S(4)} %get-tuple-element.106.tab, f32[2,24,2048]{2,1,0:T(8,128)S(1)} %get-tuple-element.105.side.w, bf16[2,2048,64]{2,1,0:T(8,128)(2,1)S(1)} %get-tuple-element.107.lhs, ...), custom_call_target="tpu_custom_call" | custom-call | flops 5000000000 | bytes 1048576 | tf_op jit(solution)/shard_map/own_build/pallas_call | solution.py:437
  42.5 1.2 %finish.2 = (f32[2,16,2048]{2,1,0:T(8,128)S(1)}, f32[16,2048]{1,0:T(8,128)S(1)}, f32[16,2048]{1,0:T(8,128)S(1)}, f32[16,128]{1,0:T(8,128)S(1)}) custom-call(s32[6]{0:T(128)S(4)} %get-tuple-element.104.flags, s32[8,128]{1,0:T(8,128)S(4)} %get-tuple-element.114.tab, bf16[8,256,768]{2,1,0:T(8,128)(2,1)S(1)} %get-tuple-element.115.k12, ...), custom_call_target="tpu_custom_call" | custom-call | flops 1000000000 | bytes 1048576 | tf_op jit(solution)/shard_map/finish/pallas_call | solution.py:437
  43.7 2.4 %collective-permute-start.26 = (f32[16,2048]{1,0:T(8,128)S(1)}, f32[16,2048]{1,0:T(8,128)S(1)}, u32[]{:S(2)}, u32[]{:S(2)}) collective-permute-start(f32[16,2048]{1,0:T(8,128)S(1)} %get-tuple-element.120), channel_id=1, source_target_pairs={{0,1},{1,0},{2,3},{3,2},{4,5},{5,4},{6,7},{7,6},{8,9},{9,8},{10,11... | collective-permute-start | bytes 393224 | tf_op jit(solution)/shard_map/ppermute | solution.py:786
  46.1 0.7 collective-permute-start.27
  46.8 4.4 %own_apply.2.acc_in = f32[2,16,2048]{2,1,0:T(8,128)S(1)} custom-call(s32[24,128]{1,0:T(8,128)S(4)} %get-tuple-element.106.tab, bf16[2,8,256,512]{3,2,1,0:T(8,128)(2,1)S(1)} %get-tuple-element.108.kd, bf16[8,256,768]{2,1,0:T(8,128)(2,1)S(1)} %get-tuple-element.112.k01, bf16[8,256,128]{2,1,0:T(8,128)(2,1)S(1)} %get-tuple-element.113.x01, ...), custom_call_target="tpu_custom_call" | custom-call | flops 2000000000 | bytes 1048576 | tf_op jit(solution)/shard_map/own_apply/pallas_call | solution.py:437
  51.3 2.6 %finish.3 = (f32[2,16,2048]{2,1,0:T(8,128)S(1)}, f32[16,2048]{1,0:T(8,128)S(1)}, f32[16,2048]{1,0:T(8,128)S(1)}, f32[16,128]{1,0:T(8,128)S(1)}) custom-call(s32[6]{0:T(128)S(4)} %get-tuple-element.104.flags, s32[8,128]{1,0:T(8,128)S(4)} %get-tuple-element.114.tab, bf16[8,256,768]{2,1,0:T(8,128)(2,1)S(1)} %get-tuple-element.115.k12, ...), custom_call_target="tpu_custom_call" | custom-call | flops 1000000000 | bytes 1048576 | tf_op jit(solution)/shard_map/finish/pallas_call | solution.py:437
  53.9 2.9 %collective-permute-start.28 = (f32[16,2048]{1,0:T(8,128)S(1)}, f32[16,2048]{1,0:T(8,128)S(1)}, u32[]{:S(2)}, u32[]{:S(2)}) collective-permute-start(f32[16,2048]{1,0:T(8,128)S(1)} %get-tuple-element.125), channel_id=1, source_target_pairs={{0,1},{1,0},{2,3},{3,2},{4,5},{5,4},{6,7},{7,6},{8,9},{9,8},{10,11... | collective-permute-start | bytes 393224 | tf_op jit(solution)/shard_map/ppermute | solution.py:786
  56.7 0.7 collective-permute-start.29
  57.4 4.4 %own_apply.3.acc = f32[2,16,2048]{2,1,0:T(8,128)S(1)} custom-call(s32[24,128]{1,0:T(8,128)S(4)} %get-tuple-element.106.tab, bf16[2,8,256,512]{3,2,1,0:T(8,128)(2,1)S(1)} %get-tuple-element.108.kd, bf16[8,256,768]{2,1,0:T(8,128)(2,1)S(1)} %get-tuple-element.112.k01, bf16[8,256,128]{2,1,0:T(8,128)(2,1)S(1)} %get-tuple-element.113.x01, ...), custom_call_target="tpu_custom_call" | custom-call | flops 2000000000 | bytes 1048576 | tf_op jit(solution)/shard_map/own_apply/pallas_call | solution.py:437
  62.0 4.2 %collective-permute-start.31 = (f32[16,128]{1,0:T(8,128)S(1)}, f32[16,128]{1,0:T(8,128)S(1)}, u32[]{:S(2)}, u32[]{:S(2)}) collective-permute-start(f32[16,128]{1,0:T(8,128)S(1)} %moment.1), channel_id=1, source_target_pairs={{0,2},{1,3},{2,0},{3,1},{4,6},{5,7},{6,4},{7,5},{8,10},{9,11},{10,... | collective-permute-start | bytes 24584 | tf_op jit(solution)/shard_map/ppermute | solution.py:800
  66.3 1.4 %last.1.wc = f32[2,16,2048]{2,1,0:T(8,128)S(1)} custom-call(s32[6]{0:T(128)S(4)} %get-tuple-element.104.flags, s32[8,128]{1,0:T(8,128)S(4)} %get-tuple-element.114.tab, bf16[8,256,768]{2,1,0:T(8,128)(2,1)S(1)} %get-tuple-element.115.k12, bf16[8,256,128]{2,1,0:T(8,128)(2,1)S(1)} %get-tuple-element.116.x12, f32[2,24,2048]{2,1,0:T(8,128)S(1)} %get-tuple-element.105.side.w, ...), custom_call_target="tpu_custom_call" | custom-call | flops 1000000000 | bytes 1048576 | tf_op jit(solution)/shard_map/last/pallas_call | solution.py:437
  67.8 1.4 %collective-permute-done.32 = f32[16,128]{1,0:T(8,128)S(1)} collective-permute-done((f32[16,128]{1,0:T(8,128)S(1)}, f32[16,128]{1,0:T(8,128)S(1)}, u32[]{:S(2)}, u32[]{:S(2)}) %collective-permute-start.32) | collective-permute-done | bytes 8224 | tf_op jit(solution)/shard_map/ppermute | solution.py:800
  69.2 3.3 %collective-permute-start.34 = (f32[16,128]{1,0:T(8,128)S(1)}, f32[16,128]{1,0:T(8,128)S(1)}, u32[]{:S(2)}, u32[]{:S(2)}) collective-permute-start(f32[16,128]{1,0:T(8,128)S(1)} %add_add_fusion.7), channel_id=1, source_target_pairs={{0,8},{1,9},{2,10},{3,11},{4,12},{5,13},{6,14},{7,15},{8,0},{9,1},... | collective-permute-start | bytes 24584 | tf_op jit(solution)/shard_map/ppermute | solution.py:800
  72.5 1.4 %collective-permute-start.35 = (f32[16,128]{1,0:T(8,128)S(1)}, f32[16,128]{1,0:T(8,128)S(1)}, u32[]{:S(2)}, u32[]{:S(2)}) collective-permute-start(f32[16,128]{1,0:T(8,128)S(1)} %add_add_fusion.7), channel_id=1, source_target_pairs={{0,12},{1,13},{2,14},{3,15},{4,8},{5,9},{6,10},{7,11},{8,4},{9,5},... | collective-permute-start | bytes 24584 | tf_op jit(solution)/shard_map/ppermute | solution.py:800
  73.9 5.0 %unsort.1 = f32[48,4096]{1,0:T(8,128)S(1)} custom-call(s32[2,1,2048]{2,1,0:T(1,128)S(1)} %get-tuple-element.129.rank, f32[2,16,2048]{2,1,0:T(8,128)S(1)} %get-tuple-element.122.w.wa, f32[2,16,2048]{2,1,0:T(8,128)S(1)} %get-tuple-element.124.w.wb, f32[2,16,2048]{2,1,0:T(8,128)S(1)} %last.1.wc), custom_call_target="tpu_custom_call" | custom-call | flops 1610612736 | bytes 1048576 | tf_op jit(solution)/shard_map/unsort/pallas_call | solution.py:437
  79.2 1.7 %conditional.1 = ((f32[16,4096]{1,0:T(8,128)}, f32[16,4096]{1,0:T(8,128)})) conditional(s32[]{:T(128)} %bitcast.3, (f32[2,24,2048]{2,1,0:T(8,128)S(1)}, s32[6]{0:T(128)S(4)}, f32[24,2048]{1,0:T(8,128)S(1)}, s32[2,1,2048]{2,1,0:T(1,128)S(1)}) %tuple.17, (f32[16,128]{1,0:T(8,128)S(1)}, f32[16,4096]{1,0:T(8,128)S(1)}, f32[48,4096]{1,0:T(8,128)S(1)}) %tuple.18), branch_computations={%region_0.0_spmd, %region_3.0_spmd} | conditional | flops 60036864 | bytes 11600933 | solution.py:941
  79.4 1.5 %combine.1 = (f32[16,4096]{1,0:T(8,128)}, f32[16,4096]{1,0:T(8,128)}) custom-call(f32[16,128]{1,0:T(8,128)S(1)} %get-tuple-element.71.steps, f32[16,4096]{1,0:T(8,128)S(1)} %get-tuple-element.72.probes, f32[48,4096]{1,0:T(8,128)S(1)} %get-tuple-element.73.u), custom_call_target="tpu_custom_call" | custom-call | flops 1000000 | bytes 1048576 | tf_op jit(solution)/shard_map/cond/branch_1_fun/combine/pallas_call | solution.py:437
  (21 shorter events, 0.6 us)
Async XLA Ops:
  19.2 8.6 %collective-permute-start.22 = (f32[24,2048]{1,0:T(8,128)S(1)}, f32[24,2048]{1,0:T(8,128)S(1)}, u32[]{:S(2)}, u32[]{:S(2)}) collective-permute-start(f32[24,2048]{1,0:T(8,128)S(1)} %get-tuple-element.109), channel_id=1, source_target_pairs={{0,1},{1,0},{2,3},{3,2},{4,5},{5,4},{6,7},{7,6},{8,9},{9,8},{10,11... | collective-permute-start | bytes 589832 | tf_op jit(solution)/shard_map/ppermute | solution.py:786
  19.8 8.1 %collective-permute-start.23 = (f32[24,2048]{1,0:T(8,128)S(1)}, f32[24,2048]{1,0:T(8,128)S(1)}, u32[]{:S(2)}, u32[]{:S(2)}) collective-permute-start(f32[24,2048]{1,0:T(8,128)S(1)} %get-tuple-element.109), channel_id=1, source_target_pairs={{0,0},{15,15},{1,2},{2,1},{3,4},{4,3},{5,6},{6,5},{7,8},{8,7},{9,1... | collective-permute-start | bytes 589832 | tf_op jit(solution)/shard_map/ppermute | solution.py:788
  33.1 9.3 %collective-permute-start.24 = (f32[16,2048]{1,0:T(8,128)S(1)}, f32[16,2048]{1,0:T(8,128)S(1)}, u32[]{:S(2)}, u32[]{:S(2)}) collective-permute-start(f32[16,2048]{1,0:T(8,128)S(1)} %get-tuple-element.118), channel_id=1, source_target_pairs={{0,1},{1,0},{2,3},{3,2},{4,5},{5,4},{6,7},{7,6},{8,9},{9,8},{10,11... | collective-permute-start | bytes 393224 | tf_op jit(solution)/shard_map/ppermute | solution.py:786
  37.1 5.4 %collective-permute-start.25 = (f32[16,2048]{1,0:T(8,128)S(1)}, f32[16,2048]{1,0:T(8,128)S(1)}, u32[]{:S(2)}, u32[]{:S(2)}) collective-permute-start(f32[16,2048]{1,0:T(8,128)S(1)} %get-tuple-element.118), channel_id=1, source_target_pairs={{0,0},{15,15},{1,2},{2,1},{3,4},{4,3},{5,6},{6,5},{7,8},{8,7},{9,1... | collective-permute-start | bytes 393224 | tf_op jit(solution)/shard_map/ppermute | solution.py:788
  43.7 7.5 %collective-permute-start.26 = (f32[16,2048]{1,0:T(8,128)S(1)}, f32[16,2048]{1,0:T(8,128)S(1)}, u32[]{:S(2)}, u32[]{:S(2)}) collective-permute-start(f32[16,2048]{1,0:T(8,128)S(1)} %get-tuple-element.120), channel_id=1, source_target_pairs={{0,1},{1,0},{2,3},{3,2},{4,5},{5,4},{6,7},{7,6},{8,9},{9,8},{10,11... | collective-permute-start | bytes 393224 | tf_op jit(solution)/shard_map/ppermute | solution.py:786
  46.1 5.1 %collective-permute-start.27 = (f32[16,2048]{1,0:T(8,128)S(1)}, f32[16,2048]{1,0:T(8,128)S(1)}, u32[]{:S(2)}, u32[]{:S(2)}) collective-permute-start(f32[16,2048]{1,0:T(8,128)S(1)} %get-tuple-element.121), channel_id=1, source_target_pairs={{0,0},{15,15},{1,2},{2,1},{3,4},{4,3},{5,6},{6,5},{7,8},{8,7},{9,1... | collective-permute-start | bytes 393224 | tf_op jit(solution)/shard_map/ppermute | solution.py:788
  53.9 8.0 %collective-permute-start.28 = (f32[16,2048]{1,0:T(8,128)S(1)}, f32[16,2048]{1,0:T(8,128)S(1)}, u32[]{:S(2)}, u32[]{:S(2)}) collective-permute-start(f32[16,2048]{1,0:T(8,128)S(1)} %get-tuple-element.125), channel_id=1, source_target_pairs={{0,1},{1,0},{2,3},{3,2},{4,5},{5,4},{6,7},{7,6},{8,9},{9,8},{10,11... | collective-permute-start | bytes 393224 | tf_op jit(solution)/shard_map/ppermute | solution.py:786
  56.7 5.1 %collective-permute-start.29 = (f32[16,2048]{1,0:T(8,128)S(1)}, f32[16,2048]{1,0:T(8,128)S(1)}, u32[]{:S(2)}, u32[]{:S(2)}) collective-permute-start(f32[16,2048]{1,0:T(8,128)S(1)} %get-tuple-element.126), channel_id=1, source_target_pairs={{0,0},{15,15},{1,2},{2,1},{3,4},{4,3},{5,6},{6,5},{7,8},{8,7},{9,1... | collective-permute-start | bytes 393224 | tf_op jit(solution)/shard_map/ppermute | solution.py:788
  62.0 5.8 %collective-permute-start.31 = (f32[16,128]{1,0:T(8,128)S(1)}, f32[16,128]{1,0:T(8,128)S(1)}, u32[]{:S(2)}, u32[]{:S(2)}) collective-permute-start(f32[16,128]{1,0:T(8,128)S(1)} %moment.1), channel_id=1, source_target_pairs={{0,2},{1,3},{2,0},{3,1},{4,6},{5,7},{6,4},{7,5},{8,10},{9,11},{10,... | collective-permute-start | bytes 24584 | tf_op jit(solution)/shard_map/ppermute | solution.py:800
  66.1 3.1 %collective-permute-start.32 = (f32[16,128]{1,0:T(8,128)S(1)}, f32[16,128]{1,0:T(8,128)S(1)}, u32[]{:S(2)}, u32[]{:S(2)}) collective-permute-start(f32[16,128]{1,0:T(8,128)S(1)} %moment.1), channel_id=1, source_target_pairs={{0,3},{1,2},{2,1},{3,0},{4,7},{5,6},{6,5},{7,4},{8,11},{9,10},{10,... | collective-permute-start | bytes 24584 | tf_op jit(solution)/shard_map/ppermute | solution.py:800
  66.1 3.1 %collective-permute-start.30 = (f32[16,128]{1,0:T(8,128)S(1)}, f32[16,128]{1,0:T(8,128)S(1)}, u32[]{:S(2)}, u32[]{:S(2)}) collective-permute-start(f32[16,128]{1,0:T(8,128)S(1)} %moment.1), channel_id=1, source_target_pairs={{0,1},{1,0},{2,3},{3,2},{4,5},{5,4},{6,7},{7,6},{8,9},{9,8},{10,11... | collective-permute-start | bytes 24584 | tf_op jit(solution)/shard_map/ppermute | solution.py:800
  69.2 9.7 %collective-permute-start.34 = (f32[16,128]{1,0:T(8,128)S(1)}, f32[16,128]{1,0:T(8,128)S(1)}, u32[]{:S(2)}, u32[]{:S(2)}) collective-permute-start(f32[16,128]{1,0:T(8,128)S(1)} %add_add_fusion.7), channel_id=1, source_target_pairs={{0,8},{1,9},{2,10},{3,11},{4,12},{5,13},{6,14},{7,15},{8,0},{9,1},... | collective-permute-start | bytes 24584 | tf_op jit(solution)/shard_map/ppermute | solution.py:800
  72.5 6.4 %collective-permute-start.35 = (f32[16,128]{1,0:T(8,128)S(1)}, f32[16,128]{1,0:T(8,128)S(1)}, u32[]{:S(2)}, u32[]{:S(2)}) collective-permute-start(f32[16,128]{1,0:T(8,128)S(1)} %add_add_fusion.7), channel_id=1, source_target_pairs={{0,12},{1,13},{2,14},{3,15},{4,8},{5,9},{6,10},{7,11},{8,4},{9,5},... | collective-permute-start | bytes 24584 | tf_op jit(solution)/shard_map/ppermute | solution.py:800
  73.9 5.0 %collective-permute-start.33 = (f32[16,128]{1,0:T(8,128)S(1)}, f32[16,128]{1,0:T(8,128)S(1)}, u32[]{:S(2)}, u32[]{:S(2)}) collective-permute-start(f32[16,128]{1,0:T(8,128)S(1)} %add_add_fusion.7), channel_id=1, source_target_pairs={{0,4},{1,5},{2,6},{3,7},{4,0},{5,1},{6,2},{7,3},{8,12},{9,13},{10,... | collective-permute-start | bytes 24584 | tf_op jit(solution)/shard_map/ppermute | solution.py:800
where the time goes:
time: 80.5 us; the launch traced here: 80.9 us
  Pallas kernels  56.2 us (70%)
  starting transfers between devices  21.5 us (27%)
  waiting for transfers between devices  1.49 us (2%)
  between operations  1.49 us (2%)
    pallas_call x13, Pallas kernels, run(): pl.pallas_call(body, out_shape=outs, in_specs=ins, out_specs=out_specs, s...  56.2 us
    ppermute x4, starting transfers between devices, swapped_both(): a = lax.ppermute(to_a, 'gx', [(k, k ^ 1) for k in range(count)])  9.77 us
    ppermute x6, starting transfers between devices, sum_over(): lax.ppermute(value, axis, [(k, k ^ m * step) for k in range(count)])  9.05 us
    ppermute x4, starting transfers between devices, swapped_both(): lax.ppermute(to_b, 'gx', ends + [(k, (k + 1 ^ 1) - 1) for k in range(1, c...  2.63 us
  transfers between devices with their start and end apart: 14, of which 1 were waited for; matrix products, arithmetic and copies ran while one was open for 0% of the time, Pallas kernels for 34%

commit v1 on v0

--- a/solution.py
+++ b/solution.py
@@ -17,7 +17,6 @@
 DIAG_W = 512
 N_PROBES = 16
 N_FEATURES = 64
-UNROLL = 2
 MIB = 1 << 20
 
 VMEM = pl.BlockSpec(memory_space=pltpu.VMEM)
@@ -55,8 +54,21 @@
     return high, mid, rest - mid
 
 
+def multiple(value, size):
+    return value if isinstance(value, int) else pl.multiple_of(value, size)
+
+
 def at(index, size):
-    return pl.ds(pl.multiple_of(index * size, size), size)
+    return pl.ds(multiple(index * size, size), size)
+
+
+def looped(count, body):
+    lax.fori_loop(0, count, body, 0)
+
+
+def each(count, body):
+    for index in range(count):
+        body(index, 0)
 
 
 def one_hot(marked, place):
@@ -101,7 +113,7 @@
         before_ref[...] += nn(one_hot(key_ref[:, at(j, STRIP)].astype(bf16), value), ones)
         return carry
 
-    lax.fori_loop(0, STRIPS, count, 0, unroll=2)
+    each(STRIPS, count)
     total = before_ref[...]
     coarse = jnp.floor(total * (1.0 / 16.0)) * 16.0
     before_ref[...] = nn(lower, coarse.astype(bf16)) + nn(lower, (total - coarse).astype(bf16))
@@ -115,7 +127,7 @@
         before_ref[...] = before + nn(hit, ones)
         return carry
 
-    lax.fori_loop(0, STRIPS, place, 0)
+    each(STRIPS, place)
 
 
 def plan(row_side, col_side, live, diag):
@@ -169,7 +181,7 @@
 
 def sort_kernel(
     pts_hbm, nv_hbm, pr_hbm, pair_hbm, count, side, first, lhs, rank, pr_ref, flags, tab,
-    pts_ref, nv_ref, pair, plan_ref, key_ref, before_ref, data_ref, rows_ref, sems
+    pts_ref, nv_ref, pair, plan_ref, key_ref, before_ref, sems
 ):
     copies = [
         pltpu.make_async_copy(src, dst, sems.at[k])
@@ -179,7 +191,10 @@
     ]
     for copy in copies:
         copy.start()
-    for copy in copies:
+    copies[0].wait()
+    for blk in range(2):
+        fill_ranks(pts_ref[1:2, at(blk, BLK)], rank.at[blk], key_ref, before_ref)
+    for copy in copies[1:]:
         copy.wait()
     for local in range(2):
         for ahead in range(2):
@@ -187,48 +202,43 @@
     position = lax.shift_right_logical(pair[0, 0], 1)
     flags[4] = jnp.bitwise_and(position, 1)
     flags[5] = jnp.where(position > 0, 1, 0)
-
-    def block(blk, carry):
+    place = places()
+    for blk in range(2):
         cols = at(blk, BLK)
-        fill_ranks(pts_ref[1:2, cols], rank.at[blk], key_ref, before_ref)
         aux = jnp.concatenate(
             [pts_ref[0:3, cols] * 2.0, nv_ref[:, cols], jnp.zeros((4, BLK), f32)], axis=0
         )
-        data_ref[...] = jnp.concatenate(
+        data = jnp.concatenate(
             [*split3(pr_ref[:, cols]), *split3(aux), jnp.zeros((8, BLK), f32)], axis=0
         ).astype(bf16)
         centre = 0.5 * (jnp.min(aux, axis=1, keepdims=True) + jnp.max(aux, axis=1, keepdims=True))
         centre = jnp.concatenate([jnp.zeros((4, 1), f32), centre[0:3], jnp.zeros((1, 1), f32)], axis=0)
-        place = places()
-
-        def strip(g, carry):
-            marked = marks(rank[blk], g)
+        ranks = rank[blk]
+        for g in range(STRIPS):
+            marked = marks(ranks, g)
             got = None
             for c in range(STRIPS):
                 here = slice(c * STRIP, (c + 1) * STRIP)
-                part = nt(data_ref[:, here], one_hot(marked[:, here], place))
+                part = nt(data[:, here], one_hot(marked[:, here], place))
                 got = part if got is None else got + part
-            side[blk, 0:16, at(g, STRIP)] = (got[0:16] + got[16:32]) + got[32:48]
-            side[blk, 16:24, at(g, STRIP)] = ((got[48:56] + got[56:64]) + got[64:72]) + centre
-            return carry
-
-        lax.fori_loop(0, STRIPS, strip, 0)
-        rows, _ = features(offset_of(side.at[blk], side.at[blk]), True)
-        rows_ref[...] = rows.astype(bf16)
-
-        def turn(c, carry):
-            lhs[blk, at(c, STRIP), :] = turned(rows_ref[:, at(c, STRIP)])
-            return carry
-
-        lax.fori_loop(0, STRIPS, turn, 0, unroll=2)
-        return carry
-
-    lax.fori_loop(0, 2, block, 0)
-    first[...] = side[0]
+            low = (got[0:16] + got[16:32]) + got[32:48]
+            high = ((got[48:56] + got[56:64]) + got[64:72]) + centre
+            side[blk, 0:16, at(g, STRIP)] = low
+            side[blk, 16:24, at(g, STRIP)] = high
+            if blk == 0:
+                first[0:16, at(g, STRIP)] = low
+                first[16:24, at(g, STRIP)] = high
     plan_ref[0:8, :] = plan(side.at[0], side.at[0], flags[0], True)
     plan_ref[8:16, :] = plan(side.at[0], side.at[1], flags[1], False)
     plan_ref[16:24, :] = plan(side.at[1], side.at[1], flags[2], True)
-    pltpu.sync_copy(plan_ref, tab)
+    copy = pltpu.make_async_copy(plan_ref, tab, sems.at[0])
+    copy.start()
+    for blk in range(2):
+        rows, _ = features(offset_of(side.at[blk], side.at[blk]), True)
+        rows = rows.astype(bf16)
+        for c in range(STRIPS):
+            lhs[blk, at(c, STRIP), :] = turned(rows[:, c * STRIP : (c + 1) * STRIP])
+    copy.wait()
 
 
 def offset_of(side_ref, centre_ref):
@@ -268,9 +278,9 @@
 
 def fast_strip(k_ref, i, lhs, rhs, start, width):
     for h in range(width // STRIP):
-        right = rhs[:, pl.ds(pl.multiple_of(start + h * STRIP, SUB), STRIP)]
+        right = rhs[:, pl.ds(multiple(start + h * STRIP, SUB), STRIP)]
         for g in range(STRIP // SUB):
-            left = lhs[pl.ds(pl.multiple_of(i * STRIP + g * SUB, SUB), SUB), :]
+            left = lhs[pl.ds(multiple(i * STRIP + g * SUB, SUB), SUB), :]
             k_ref[i, g * SUB : (g + 1) * SUB, h * STRIP : (h + 1) * STRIP] = kernel_values(nn(left, right))
 
 
@@ -310,12 +320,12 @@
             partner_strip(k_ref, i, start, v_row, acc_col)
             return carry
 
-        lax.fori_loop(0, STRIPS, strip, 0, unroll=UNROLL)
+        each(STRIPS, strip)
 
     @pl.when(jnp.logical_not(near))
     def _():
         slow_build(k_ref, row_side, col_side, lambda i: tab_ref[base + i, T_START], OFF_SUBS)
-        off_products(k_ref, tab_ref, base, v_row, v_col, acc_row, acc_col)
+        off_products(k_ref, tab_ref, base, v_row, v_col, acc_row, acc_col, looped)
 
     return near, lhs, rhs
 
@@ -330,14 +340,14 @@
             diag_strip(k_ref, i, v, acc, DIAG_W)
             return carry
 
-        lax.fori_loop(0, STRIPS - 1, strip, 0)
+        each(STRIPS - 1, strip)
         fast_strip(k_ref, STRIPS - 1, lhs, rhs, (STRIPS - 1) * STRIP, STRIP)
         diag_strip(k_ref, STRIPS - 1, v, acc, STRIP)
 
     @pl.when(jnp.logical_not(near))
     def _():
         slow_build(k_ref, side, side, lambda i: 2 * i, DIAG_W // SUB)
-        diag_products(k_ref, v, acc)
+        diag_products(k_ref, v, acc, looped)
 
 
 def owner_strip(k_ref, i, start, v_col, acc_row):
@@ -348,7 +358,7 @@
     acc_col[:, pl.ds(start, OFF_W)] += halves(nn(v_row[:, at(i, STRIP)], k_ref[i]))
 
 
-def off_products(k_ref, tab_ref, base, v_row, v_col, acc_row, acc_col):
+def off_products(k_ref, tab_ref, base, v_row, v_col, acc_row, acc_col, repeat=each):
     def strip(i, carry):
         start = pl.multiple_of(tab_ref[base + i, T_START] * SUB, SUB)
         if acc_row is not None:
@@ -357,22 +367,22 @@
             partner_strip(k_ref, i, start, v_row, acc_col)
         return carry
 
-    lax.fori_loop(0, STRIPS, strip, 0, unroll=UNROLL)
+    repeat(STRIPS, strip)
 
 
 def diag_strip(k_ref, i, v_ref, acc_ref, width):
-    start = pl.multiple_of(i * STRIP, STRIP)
+    start = multiple(i * STRIP, STRIP)
     acc_ref[:, at(i, STRIP)] += halves(nt(v_ref[:, pl.ds(start, width)], k_ref[i, :, :width]))
     if width > STRIP:
         acc_ref[:, at(i + 1, STRIP)] += halves(nn(v_ref[:, at(i, STRIP)], k_ref[i, :, STRIP:width]))
 
 
-def diag_products(k_ref, v_ref, acc_ref):
+def diag_products(k_ref, v_ref, acc_ref, repeat=each):
     def strip(i, carry):
         diag_strip(k_ref, i, v_ref, acc_ref, DIAG_W)
         return carry
 
-    lax.fori_loop(0, STRIPS - 1, strip, 0, unroll=UNROLL)
+    repeat(STRIPS - 1, strip)
     diag_strip(k_ref, STRIPS - 1, v_ref, acc_ref, STRIP)
 
 
@@ -461,7 +471,7 @@
 
         return carry
 
-    lax.fori_loop(0, 2, block, 0)
+    each(2, block)
 
 
 def halo_build_kernel(
@@ -511,7 +521,7 @@
 
         return carry
 
-    lax.fori_loop(0, 2, block, 0)
+    each(2, block)
 
     @pl.when(tab[STRIPS, T_LIVE] > 0)
     def _():
@@ -589,7 +599,7 @@
     halo_product(tab, k12, x12, side, halo, halo_w, tile, v2, new.at[1])
 
 
-def unsort(rank, fields, store):
+def unsort(rank, fields, store, repeat):
     def block(blk, carry):
         stacked = jnp.concatenate([split2(field[blk]) for field in fields], axis=0)
         place = places()
@@ -604,10 +614,10 @@
             store(blk, at(blk * STRIPS + c, STRIP), [halves(got[size * k : size * (k + 1)]) for k in range(len(fields))])
             return carry
 
-        lax.fori_loop(0, STRIPS, strip, 0)
+        repeat(STRIPS, strip)
         return carry
 
-    lax.fori_loop(0, 2, block, 0)
+    repeat(2, block)
 
 
 def unsort_kernel(rank, wa, wb, wc, out):
@@ -615,7 +625,7 @@
         for k, value in enumerate(values):
             out[16 * k : 16 * (k + 1), cols] = value
 
-    unsort(rank, (wa, wb, wc), store)
+    unsort(rank, (wa, wb, wc), store, each)
 
 
 def steps_kernel(mom, out, sound):
@@ -666,13 +676,13 @@
     c = [steps[:, k : k + 1] for k in range(7)]
 
     def part(b, carry):
-        here = at(b, 512)
+        here = at(b, BLK)
         w = [probes[:, here], u[0:16, here], u[16:32, here], u[32:48, here]]
         sol[:, here] = (c[0] * w[0] + c[1] * w[1]) + c[2] * w[2]
         res[:, here] = ((c[3] * w[0] + c[4] * w[1]) + c[5] * w[2]) + c[6] * w[3]
         return carry
 
-    lax.fori_loop(0, 2 * BLK // 512, part, 0)
+    each(2, part)
 
 
 def plain_product_kernel(flags, side, halo, got_a, got_b, d, acc, back, v, v2):
@@ -746,7 +756,7 @@
     def store(blk, cols, values):
         sol[:, cols], res[:, cols] = values
 
-    unsort(rank, (x, r), store)
+    unsort(rank, (x, r), store, looped)
 
 
 def plain_steps(flags, side, halo, rank, shape):
@@ -839,8 +849,6 @@
             pltpu.VMEM((3 * STRIPS, SUB), jnp.int32),
             pltpu.VMEM((1, BLK), f32),
             pltpu.VMEM((STRIP, SUB), f32),
-            pltpu.VMEM((80, BLK), bf16),
-            right,
             pltpu.SemaphoreType.DMA((4,)),
         ],
         10**9,

time: 80.5 us -> 67.1 us (0.83)
  Pallas kernels: 56.2 us -> 37.9 us
  starting transfers between devices: 21.5 us -> 26 us
    pallas_call x13, Pallas kernels: 56.2 us -> 37.9 us  [run(): pl.pallas_call(body, out_shape=outs, in_specs=ins, out_specs=out_specs, s...]
    ppermute x6, starting transfers between devices: 9.05 us -> 11.3 us  [sum_over(): lax.ppermute(value, axis, [(k, k ^ m * step) for k in range(count)])]
    ppermute x4, starting transfers between devices: 9.77 us -> 12.1 us  [swapped_both(): a = lax.ppermute(to_a, 'gx', [(k, k ^ 1) for k in range(count)])]
  transfers between devices with their start and end apart: 14 -> 14, of which waited for: 1 -> 2; matrix products, arithmetic and copies ran while one was open for 0% -> 0% of each run, Pallas kernels for 34% -> 29%
where the time goes in v1:
time: 67.1 us
  Pallas kernels  37.9 us (56%)
  starting transfers between devices  26 us (39%)
  waiting for transfers between devices  1.71 us (3%)
  between operations  1.48 us (2%)
    pallas_call x13, Pallas kernels, run(): pl.pallas_call(body, out_shape=outs, in_specs=ins, out_specs=out_specs, s...  37.9 us
    ppermute x4, starting transfers between devices, swapped_both(): a = lax.ppermute(to_a, 'gx', [(k, k ^ 1) for k in range(count)])  12.1 us
    ppermute x6, starting transfers between devices, sum_over(): lax.ppermute(value, axis, [(k, k ^ m * step) for k in range(count)])  11.3 us
    ppermute x4, starting transfers between devices, swapped_both(): lax.ppermute(to_b, 'gx', ends + [(k, (k + 1 ^ 1) - 1) for k in range(1, c...  2.63 us
    ppermute x6, waiting for transfers between devices, sum_over(): lax.ppermute(value, axis, [(k, k ^ m * step) for k in range(count)])  1.68 us
  transfers between devices with their start and end apart: 14, of which 2 were waited for; matrix products, arithmetic and copies ran while one was open for 0% of the time, Pallas kernels for 29%

profile of v1, /device:TPU:0, one launch (start us, length us, event | category | flops | bytes accessed | tf_op | source)
XLA Modules:
  0.0 67.1 jit_solution(832667921070091914)
XLA Ops:
  1.3 9.3 %sort_blocks.1 = (f32[2,24,2048]{2,1,0:T(8,128)S(1)}, f32[24,2048]{1,0:T(8,128)S(1)}, bf16[2,2048,64]{2,1,0:T(8,128)(2,1)S(1)}, s32[2,1,2048]{2,1,0:T(1,128)S(1)...) custom-call(f32[3,4096]{1,0:T(4,128)} %pts_hbm.1, f32[1,4096]{1,0:T(1,128)} %bitcast.7, ...), custom_call_target="tpu_custom_call" | custom-call | flops 1000000000 | bytes 1048576 | tf_op jit(solution)/shard_map/sort_blocks/pallas_call | solution.py:447
  10.6 0.5 collective-permute-start.22
  11.1 0.7 collective-permute-start.23
  11.7 5.8 %diag_build.1 = (bf16[2,8,256,512]{3,2,1,0:T(8,128)(2,1)S(1)}, f32[2,16,2048]{2,1,0:T(8,128)S(1)}) custom-call(s32[24,128]{1,0:T(8,128)S(4)} %get-tuple-element.106.tab, f32[2,24,2048]{2,1,0:T(8,128)S(1)} %get-tuple-element.105.side.w, bf16[2,2048,64]{2,1,0:T(8,128)(2,1)S(1)} %get-tuple-element.107.lhs), custom_call_target="tpu_custom_call" | custom-call | flops 3000000000 | bytes 1048576 | tf_op jit(solution)/shard_map/diag_build/pallas_call | solution.py:447
  17.6 5.0 %halo_build.1 = (bf16[8,256,768]{2,1,0:T(8,128)(2,1)S(1)}, bf16[8,256,128]{2,1,0:T(8,128)(2,1)S(1)}, s32[8,128]{1,0:T(8,128)S(4)}, f32[2,16,2048]{2,1,0:T(8,128)...) custom-call(s32[6]{0:T(128)S(4)} %get-tuple-element.104.flags, f32[2,24,2048]{2,1,0:T(8,128)S(1)} %get-tuple-element.105.side.w, ...), custom_call_target="tpu_custom_call" | custom-call | flops 3000000000 | bytes 1048576 | tf_op jit(solution)/shard_map/halo_build/pallas_call | solution.py:447
  22.6 4.4 %collective-permute-start.24 = (f32[16,2048]{1,0:T(8,128)S(1)}, f32[16,2048]{1,0:T(8,128)S(1)}, u32[]{:S(2)}, u32[]{:S(2)}) collective-permute-start(f32[16,2048]{1,0:T(8,128)S(1)} %get-tuple-element.118), channel_id=1, source_target_pairs={{0,1},{1,0},{2,3},{3,2},{4,5},{5,4},{6,7},{7,6},{8,9},{9,8},{10,11... | collective-permute-start | bytes 393224 | tf_op jit(solution)/shard_map/ppermute | solution.py:796
  27.0 0.7 collective-permute-start.25
  27.7 3.9 %own_build.1 = (bf16[8,256,768]{2,1,0:T(8,128)(2,1)S(1)}, bf16[8,256,128]{2,1,0:T(8,128)(2,1)S(1)}, f32[2,16,2048]{2,1,0:T(8,128)S(1)}) custom-call(s32[24,128]{1,0:T(8,128)S(4)} %get-tuple-element.106.tab, f32[2,24,2048]{2,1,0:T(8,128)S(1)} %get-tuple-element.105.side.w, bf16[2,2048,64]{2,1,0:T(8,128)(2,1)S(1)} %get-tuple-element.107.lhs, ...), custom_call_target="tpu_custom_call" | custom-call | flops 5000000000 | bytes 1048576 | tf_op jit(solution)/shard_map/own_build/pallas_call | solution.py:447
  31.6 0.9 %finish.2 = (f32[2,16,2048]{2,1,0:T(8,128)S(1)}, f32[16,2048]{1,0:T(8,128)S(1)}, f32[16,2048]{1,0:T(8,128)S(1)}, f32[16,128]{1,0:T(8,128)S(1)}) custom-call(s32[6]{0:T(128)S(4)} %get-tuple-element.104.flags, s32[8,128]{1,0:T(8,128)S(4)} %get-tuple-element.114.tab, bf16[8,256,768]{2,1,0:T(8,128)(2,1)S(1)} %get-tuple-element.115.k12, ...), custom_call_target="tpu_custom_call" | custom-call | flops 1000000000 | bytes 1048576 | tf_op jit(solution)/shard_map/finish/pallas_call | solution.py:447
  32.5 2.8 %collective-permute-start.26 = (f32[16,2048]{1,0:T(8,128)S(1)}, f32[16,2048]{1,0:T(8,128)S(1)}, u32[]{:S(2)}, u32[]{:S(2)}) collective-permute-start(f32[16,2048]{1,0:T(8,128)S(1)} %get-tuple-element.120), channel_id=1, source_target_pairs={{0,1},{1,0},{2,3},{3,2},{4,5},{5,4},{6,7},{7,6},{8,9},{9,8},{10,11... | collective-permute-start | bytes 393224 | tf_op jit(solution)/shard_map/ppermute | solution.py:796
  35.3 0.7 collective-permute-start.27
  35.9 3.1 %own_apply.2.acc_in = f32[2,16,2048]{2,1,0:T(8,128)S(1)} custom-call(s32[24,128]{1,0:T(8,128)S(4)} %get-tuple-element.106.tab, bf16[2,8,256,512]{3,2,1,0:T(8,128)(2,1)S(1)} %get-tuple-element.108.kd, bf16[8,256,768]{2,1,0:T(8,128)(2,1)S(1)} %get-tuple-element.112.k01, bf16[8,256,128]{2,1,0:T(8,128)(2,1)S(1)} %get-tuple-element.113.x01, ...), custom_call_target="tpu_custom_call" | custom-call | flops 2000000000 | bytes 1048576 | tf_op jit(solution)/shard_map/own_apply/pallas_call | solution.py:447
  39.1 1.9 %finish.3 = (f32[2,16,2048]{2,1,0:T(8,128)S(1)}, f32[16,2048]{1,0:T(8,128)S(1)}, f32[16,2048]{1,0:T(8,128)S(1)}, f32[16,128]{1,0:T(8,128)S(1)}) custom-call(s32[6]{0:T(128)S(4)} %get-tuple-element.104.flags, s32[8,128]{1,0:T(8,128)S(4)} %get-tuple-element.114.tab, bf16[8,256,768]{2,1,0:T(8,128)(2,1)S(1)} %get-tuple-element.115.k12, ...), custom_call_target="tpu_custom_call" | custom-call | flops 1000000000 | bytes 1048576 | tf_op jit(solution)/shard_map/finish/pallas_call | solution.py:447
  41.0 4.3 %collective-permute-start.28 = (f32[16,2048]{1,0:T(8,128)S(1)}, f32[16,2048]{1,0:T(8,128)S(1)}, u32[]{:S(2)}, u32[]{:S(2)}) collective-permute-start(f32[16,2048]{1,0:T(8,128)S(1)} %get-tuple-element.125), channel_id=1, source_target_pairs={{0,1},{1,0},{2,3},{3,2},{4,5},{5,4},{6,7},{7,6},{8,9},{9,8},{10,11... | collective-permute-start | bytes 393224 | tf_op jit(solution)/shard_map/ppermute | solution.py:796
  45.2 0.7 collective-permute-start.29
  45.9 3.1 %own_apply.3.acc = f32[2,16,2048]{2,1,0:T(8,128)S(1)} custom-call(s32[24,128]{1,0:T(8,128)S(4)} %get-tuple-element.106.tab, bf16[2,8,256,512]{3,2,1,0:T(8,128)(2,1)S(1)} %get-tuple-element.108.kd, bf16[8,256,768]{2,1,0:T(8,128)(2,1)S(1)} %get-tuple-element.112.k01, bf16[8,256,128]{2,1,0:T(8,128)(2,1)S(1)} %get-tuple-element.113.x01, ...), custom_call_target="tpu_custom_call" | custom-call | flops 2000000000 | bytes 1048576 | tf_op jit(solution)/shard_map/own_apply/pallas_call | solution.py:447
  49.2 7.6 %collective-permute-start.31 = (f32[16,128]{1,0:T(8,128)S(1)}, f32[16,128]{1,0:T(8,128)S(1)}, u32[]{:S(2)}, u32[]{:S(2)}) collective-permute-start(f32[16,128]{1,0:T(8,128)S(1)} %moment.1), channel_id=1, source_target_pairs={{0,2},{1,3},{2,0},{3,1},{4,6},{5,7},{6,4},{7,5},{8,10},{9,11},{10,... | collective-permute-start | bytes 24584 | tf_op jit(solution)/shard_map/ppermute | solution.py:810
  57.0 1.2 %last.1.wc = f32[2,16,2048]{2,1,0:T(8,128)S(1)} custom-call(s32[6]{0:T(128)S(4)} %get-tuple-element.104.flags, s32[8,128]{1,0:T(8,128)S(4)} %get-tuple-element.114.tab, bf16[8,256,768]{2,1,0:T(8,128)(2,1)S(1)} %get-tuple-element.115.k12, bf16[8,256,128]{2,1,0:T(8,128)(2,1)S(1)} %get-tuple-element.116.x12, f32[2,24,2048]{2,1,0:T(8,128)S(1)} %get-tuple-element.105.side.w, ...), custom_call_target="tpu_custom_call" | custom-call | flops 1000000000 | bytes 1048576 | tf_op jit(solution)/shard_map/last/pallas_call | solution.py:447
  58.4 1.4 %collective-permute-done.32 = f32[16,128]{1,0:T(8,128)S(1)} collective-permute-done((f32[16,128]{1,0:T(8,128)S(1)}, f32[16,128]{1,0:T(8,128)S(1)}, u32[]{:S(2)}, u32[]{:S(2)}) %collective-permute-start.32) | collective-permute-done | bytes 8224 | tf_op jit(solution)/shard_map/ppermute | solution.py:810
  60.0 2.0 %collective-permute-start.35 = (f32[16,128]{1,0:T(8,128)S(1)}, f32[16,128]{1,0:T(8,128)S(1)}, u32[]{:S(2)}, u32[]{:S(2)}) collective-permute-start(f32[16,128]{1,0:T(8,128)S(1)} %add_add_fusion.7), channel_id=1, source_target_pairs={{0,12},{1,13},{2,14},{3,15},{4,8},{5,9},{6,10},{7,11},{8,4},{9,5},... | collective-permute-start | bytes 24584 | tf_op jit(solution)/shard_map/ppermute | solution.py:810
  61.9 1.5 %collective-permute-start.33 = (f32[16,128]{1,0:T(8,128)S(1)}, f32[16,128]{1,0:T(8,128)S(1)}, u32[]{:S(2)}, u32[]{:S(2)}) collective-permute-start(f32[16,128]{1,0:T(8,128)S(1)} %add_add_fusion.7), channel_id=1, source_target_pairs={{0,4},{1,5},{2,6},{3,7},{4,0},{5,1},{6,2},{7,3},{8,12},{9,13},{10,... | collective-permute-start | bytes 24584 | tf_op jit(solution)/shard_map/ppermute | solution.py:810
  63.4 2.4 %unsort.1 = f32[48,4096]{1,0:T(8,128)S(1)} custom-call(s32[2,1,2048]{2,1,0:T(1,128)S(1)} %get-tuple-element.129.rank, f32[2,16,2048]{2,1,0:T(8,128)S(1)} %get-tuple-element.122.w.wa, f32[2,16,2048]{2,1,0:T(8,128)S(1)} %get-tuple-element.124.w.wb, f32[2,16,2048]{2,1,0:T(8,128)S(1)} %last.1.wc), custom_call_target="tpu_custom_call" | custom-call | flops 1610612736 | bytes 1048576 | tf_op jit(solution)/shard_map/unsort/pallas_call | solution.py:447
  66.1 1.0 %conditional.1 = ((f32[16,4096]{1,0:T(8,128)}, f32[16,4096]{1,0:T(8,128)})) conditional(s32[]{:T(128)} %bitcast.3, (f32[2,24,2048]{2,1,0:T(8,128)S(1)}, s32[6]{0:T(128)S(4)}, f32[24,2048]{1,0:T(8,128)S(1)}, s32[2,1,2048]{2,1,0:T(1,128)S(1)}) %tuple.17, (f32[16,128]{1,0:T(8,128)S(1)}, f32[16,4096]{1,0:T(8,128)S(1)}, f32[48,4096]{1,0:T(8,128)S(1)}) %tuple.18), branch_computations={%region_0.0_spmd, %region_3.0_spmd} | conditional | flops 60036864 | bytes 11600933 | solution.py:949
  66.2 1.0 %combine.1 = (f32[16,4096]{1,0:T(8,128)}, f32[16,4096]{1,0:T(8,128)}) custom-call(f32[16,128]{1,0:T(8,128)S(1)} %get-tuple-element.71.steps, f32[16,4096]{1,0:T(8,128)S(1)} %get-tuple-element.72.probes, f32[48,4096]{1,0:T(8,128)S(1)} %get-tuple-element.73.u), custom_call_target="tpu_custom_call" | custom-call | flops 1000000 | bytes 1048576 | tf_op jit(solution)/shard_map/cond/branch_1_fun/combine/pallas_call | solution.py:447
  (21 shorter events, 0.9 us)
Async XLA Ops:
  10.6 7.0 %collective-permute-start.22 = (f32[24,2048]{1,0:T(8,128)S(1)}, f32[24,2048]{1,0:T(8,128)S(1)}, u32[]{:S(2)}, u32[]{:S(2)}) collective-permute-start(f32[24,2048]{1,0:T(8,128)S(1)} %get-tuple-element.109), channel_id=1, source_target_pairs={{0,1},{1,0},{2,3},{3,2},{4,5},{5,4},{6,7},{7,6},{8,9},{9,8},{10,11... | collective-permute-start | bytes 589832 | tf_op jit(solution)/shard_map/ppermute | solution.py:796
  11.1 6.5 %collective-permute-start.23 = (f32[24,2048]{1,0:T(8,128)S(1)}, f32[24,2048]{1,0:T(8,128)S(1)}, u32[]{:S(2)}, u32[]{:S(2)}) collective-permute-start(f32[24,2048]{1,0:T(8,128)S(1)} %get-tuple-element.109), channel_id=1, source_target_pairs={{0,0},{15,15},{1,2},{2,1},{3,4},{4,3},{5,6},{6,5},{7,8},{8,7},{9,1... | collective-permute-start | bytes 589832 | tf_op jit(solution)/shard_map/ppermute | solution.py:798
  22.6 9.0 %collective-permute-start.24 = (f32[16,2048]{1,0:T(8,128)S(1)}, f32[16,2048]{1,0:T(8,128)S(1)}, u32[]{:S(2)}, u32[]{:S(2)}) collective-permute-start(f32[16,2048]{1,0:T(8,128)S(1)} %get-tuple-element.118), channel_id=1, source_target_pairs={{0,1},{1,0},{2,3},{3,2},{4,5},{5,4},{6,7},{7,6},{8,9},{9,8},{10,11... | collective-permute-start | bytes 393224 | tf_op jit(solution)/shard_map/ppermute | solution.py:796
  27.0 4.6 %collective-permute-start.25 = (f32[16,2048]{1,0:T(8,128)S(1)}, f32[16,2048]{1,0:T(8,128)S(1)}, u32[]{:S(2)}, u32[]{:S(2)}) collective-permute-start(f32[16,2048]{1,0:T(8,128)S(1)} %get-tuple-element.118), channel_id=1, source_target_pairs={{0,0},{15,15},{1,2},{2,1},{3,4},{4,3},{5,6},{6,5},{7,8},{8,7},{9,1... | collective-permute-start | bytes 393224 | tf_op jit(solution)/shard_map/ppermute | solution.py:798
  32.5 6.6 %collective-permute-start.26 = (f32[16,2048]{1,0:T(8,128)S(1)}, f32[16,2048]{1,0:T(8,128)S(1)}, u32[]{:S(2)}, u32[]{:S(2)}) collective-permute-start(f32[16,2048]{1,0:T(8,128)S(1)} %get-tuple-element.120), channel_id=1, source_target_pairs={{0,1},{1,0},{2,3},{3,2},{4,5},{5,4},{6,7},{7,6},{8,9},{9,8},{10,11... | collective-permute-start | bytes 393224 | tf_op jit(solution)/shard_map/ppermute | solution.py:796
  35.3 3.8 %collective-permute-start.27 = (f32[16,2048]{1,0:T(8,128)S(1)}, f32[16,2048]{1,0:T(8,128)S(1)}, u32[]{:S(2)}, u32[]{:S(2)}) collective-permute-start(f32[16,2048]{1,0:T(8,128)S(1)} %get-tuple-element.121), channel_id=1, source_target_pairs={{0,0},{15,15},{1,2},{2,1},{3,4},{4,3},{5,6},{6,5},{7,8},{8,7},{9,1... | collective-permute-start | bytes 393224 | tf_op jit(solution)/shard_map/ppermute | solution.py:798
  41.0 8.1 %collective-permute-start.28 = (f32[16,2048]{1,0:T(8,128)S(1)}, f32[16,2048]{1,0:T(8,128)S(1)}, u32[]{:S(2)}, u32[]{:S(2)}) collective-permute-start(f32[16,2048]{1,0:T(8,128)S(1)} %get-tuple-element.125), channel_id=1, source_target_pairs={{0,1},{1,0},{2,3},{3,2},{4,5},{5,4},{6,7},{7,6},{8,9},{9,8},{10,11... | collective-permute-start | bytes 393224 | tf_op jit(solution)/shard_map/ppermute | solution.py:796
  45.2 3.8 %collective-permute-start.29 = (f32[16,2048]{1,0:T(8,128)S(1)}, f32[16,2048]{1,0:T(8,128)S(1)}, u32[]{:S(2)}, u32[]{:S(2)}) collective-permute-start(f32[16,2048]{1,0:T(8,128)S(1)} %get-tuple-element.126), channel_id=1, source_target_pairs={{0,0},{15,15},{1,2},{2,1},{3,4},{4,3},{5,6},{6,5},{7,8},{8,7},{9,1... | collective-permute-start | bytes 393224 | tf_op jit(solution)/shard_map/ppermute | solution.py:798
  49.2 9.2 %collective-permute-start.31 = (f32[16,128]{1,0:T(8,128)S(1)}, f32[16,128]{1,0:T(8,128)S(1)}, u32[]{:S(2)}, u32[]{:S(2)}) collective-permute-start(f32[16,128]{1,0:T(8,128)S(1)} %moment.1), channel_id=1, source_target_pairs={{0,2},{1,3},{2,0},{3,1},{4,6},{5,7},{6,4},{7,5},{8,10},{9,11},{10,... | collective-permute-start | bytes 24584 | tf_op jit(solution)/shard_map/ppermute | solution.py:810
  56.8 3.1 %collective-permute-start.32 = (f32[16,128]{1,0:T(8,128)S(1)}, f32[16,128]{1,0:T(8,128)S(1)}, u32[]{:S(2)}, u32[]{:S(2)}) collective-permute-start(f32[16,128]{1,0:T(8,128)S(1)} %moment.1), channel_id=1, source_target_pairs={{0,3},{1,2},{2,1},{3,0},{4,7},{5,6},{6,5},{7,4},{8,11},{9,10},{10,... | collective-permute-start | bytes 24584 | tf_op jit(solution)/shard_map/ppermute | solution.py:810
  56.8 3.1 %collective-permute-start.30 = (f32[16,128]{1,0:T(8,128)S(1)}, f32[16,128]{1,0:T(8,128)S(1)}, u32[]{:S(2)}, u32[]{:S(2)}) collective-permute-start(f32[16,128]{1,0:T(8,128)S(1)} %moment.1), channel_id=1, source_target_pairs={{0,1},{1,0},{2,3},{3,2},{4,5},{5,4},{6,7},{7,6},{8,9},{9,8},{10,11... | collective-permute-start | bytes 24584 | tf_op jit(solution)/shard_map/ppermute | solution.py:810
  59.9 6.0 %collective-permute-start.34 = (f32[16,128]{1,0:T(8,128)S(1)}, f32[16,128]{1,0:T(8,128)S(1)}, u32[]{:S(2)}, u32[]{:S(2)}) collective-permute-start(f32[16,128]{1,0:T(8,128)S(1)} %add_add_fusion.7), channel_id=1, source_target_pairs={{0,8},{1,9},{2,10},{3,11},{4,12},{5,13},{6,14},{7,15},{8,0},{9,1},... | collective-permute-start | bytes 24584 | tf_op jit(solution)/shard_map/ppermute | solution.py:810
  60.0 5.9 %collective-permute-start.35 = (f32[16,128]{1,0:T(8,128)S(1)}, f32[16,128]{1,0:T(8,128)S(1)}, u32[]{:S(2)}, u32[]{:S(2)}) collective-permute-start(f32[16,128]{1,0:T(8,128)S(1)} %add_add_fusion.7), channel_id=1, source_target_pairs={{0,12},{1,13},{2,14},{3,15},{4,8},{5,9},{6,10},{7,11},{8,4},{9,5},... | collective-permute-start | bytes 24584 | tf_op jit(solution)/shard_map/ppermute | solution.py:810
  61.9 4.0 %collective-permute-start.33 = (f32[16,128]{1,0:T(8,128)S(1)}, f32[16,128]{1,0:T(8,128)S(1)}, u32[]{:S(2)}, u32[]{:S(2)}) collective-permute-start(f32[16,128]{1,0:T(8,128)S(1)} %add_add_fusion.7), channel_id=1, source_target_pairs={{0,4},{1,5},{2,6},{3,7},{4,0},{5,1},{6,2},{7,3},{8,12},{9,13},{10,... | collective-permute-start | bytes 24584 | tf_op jit(solution)/shard_map/ppermute | solution.py:810

commit v2 on v1

--- a/solution.py
+++ b/solution.py
@@ -14,6 +14,7 @@
 SUBS = BLK // SUB
 OFF_W = 768
 OFF_SUBS = OFF_W // SUB
+EDGE_W = 512
 DIAG_W = 512
 N_PROBES = 16
 N_FEATURES = 64
@@ -25,7 +26,7 @@
 f32 = jnp.float32
 bf16 = jnp.bfloat16
 
-T_START, T_END, T_EXTRA, T_LIVE = 0, 1, 2, 3
+T_START, T_END, T_EXTRA, T_LIVE, T_NEXT = 0, 1, 2, 3, 4
 
 
 def nt(left, right):
@@ -107,27 +108,23 @@
     lower = jnp.where(second < first, 1.0, 0.0).astype(bf16)
     ones = jnp.ones((STRIP, SUB), bf16)
     value = places()
-    before_ref[...] = jnp.zeros((STRIP, SUB), f32)
-
-    def count(j, carry):
-        before_ref[...] += nn(one_hot(key_ref[:, at(j, STRIP)].astype(bf16), value), ones)
-        return carry
-
-    each(STRIPS, count)
-    total = before_ref[...]
+    total = None
+    for j in range(STRIPS):
+        counts = nn(one_hot(key_ref[:, at(j, STRIP)].astype(bf16), value), ones)
+        before_ref[j] = counts
+        total = counts if total is None else total + counts
     coarse = jnp.floor(total * (1.0 / 16.0)) * 16.0
-    before_ref[...] = nn(lower, coarse.astype(bf16)) + nn(lower, (total - coarse).astype(bf16))
-
-    def place(j, carry):
+    before = nn(lower, coarse.astype(bf16)) + nn(lower, (total - coarse).astype(bf16))
+    for j in range(STRIPS):
+        after = before + before_ref[j]
+        before_ref[j] = before
+        before = after
+    for j in range(STRIPS):
         hit = one_hot(key_ref[:, at(j, STRIP)].astype(bf16), value)
-        before = before_ref[...]
+        before = before_ref[j]
         ahead = nn(hit, upper) + jnp.concatenate([before, before], axis=1)
         rank = jnp.sum(hit.astype(f32) * ahead, axis=0, keepdims=True)
         rank_ref[:, at(j, STRIP)] = rank.astype(jnp.int32)
-        before_ref[...] = before + nn(hit, ones)
-        return carry
-
-    each(STRIPS, place)
 
 
 def plan(row_side, col_side, live, diag):
@@ -148,14 +145,19 @@
     place = lane.astype(f32)
     reached = (group_low < high) & (group_high > low) & (lane < SUBS)
     end = jnp.max(jnp.where(reached, place + 1.0, 0.0), axis=1, keepdims=True)
+    strip = lax.broadcasted_iota(jnp.int32, (STRIPS, 1), 0)
     if diag:
-        start = lax.broadcasted_iota(jnp.int32, (STRIPS, 1), 0).astype(f32) * 2.0 + (DIAG_W // SUB - OFF_SUBS)
+        start = strip.astype(f32) * 2.0
+        after = start + DIAG_W // SUB
     else:
         first = jnp.min(jnp.where(reached, place, float(SUBS)), axis=1, keepdims=True)
-        start = jnp.minimum(first, float(SUBS - OFF_SUBS))
-    extra = jnp.sum(jnp.maximum(end - (start + OFF_SUBS), 0.0), axis=0, keepdims=True)
+        width = jnp.where((strip == 0) | (strip == STRIPS - 1), float(EDGE_W // SUB), float(OFF_SUBS))
+        start = jnp.minimum(first, SUBS - width)
+        after = start + width
+    extra = jnp.sum(jnp.maximum(end - after, 0.0), axis=0, keepdims=True)
     alive = live.astype(f32)
     table = jnp.where(lane == T_START, start, jnp.where(lane == T_END, end, extra))
+    table = jnp.where(lane == T_NEXT, after, table)
     return jnp.where(lane == T_LIVE, alive, table).astype(jnp.int32)
 
 
@@ -193,7 +195,7 @@
         copy.start()
     copies[0].wait()
     for blk in range(2):
-        fill_ranks(pts_ref[1:2, at(blk, BLK)], rank.at[blk], key_ref, before_ref)
+        fill_ranks(pts_ref[1:2, at(blk, BLK)], rank.at[blk], key_ref.at[blk], before_ref.at[blk])
     for copy in copies[1:]:
         copy.wait()
     for local in range(2):
@@ -315,7 +317,7 @@
     def _():
         def strip(i, carry):
             start = pl.multiple_of(tab_ref[base + i, T_START] * SUB, SUB)
-            fast_strip(k_ref, i, lhs, rhs, start, OFF_W)
+            fast_strip(k_ref, i, lhs, rhs, start, off_width(i))
             owner_strip(k_ref, i, start, v_col, acc_row)
             partner_strip(k_ref, i, start, v_row, acc_col)
             return carry
@@ -350,12 +352,18 @@
         diag_products(k_ref, v, acc, looped)
 
 
+def off_width(i):
+    return EDGE_W if isinstance(i, int) and i in (0, STRIPS - 1) else OFF_W
+
+
 def owner_strip(k_ref, i, start, v_col, acc_row):
-    acc_row[:, at(i, STRIP)] += halves(nt(v_col[:, pl.ds(start, OFF_W)], k_ref[i]))
+    width = off_width(i)
+    acc_row[:, at(i, STRIP)] += halves(nt(v_col[:, pl.ds(start, width)], k_ref[i, :, :width]))
 
 
 def partner_strip(k_ref, i, start, v_row, acc_col):
-    acc_col[:, pl.ds(start, OFF_W)] += halves(nn(v_row[:, at(i, STRIP)], k_ref[i]))
+    width = off_width(i)
+    acc_col[:, pl.ds(start, width)] += halves(nn(v_row[:, at(i, STRIP)], k_ref[i, :, :width]))
 
 
 def off_products(k_ref, tab_ref, base, v_row, v_col, acc_row, acc_col, repeat=each):
@@ -367,7 +375,9 @@
             partner_strip(k_ref, i, start, v_row, acc_col)
         return carry
 
-    repeat(STRIPS, strip)
+    strip(0, 0)
+    repeat(STRIPS - 2, lambda i, carry: strip(i + 1, carry))
+    strip(STRIPS - 1, 0)
 
 
 def diag_strip(k_ref, i, v_ref, acc_ref, width):
@@ -393,7 +403,7 @@
     def _():
         def strip(i, carry):
             here = pl.ds(pl.multiple_of(i * STRIP, STRIP), STRIP)
-            first = tab_ref[base + i, T_START] + OFF_SUBS
+            first = tab_ref[base + i, T_NEXT]
 
             def tile(j, carry):
                 col_at = pl.multiple_of(j * SUB, SUB)
@@ -847,8 +857,8 @@
             pltpu.VMEM(noise.shape, f32),
             pltpu.SMEM(pair_list.shape[::-1], jnp.int32),
             pltpu.VMEM((3 * STRIPS, SUB), jnp.int32),
-            pltpu.VMEM((1, BLK), f32),
-            pltpu.VMEM((STRIP, SUB), f32),
+            pltpu.VMEM((2, 1, BLK), f32),
+            pltpu.VMEM((2, STRIPS, STRIP, SUB), f32),
             pltpu.SemaphoreType.DMA((4,)),
         ],
         10**9,

time: 67.1 us -> 65.8 us (0.981); the launches traced: 67.1 us -> 64.7 us
  starting transfers between devices: 26 us -> 23.6 us
    ppermute x4, starting transfers between devices: 12.1 us -> 9.86 us  [swapped_both(): a = lax.ppermute(to_a, 'gx', [(k, k ^ 1) for k in range(count)])]
  transfers between devices with their start and end apart: 14 -> 14, of which waited for: 2 -> 2; matrix products, arithmetic and copies ran while one was open for 0% -> 0% of each run, Pallas kernels for 29% -> 30%
where the time goes in v2:
time: 65.8 us; the launch traced here: 64.7 us
  Pallas kernels  37.7 us (57%)
  starting transfers between devices  23.6 us (36%)
  waiting for transfers between devices  1.88 us (3%)
  between operations  1.5 us (2%)
    pallas_call x13, Pallas kernels, run(): pl.pallas_call(body, out_shape=outs, in_specs=ins, out_specs=out_specs, s...  37.7 us
    ppermute x6, starting transfers between devices, sum_over(): lax.ppermute(value, axis, [(k, k ^ m * step) for k in range(count)])  11.1 us
    ppermute x4, starting transfers between devices, swapped_both(): a = lax.ppermute(to_a, 'gx', [(k, k ^ 1) for k in range(count)])  9.86 us
    ppermute x4, starting transfers between devices, swapped_both(): lax.ppermute(to_b, 'gx', ends + [(k, (k + 1 ^ 1) - 1) for k in range(1, c...  2.63 us
    ppermute x6, waiting for transfers between devices, sum_over(): lax.ppermute(value, axis, [(k, k ^ m * step) for k in range(count)])  1.84 us
  transfers between devices with their start and end apart: 14, of which 2 were waited for; matrix products, arithmetic and copies ran while one was open for 0% of the time, Pallas kernels for 30%

profile of v2, /device:TPU:0, one launch (start us, length us, event | category | flops | bytes accessed | tf_op | source)
XLA Modules:
  0.0 64.7 jit_solution(8180734637109215216)
XLA Ops:
  1.3 8.9 %sort_blocks.1 = (f32[2,24,2048]{2,1,0:T(8,128)S(1)}, f32[24,2048]{1,0:T(8,128)S(1)}, bf16[2,2048,64]{2,1,0:T(8,128)(2,1)S(1)}, s32[2,1,2048]{2,1,0:T(1,128)S(1)...) custom-call(f32[3,4096]{1,0:T(4,128)} %pts_hbm.1, f32[1,4096]{1,0:T(1,128)} %bitcast.7, ...), custom_call_target="tpu_custom_call" | custom-call | flops 1000000000 | bytes 1048576 | tf_op jit(solution)/shard_map/sort_blocks/pallas_call | solution.py:457
  10.7 0.7 %collective-permute-start.23 = (f32[24,2048]{1,0:T(8,128)S(1)}, f32[24,2048]{1,0:T(8,128)S(1)}, u32[]{:S(2)}, u32[]{:S(2)}) collective-permute-start(f32[24,2048]{1,0:T(8,128)S(1)} %get-tuple-element.109), channel_id=1, source_target_pairs={{0,0},{15,15},{1,2},{2,1},{3,4},{4,3},{5,6},{6,5},{7,8},{8,7},{9,1... | collective-permute-start | bytes 589832 | tf_op jit(solution)/shard_map/ppermute | solution.py:808
  11.3 5.8 %diag_build.1 = (bf16[2,8,256,512]{3,2,1,0:T(8,128)(2,1)S(1)}, f32[2,16,2048]{2,1,0:T(8,128)S(1)}) custom-call(s32[24,128]{1,0:T(8,128)S(4)} %get-tuple-element.106.tab, f32[2,24,2048]{2,1,0:T(8,128)S(1)} %get-tuple-element.105.side.w, bf16[2,2048,64]{2,1,0:T(8,128)(2,1)S(1)} %get-tuple-element.107.lhs), custom_call_target="tpu_custom_call" | custom-call | flops 3000000000 | bytes 1048576 | tf_op jit(solution)/shard_map/diag_build/pallas_call | solution.py:457
  17.2 5.3 %halo_build.1 = (bf16[8,256,768]{2,1,0:T(8,128)(2,1)S(1)}, bf16[8,256,128]{2,1,0:T(8,128)(2,1)S(1)}, s32[8,128]{1,0:T(8,128)S(4)}, f32[2,16,2048]{2,1,0:T(8,128)...) custom-call(s32[6]{0:T(128)S(4)} %get-tuple-element.104.flags, f32[2,24,2048]{2,1,0:T(8,128)S(1)} %get-tuple-element.105.side.w, ...), custom_call_target="tpu_custom_call" | custom-call | flops 3000000000 | bytes 1048576 | tf_op jit(solution)/shard_map/halo_build/pallas_call | solution.py:457
  22.4 3.5 %collective-permute-start.24 = (f32[16,2048]{1,0:T(8,128)S(1)}, f32[16,2048]{1,0:T(8,128)S(1)}, u32[]{:S(2)}, u32[]{:S(2)}) collective-permute-start(f32[16,2048]{1,0:T(8,128)S(1)} %get-tuple-element.118), channel_id=1, source_target_pairs={{0,1},{1,0},{2,3},{3,2},{4,5},{5,4},{6,7},{7,6},{8,9},{9,8},{10,11... | collective-permute-start | bytes 393224 | tf_op jit(solution)/shard_map/ppermute | solution.py:806
  25.9 0.7 %collective-permute-start.25 = (f32[16,2048]{1,0:T(8,128)S(1)}, f32[16,2048]{1,0:T(8,128)S(1)}, u32[]{:S(2)}, u32[]{:S(2)}) collective-permute-start(f32[16,2048]{1,0:T(8,128)S(1)} %get-tuple-element.118), channel_id=1, source_target_pairs={{0,0},{15,15},{1,2},{2,1},{3,4},{4,3},{5,6},{6,5},{7,8},{8,7},{9,1... | collective-permute-start | bytes 393224 | tf_op jit(solution)/shard_map/ppermute | solution.py:808
  26.6 3.6 %own_build.1 = (bf16[8,256,768]{2,1,0:T(8,128)(2,1)S(1)}, bf16[8,256,128]{2,1,0:T(8,128)(2,1)S(1)}, f32[2,16,2048]{2,1,0:T(8,128)S(1)}) custom-call(s32[24,128]{1,0:T(8,128)S(4)} %get-tuple-element.106.tab, f32[2,24,2048]{2,1,0:T(8,128)S(1)} %get-tuple-element.105.side.w, bf16[2,2048,64]{2,1,0:T(8,128)(2,1)S(1)} %get-tuple-element.107.lhs, ...), custom_call_target="tpu_custom_call" | custom-call | flops 5000000000 | bytes 1048576 | tf_op jit(solution)/shard_map/own_build/pallas_call | solution.py:457
  30.3 0.9 %finish.2 = (f32[2,16,2048]{2,1,0:T(8,128)S(1)}, f32[16,2048]{1,0:T(8,128)S(1)}, f32[16,2048]{1,0:T(8,128)S(1)}, f32[16,128]{1,0:T(8,128)S(1)}) custom-call(s32[6]{0:T(128)S(4)} %get-tuple-element.104.flags, s32[8,128]{1,0:T(8,128)S(4)} %get-tuple-element.114.tab, bf16[8,256,768]{2,1,0:T(8,128)(2,1)S(1)} %get-tuple-element.115.k12, ...), custom_call_target="tpu_custom_call" | custom-call | flops 1000000000 | bytes 1048576 | tf_op jit(solution)/shard_map/finish/pallas_call | solution.py:457
  31.2 2.2 %collective-permute-start.26 = (f32[16,2048]{1,0:T(8,128)S(1)}, f32[16,2048]{1,0:T(8,128)S(1)}, u32[]{:S(2)}, u32[]{:S(2)}) collective-permute-start(f32[16,2048]{1,0:T(8,128)S(1)} %get-tuple-element.120), channel_id=1, source_target_pairs={{0,1},{1,0},{2,3},{3,2},{4,5},{5,4},{6,7},{7,6},{8,9},{9,8},{10,11... | collective-permute-start | bytes 393224 | tf_op jit(solution)/shard_map/ppermute | solution.py:806
  33.4 0.7 %collective-permute-start.27 = (f32[16,2048]{1,0:T(8,128)S(1)}, f32[16,2048]{1,0:T(8,128)S(1)}, u32[]{:S(2)}, u32[]{:S(2)}) collective-permute-start(f32[16,2048]{1,0:T(8,128)S(1)} %get-tuple-element.121), channel_id=1, source_target_pairs={{0,0},{15,15},{1,2},{2,1},{3,4},{4,3},{5,6},{6,5},{7,8},{8,7},{9,1... | collective-permute-start | bytes 393224 | tf_op jit(solution)/shard_map/ppermute | solution.py:808
  34.0 3.0 %own_apply.2.acc_in = f32[2,16,2048]{2,1,0:T(8,128)S(1)} custom-call(s32[24,128]{1,0:T(8,128)S(4)} %get-tuple-element.106.tab, bf16[2,8,256,512]{3,2,1,0:T(8,128)(2,1)S(1)} %get-tuple-element.108.kd, bf16[8,256,768]{2,1,0:T(8,128)(2,1)S(1)} %get-tuple-element.112.k01, bf16[8,256,128]{2,1,0:T(8,128)(2,1)S(1)} %get-tuple-element.113.x01, ...), custom_call_target="tpu_custom_call" | custom-call | flops 2000000000 | bytes 1048576 | tf_op jit(solution)/shard_map/own_apply/pallas_call | solution.py:457
  37.1 2.0 %finish.3 = (f32[2,16,2048]{2,1,0:T(8,128)S(1)}, f32[16,2048]{1,0:T(8,128)S(1)}, f32[16,2048]{1,0:T(8,128)S(1)}, f32[16,128]{1,0:T(8,128)S(1)}) custom-call(s32[6]{0:T(128)S(4)} %get-tuple-element.104.flags, s32[8,128]{1,0:T(8,128)S(4)} %get-tuple-element.114.tab, bf16[8,256,768]{2,1,0:T(8,128)(2,1)S(1)} %get-tuple-element.115.k12, ...), custom_call_target="tpu_custom_call" | custom-call | flops 1000000000 | bytes 1048576 | tf_op jit(solution)/shard_map/finish/pallas_call | solution.py:457
  39.1 3.7 %collective-permute-start.28 = (f32[16,2048]{1,0:T(8,128)S(1)}, f32[16,2048]{1,0:T(8,128)S(1)}, u32[]{:S(2)}, u32[]{:S(2)}) collective-permute-start(f32[16,2048]{1,0:T(8,128)S(1)} %get-tuple-element.125), channel_id=1, source_target_pairs={{0,1},{1,0},{2,3},{3,2},{4,5},{5,4},{6,7},{7,6},{8,9},{9,8},{10,11... | collective-permute-start | bytes 393224 | tf_op jit(solution)/shard_map/ppermute | solution.py:806
  42.8 0.7 %collective-permute-start.29 = (f32[16,2048]{1,0:T(8,128)S(1)}, f32[16,2048]{1,0:T(8,128)S(1)}, u32[]{:S(2)}, u32[]{:S(2)}) collective-permute-start(f32[16,2048]{1,0:T(8,128)S(1)} %get-tuple-element.126), channel_id=1, source_target_pairs={{0,0},{15,15},{1,2},{2,1},{3,4},{4,3},{5,6},{6,5},{7,8},{8,7},{9,1... | collective-permute-start | bytes 393224 | tf_op jit(solution)/shard_map/ppermute | solution.py:808
  43.5 3.0 %own_apply.3.acc = f32[2,16,2048]{2,1,0:T(8,128)S(1)} custom-call(s32[24,128]{1,0:T(8,128)S(4)} %get-tuple-element.106.tab, bf16[2,8,256,512]{3,2,1,0:T(8,128)(2,1)S(1)} %get-tuple-element.108.kd, bf16[8,256,768]{2,1,0:T(8,128)(2,1)S(1)} %get-tuple-element.112.k01, bf16[8,256,128]{2,1,0:T(8,128)(2,1)S(1)} %get-tuple-element.113.x01, ...), custom_call_target="tpu_custom_call" | custom-call | flops 2000000000 | bytes 1048576 | tf_op jit(solution)/shard_map/own_apply/pallas_call | solution.py:457
  46.7 7.3 %collective-permute-start.31 = (f32[16,128]{1,0:T(8,128)S(1)}, f32[16,128]{1,0:T(8,128)S(1)}, u32[]{:S(2)}, u32[]{:S(2)}) collective-permute-start(f32[16,128]{1,0:T(8,128)S(1)} %moment.1), channel_id=1, source_target_pairs={{0,2},{1,3},{2,0},{3,1},{4,6},{5,7},{6,4},{7,5},{8,10},{9,11},{10,... | collective-permute-start | bytes 24584 | tf_op jit(solution)/shard_map/ppermute | solution.py:820
  54.2 1.4 %last.1.wc = f32[2,16,2048]{2,1,0:T(8,128)S(1)} custom-call(s32[6]{0:T(128)S(4)} %get-tuple-element.104.flags, s32[8,128]{1,0:T(8,128)S(4)} %get-tuple-element.114.tab, bf16[8,256,768]{2,1,0:T(8,128)(2,1)S(1)} %get-tuple-element.115.k12, bf16[8,256,128]{2,1,0:T(8,128)(2,1)S(1)} %get-tuple-element.116.x12, f32[2,24,2048]{2,1,0:T(8,128)S(1)} %get-tuple-element.105.side.w, ...), custom_call_target="tpu_custom_call" | custom-call | flops 1000000000 | bytes 1048576 | tf_op jit(solution)/shard_map/last/pallas_call | solution.py:457
  55.7 1.4 %collective-permute-done.32 = f32[16,128]{1,0:T(8,128)S(1)} collective-permute-done((f32[16,128]{1,0:T(8,128)S(1)}, f32[16,128]{1,0:T(8,128)S(1)}, u32[]{:S(2)}, u32[]{:S(2)}) %collective-permute-start.32) | collective-permute-done | bytes 8224 | tf_op jit(solution)/shard_map/ppermute | solution.py:820
  57.1 0.9 %collective-permute-start.34 = (f32[16,128]{1,0:T(8,128)S(1)}, f32[16,128]{1,0:T(8,128)S(1)}, u32[]{:S(2)}, u32[]{:S(2)}) collective-permute-start(f32[16,128]{1,0:T(8,128)S(1)} %add_add_fusion.7), channel_id=1, source_target_pairs={{0,8},{1,9},{2,10},{3,11},{4,12},{5,13},{6,14},{7,15},{8,0},{9,1},... | collective-permute-start | bytes 24584 | tf_op jit(solution)/shard_map/ppermute | solution.py:820
  58.0 1.3 %collective-permute-start.35 = (f32[16,128]{1,0:T(8,128)S(1)}, f32[16,128]{1,0:T(8,128)S(1)}, u32[]{:S(2)}, u32[]{:S(2)}) collective-permute-start(f32[16,128]{1,0:T(8,128)S(1)} %add_add_fusion.7), channel_id=1, source_target_pairs={{0,12},{1,13},{2,14},{3,15},{4,8},{5,9},{6,10},{7,11},{8,4},{9,5},... | collective-permute-start | bytes 24584 | tf_op jit(solution)/shard_map/ppermute | solution.py:820
  59.4 1.3 %collective-permute-start.33 = (f32[16,128]{1,0:T(8,128)S(1)}, f32[16,128]{1,0:T(8,128)S(1)}, u32[]{:S(2)}, u32[]{:S(2)}) collective-permute-start(f32[16,128]{1,0:T(8,128)S(1)} %add_add_fusion.7), channel_id=1, source_target_pairs={{0,4},{1,5},{2,6},{3,7},{4,0},{5,1},{6,2},{7,3},{8,12},{9,13},{10,... | collective-permute-start | bytes 24584 | tf_op jit(solution)/shard_map/ppermute | solution.py:820
  60.7 2.4 %unsort.1 = f32[48,4096]{1,0:T(8,128)S(1)} custom-call(s32[2,1,2048]{2,1,0:T(1,128)S(1)} %get-tuple-element.129.rank, f32[2,16,2048]{2,1,0:T(8,128)S(1)} %get-tuple-element.122.w.wa, f32[2,16,2048]{2,1,0:T(8,128)S(1)} %get-tuple-element.124.w.wb, f32[2,16,2048]{2,1,0:T(8,128)S(1)} %last.1.wc), custom_call_target="tpu_custom_call" | custom-call | flops 1610612736 | bytes 1048576 | tf_op jit(solution)/shard_map/unsort/pallas_call | solution.py:457
  63.7 1.0 %conditional.1 = ((f32[16,4096]{1,0:T(8,128)}, f32[16,4096]{1,0:T(8,128)})) conditional(s32[]{:T(128)} %bitcast.3, (f32[2,24,2048]{2,1,0:T(8,128)S(1)}, s32[6]{0:T(128)S(4)}, f32[24,2048]{1,0:T(8,128)S(1)}, s32[2,1,2048]{2,1,0:T(1,128)S(1)}) %tuple.17, (f32[16,128]{1,0:T(8,128)S(1)}, f32[16,4096]{1,0:T(8,128)S(1)}, f32[48,4096]{1,0:T(8,128)S(1)}) %tuple.18), branch_computations={%region_0.0_spmd, %region_3.0_spmd} | conditional | flops 60036864 | bytes 11600933 | solution.py:959
  63.7 1.0 %combine.1 = (f32[16,4096]{1,0:T(8,128)}, f32[16,4096]{1,0:T(8,128)}) custom-call(f32[16,128]{1,0:T(8,128)S(1)} %get-tuple-element.71.steps, f32[16,4096]{1,0:T(8,128)S(1)} %get-tuple-element.72.probes, f32[48,4096]{1,0:T(8,128)S(1)} %get-tuple-element.73.u), custom_call_target="tpu_custom_call" | custom-call | flops 1000000 | bytes 1048576 | tf_op jit(solution)/shard_map/cond/branch_1_fun/combine/pallas_call | solution.py:457
  (21 shorter events, 1.5 us)
Async XLA Ops:
  10.2 7.0 %collective-permute-start.22 = (f32[24,2048]{1,0:T(8,128)S(1)}, f32[24,2048]{1,0:T(8,128)S(1)}, u32[]{:S(2)}, u32[]{:S(2)}) collective-permute-start(f32[24,2048]{1,0:T(8,128)S(1)} %get-tuple-element.109), channel_id=1, source_target_pairs={{0,1},{1,0},{2,3},{3,2},{4,5},{5,4},{6,7},{7,6},{8,9},{9,8},{10,11... | collective-permute-start | bytes 589832 | tf_op jit(solution)/shard_map/ppermute | solution.py:806
  10.7 6.5 %collective-permute-start.23 = (f32[24,2048]{1,0:T(8,128)S(1)}, f32[24,2048]{1,0:T(8,128)S(1)}, u32[]{:S(2)}, u32[]{:S(2)}) collective-permute-start(f32[24,2048]{1,0:T(8,128)S(1)} %get-tuple-element.109), channel_id=1, source_target_pairs={{0,0},{15,15},{1,2},{2,1},{3,4},{4,3},{5,6},{6,5},{7,8},{8,7},{9,1... | collective-permute-start | bytes 589832 | tf_op jit(solution)/shard_map/ppermute | solution.py:808
  22.4 7.8 %collective-permute-start.24 = (f32[16,2048]{1,0:T(8,128)S(1)}, f32[16,2048]{1,0:T(8,128)S(1)}, u32[]{:S(2)}, u32[]{:S(2)}) collective-permute-start(f32[16,2048]{1,0:T(8,128)S(1)} %get-tuple-element.118), channel_id=1, source_target_pairs={{0,1},{1,0},{2,3},{3,2},{4,5},{5,4},{6,7},{7,6},{8,9},{9,8},{10,11... | collective-permute-start | bytes 393224 | tf_op jit(solution)/shard_map/ppermute | solution.py:806
  25.9 4.3 %collective-permute-start.25 = (f32[16,2048]{1,0:T(8,128)S(1)}, f32[16,2048]{1,0:T(8,128)S(1)}, u32[]{:S(2)}, u32[]{:S(2)}) collective-permute-start(f32[16,2048]{1,0:T(8,128)S(1)} %get-tuple-element.118), channel_id=1, source_target_pairs={{0,0},{15,15},{1,2},{2,1},{3,4},{4,3},{5,6},{6,5},{7,8},{8,7},{9,1... | collective-permute-start | bytes 393224 | tf_op jit(solution)/shard_map/ppermute | solution.py:808
  31.2 5.9 %collective-permute-start.26 = (f32[16,2048]{1,0:T(8,128)S(1)}, f32[16,2048]{1,0:T(8,128)S(1)}, u32[]{:S(2)}, u32[]{:S(2)}) collective-permute-start(f32[16,2048]{1,0:T(8,128)S(1)} %get-tuple-element.120), channel_id=1, source_target_pairs={{0,1},{1,0},{2,3},{3,2},{4,5},{5,4},{6,7},{7,6},{8,9},{9,8},{10,11... | collective-permute-start | bytes 393224 | tf_op jit(solution)/shard_map/ppermute | solution.py:806
  33.4 3.7 %collective-permute-start.27 = (f32[16,2048]{1,0:T(8,128)S(1)}, f32[16,2048]{1,0:T(8,128)S(1)}, u32[]{:S(2)}, u32[]{:S(2)}) collective-permute-start(f32[16,2048]{1,0:T(8,128)S(1)} %get-tuple-element.121), channel_id=1, source_target_pairs={{0,0},{15,15},{1,2},{2,1},{3,4},{4,3},{5,6},{6,5},{7,8},{8,7},{9,1... | collective-permute-start | bytes 393224 | tf_op jit(solution)/shard_map/ppermute | solution.py:808
  39.1 7.4 %collective-permute-start.28 = (f32[16,2048]{1,0:T(8,128)S(1)}, f32[16,2048]{1,0:T(8,128)S(1)}, u32[]{:S(2)}, u32[]{:S(2)}) collective-permute-start(f32[16,2048]{1,0:T(8,128)S(1)} %get-tuple-element.125), channel_id=1, source_target_pairs={{0,1},{1,0},{2,3},{3,2},{4,5},{5,4},{6,7},{7,6},{8,9},{9,8},{10,11... | collective-permute-start | bytes 393224 | tf_op jit(solution)/shard_map/ppermute | solution.py:806
  42.8 3.7 %collective-permute-start.29 = (f32[16,2048]{1,0:T(8,128)S(1)}, f32[16,2048]{1,0:T(8,128)S(1)}, u32[]{:S(2)}, u32[]{:S(2)}) collective-permute-start(f32[16,2048]{1,0:T(8,128)S(1)} %get-tuple-element.126), channel_id=1, source_target_pairs={{0,0},{15,15},{1,2},{2,1},{3,4},{4,3},{5,6},{6,5},{7,8},{8,7},{9,1... | collective-permute-start | bytes 393224 | tf_op jit(solution)/shard_map/ppermute | solution.py:808
  46.7 9.0 %collective-permute-start.31 = (f32[16,128]{1,0:T(8,128)S(1)}, f32[16,128]{1,0:T(8,128)S(1)}, u32[]{:S(2)}, u32[]{:S(2)}) collective-permute-start(f32[16,128]{1,0:T(8,128)S(1)} %moment.1), channel_id=1, source_target_pairs={{0,2},{1,3},{2,0},{3,1},{4,6},{5,7},{6,4},{7,5},{8,10},{9,11},{10,... | collective-permute-start | bytes 24584 | tf_op jit(solution)/shard_map/ppermute | solution.py:820
  54.0 3.1 %collective-permute-start.32 = (f32[16,128]{1,0:T(8,128)S(1)}, f32[16,128]{1,0:T(8,128)S(1)}, u32[]{:S(2)}, u32[]{:S(2)}) collective-permute-start(f32[16,128]{1,0:T(8,128)S(1)} %moment.1), channel_id=1, source_target_pairs={{0,3},{1,2},{2,1},{3,0},{4,7},{5,6},{6,5},{7,4},{8,11},{9,10},{10,... | collective-permute-start | bytes 24584 | tf_op jit(solution)/shard_map/ppermute | solution.py:820
  54.0 3.1 %collective-permute-start.30 = (f32[16,128]{1,0:T(8,128)S(1)}, f32[16,128]{1,0:T(8,128)S(1)}, u32[]{:S(2)}, u32[]{:S(2)}) collective-permute-start(f32[16,128]{1,0:T(8,128)S(1)} %moment.1), channel_id=1, source_target_pairs={{0,1},{1,0},{2,3},{3,2},{4,5},{5,4},{6,7},{7,6},{8,9},{9,8},{10,11... | collective-permute-start | bytes 24584 | tf_op jit(solution)/shard_map/ppermute | solution.py:820
  57.1 6.0 %collective-permute-start.34 = (f32[16,128]{1,0:T(8,128)S(1)}, f32[16,128]{1,0:T(8,128)S(1)}, u32[]{:S(2)}, u32[]{:S(2)}) collective-permute-start(f32[16,128]{1,0:T(8,128)S(1)} %add_add_fusion.7), channel_id=1, source_target_pairs={{0,8},{1,9},{2,10},{3,11},{4,12},{5,13},{6,14},{7,15},{8,0},{9,1},... | collective-permute-start | bytes 24584 | tf_op jit(solution)/shard_map/ppermute | solution.py:820
  58.0 5.4 %collective-permute-start.35 = (f32[16,128]{1,0:T(8,128)S(1)}, f32[16,128]{1,0:T(8,128)S(1)}, u32[]{:S(2)}, u32[]{:S(2)}) collective-permute-start(f32[16,128]{1,0:T(8,128)S(1)} %add_add_fusion.7), channel_id=1, source_target_pairs={{0,12},{1,13},{2,14},{3,15},{4,8},{5,9},{6,10},{7,11},{8,4},{9,5},... | collective-permute-start | bytes 24584 | tf_op jit(solution)/shard_map/ppermute | solution.py:820
  59.4 4.1 %collective-permute-start.33 = (f32[16,128]{1,0:T(8,128)S(1)}, f32[16,128]{1,0:T(8,128)S(1)}, u32[]{:S(2)}, u32[]{:S(2)}) collective-permute-start(f32[16,128]{1,0:T(8,128)S(1)} %add_add_fusion.7), channel_id=1, source_target_pairs={{0,4},{1,5},{2,6},{3,7},{4,0},{5,1},{6,2},{7,3},{8,12},{9,13},{10,... | collective-permute-start | bytes 24584 | tf_op jit(solution)/shard_map/ppermute | solution.py:820

commit v3 on v2

--- a/solution.py
+++ b/solution.py
@@ -236,7 +236,8 @@
     copy = pltpu.make_async_copy(plan_ref, tab, sems.at[0])
     copy.start()
     for blk in range(2):
-        rows, _ = features(offset_of(side.at[blk], side.at[blk]), True)
+        rows, norm = features(offset_of(side.at[blk], side.at[blk]), True)
+        side[blk, 23:24, :] = norm
         rows = rows.astype(bf16)
         for c in range(STRIPS):
             lhs[blk, at(c, STRIP), :] = turned(rows[:, c * STRIP : (c + 1) * STRIP])
@@ -306,8 +307,7 @@
     offset = offset_of(col_side, row_side)
     rows, norm = features(offset, False)
     rhs[...] = rows.astype(bf16)
-    offset = offset_of(row_side, row_side)
-    return jnp.maximum(jnp.max(norm), jnp.max(jnp.sum(offset * offset, axis=0, keepdims=True))) <= 100.0
+    return jnp.max(jnp.maximum(norm, row_side[23:24, :])) <= 100.0
 
 
 def off_pair(k_ref, tab_ref, base, lhs, rhs, row_side, col_side, v_row, v_col, acc_row, acc_col):

time: 65.8 us -> 66.4 us (level); the launches traced: 64.7 us -> 67 us
  starting transfers between devices: 23.6 us -> 26 us
  Pallas kernels: 37.7 us -> 36.5 us
  waiting for transfers between devices: 1.88 us -> 3.08 us
    ppermute x4, starting transfers between devices: 9.86 us -> 11.3 us  [swapped_both(): a = lax.ppermute(to_a, 'gx', [(k, k ^ 1) for k in range(count)])]
    pallas_call x13, Pallas kernels: 37.7 us -> 36.5 us  [run(): pl.pallas_call(body, out_shape=outs, in_specs=ins, out_specs=out_specs, s...]
    ppermute x6, waiting for transfers between devices: 1.84 us -> 3.04 us  [sum_over(): lax.ppermute(value, axis, [(k, k ^ m * step) for k in range(count)])]
    ppermute x6, starting transfers between devices: 11.1 us -> 12 us  [sum_over(): lax.ppermute(value, axis, [(k, k ^ m * step) for k in range(count)])]
  transfers between devices with their start and end apart: 14 -> 14, of which waited for: 2 -> 2; matrix products, arithmetic and copies ran while one was open for 0% -> 0% of each run, Pallas kernels for 30% -> 28%
where the time goes in v3:
time: 66.4 us; the launch traced here: 67 us
  Pallas kernels  36.5 us (55%)
  starting transfers between devices  26 us (39%)
  waiting for transfers between devices  3.08 us (5%)
  between operations  1.51 us (2%)
    pallas_call x13, Pallas kernels, run(): pl.pallas_call(body, out_shape=outs, in_specs=ins, out_specs=out_specs, s...  36.5 us
    ppermute x6, starting transfers between devices, sum_over(): lax.ppermute(value, axis, [(k, k ^ m * step) for k in range(count)])  12 us
    ppermute x4, starting transfers between devices, swapped_both(): a = lax.ppermute(to_a, 'gx', [(k, k ^ 1) for k in range(count)])  11.3 us
    ppermute x6, waiting for transfers between devices, sum_over(): lax.ppermute(value, axis, [(k, k ^ m * step) for k in range(count)])  3.04 us
    ppermute x4, starting transfers between devices, swapped_both(): lax.ppermute(to_b, 'gx', ends + [(k, (k + 1 ^ 1) - 1) for k in range(1, c...  2.63 us
  transfers between devices with their start and end apart: 14, of which 2 were waited for; matrix products, arithmetic and copies ran while one was open for 0% of the time, Pallas kernels for 28%

profile of v3, /device:TPU:0, one launch (start us, length us, event | category | flops | bytes accessed | tf_op | source)
XLA Modules:
  0.0 67.0 jit_solution(16035386518521363809)
XLA Ops:
  1.3 8.9 %sort_blocks.1 = (f32[2,24,2048]{2,1,0:T(8,128)S(1)}, f32[24,2048]{1,0:T(8,128)S(1)}, bf16[2,2048,64]{2,1,0:T(8,128)(2,1)S(1)}, s32[2,1,2048]{2,1,0:T(1,128)S(1)...) custom-call(f32[3,4096]{1,0:T(4,128)} %pts_hbm.1, f32[1,4096]{1,0:T(1,128)} %bitcast.7, ...), custom_call_target="tpu_custom_call" | custom-call | flops 1000000000 | bytes 1048576 | tf_op jit(solution)/shard_map/sort_blocks/pallas_call | solution.py:457
  10.7 0.7 collective-permute-start.23
  11.3 5.8 %diag_build.1 = (bf16[2,8,256,512]{3,2,1,0:T(8,128)(2,1)S(1)}, f32[2,16,2048]{2,1,0:T(8,128)S(1)}) custom-call(s32[24,128]{1,0:T(8,128)S(4)} %get-tuple-element.106.tab, f32[2,24,2048]{2,1,0:T(8,128)S(1)} %get-tuple-element.105.side.w, bf16[2,2048,64]{2,1,0:T(8,128)(2,1)S(1)} %get-tuple-element.107.lhs), custom_call_target="tpu_custom_call" | custom-call | flops 3000000000 | bytes 1048576 | tf_op jit(solution)/shard_map/diag_build/pallas_call | solution.py:457
  17.1 4.7 %halo_build.1 = (bf16[8,256,768]{2,1,0:T(8,128)(2,1)S(1)}, bf16[8,256,128]{2,1,0:T(8,128)(2,1)S(1)}, s32[8,128]{1,0:T(8,128)S(4)}, f32[2,16,2048]{2,1,0:T(8,128)...) custom-call(s32[6]{0:T(128)S(4)} %get-tuple-element.104.flags, f32[2,24,2048]{2,1,0:T(8,128)S(1)} %get-tuple-element.105.side.w, ...), custom_call_target="tpu_custom_call" | custom-call | flops 3000000000 | bytes 1048576 | tf_op jit(solution)/shard_map/halo_build/pallas_call | solution.py:457
  21.9 4.0 %collective-permute-start.24 = (f32[16,2048]{1,0:T(8,128)S(1)}, f32[16,2048]{1,0:T(8,128)S(1)}, u32[]{:S(2)}, u32[]{:S(2)}) collective-permute-start(f32[16,2048]{1,0:T(8,128)S(1)} %get-tuple-element.118), channel_id=1, source_target_pairs={{0,1},{1,0},{2,3},{3,2},{4,5},{5,4},{6,7},{7,6},{8,9},{9,8},{10,11... | collective-permute-start | bytes 393224 | tf_op jit(solution)/shard_map/ppermute | solution.py:806
  26.5 3.6 %own_build.1 = (bf16[8,256,768]{2,1,0:T(8,128)(2,1)S(1)}, bf16[8,256,128]{2,1,0:T(8,128)(2,1)S(1)}, f32[2,16,2048]{2,1,0:T(8,128)S(1)}) custom-call(s32[24,128]{1,0:T(8,128)S(4)} %get-tuple-element.106.tab, f32[2,24,2048]{2,1,0:T(8,128)S(1)} %get-tuple-element.105.side.w, bf16[2,2048,64]{2,1,0:T(8,128)(2,1)S(1)} %get-tuple-element.107.lhs, ...), custom_call_target="tpu_custom_call" | custom-call | flops 5000000000 | bytes 1048576 | tf_op jit(solution)/shard_map/own_build/pallas_call | solution.py:457
  30.2 0.8 %finish.2 = (f32[2,16,2048]{2,1,0:T(8,128)S(1)}, f32[16,2048]{1,0:T(8,128)S(1)}, f32[16,2048]{1,0:T(8,128)S(1)}, f32[16,128]{1,0:T(8,128)S(1)}) custom-call(s32[6]{0:T(128)S(4)} %get-tuple-element.104.flags, s32[8,128]{1,0:T(8,128)S(4)} %get-tuple-element.114.tab, bf16[8,256,768]{2,1,0:T(8,128)(2,1)S(1)} %get-tuple-element.115.k12, ...), custom_call_target="tpu_custom_call" | custom-call | flops 1000000000 | bytes 1048576 | tf_op jit(solution)/shard_map/finish/pallas_call | solution.py:457
  31.0 3.4 %collective-permute-start.26 = (f32[16,2048]{1,0:T(8,128)S(1)}, f32[16,2048]{1,0:T(8,128)S(1)}, u32[]{:S(2)}, u32[]{:S(2)}) collective-permute-start(f32[16,2048]{1,0:T(8,128)S(1)} %get-tuple-element.120), channel_id=1, source_target_pairs={{0,1},{1,0},{2,3},{3,2},{4,5},{5,4},{6,7},{7,6},{8,9},{9,8},{10,11... | collective-permute-start | bytes 393224 | tf_op jit(solution)/shard_map/ppermute | solution.py:806
  34.4 0.7 collective-permute-start.27
  35.1 3.0 %own_apply.2.acc_in = f32[2,16,2048]{2,1,0:T(8,128)S(1)} custom-call(s32[24,128]{1,0:T(8,128)S(4)} %get-tuple-element.106.tab, bf16[2,8,256,512]{3,2,1,0:T(8,128)(2,1)S(1)} %get-tuple-element.108.kd, bf16[8,256,768]{2,1,0:T(8,128)(2,1)S(1)} %get-tuple-element.112.k01, bf16[8,256,128]{2,1,0:T(8,128)(2,1)S(1)} %get-tuple-element.113.x01, ...), custom_call_target="tpu_custom_call" | custom-call | flops 2000000000 | bytes 1048576 | tf_op jit(solution)/shard_map/own_apply/pallas_call | solution.py:457
  38.2 1.7 %finish.3 = (f32[2,16,2048]{2,1,0:T(8,128)S(1)}, f32[16,2048]{1,0:T(8,128)S(1)}, f32[16,2048]{1,0:T(8,128)S(1)}, f32[16,128]{1,0:T(8,128)S(1)}) custom-call(s32[6]{0:T(128)S(4)} %get-tuple-element.104.flags, s32[8,128]{1,0:T(8,128)S(4)} %get-tuple-element.114.tab, bf16[8,256,768]{2,1,0:T(8,128)(2,1)S(1)} %get-tuple-element.115.k12, ...), custom_call_target="tpu_custom_call" | custom-call | flops 1000000000 | bytes 1048576 | tf_op jit(solution)/shard_map/finish/pallas_call | solution.py:457
  39.9 3.4 %collective-permute-start.28 = (f32[16,2048]{1,0:T(8,128)S(1)}, f32[16,2048]{1,0:T(8,128)S(1)}, u32[]{:S(2)}, u32[]{:S(2)}) collective-permute-start(f32[16,2048]{1,0:T(8,128)S(1)} %get-tuple-element.125), channel_id=1, source_target_pairs={{0,1},{1,0},{2,3},{3,2},{4,5},{5,4},{6,7},{7,6},{8,9},{9,8},{10,11... | collective-permute-start | bytes 393224 | tf_op jit(solution)/shard_map/ppermute | solution.py:806
  43.3 0.7 collective-permute-start.29
  43.9 3.0 %own_apply.3.acc = f32[2,16,2048]{2,1,0:T(8,128)S(1)} custom-call(s32[24,128]{1,0:T(8,128)S(4)} %get-tuple-element.106.tab, bf16[2,8,256,512]{3,2,1,0:T(8,128)(2,1)S(1)} %get-tuple-element.108.kd, bf16[8,256,768]{2,1,0:T(8,128)(2,1)S(1)} %get-tuple-element.112.k01, bf16[8,256,128]{2,1,0:T(8,128)(2,1)S(1)} %get-tuple-element.113.x01, ...), custom_call_target="tpu_custom_call" | custom-call | flops 2000000000 | bytes 1048576 | tf_op jit(solution)/shard_map/own_apply/pallas_call | solution.py:457
  47.1 5.8 %collective-permute-start.31 = (f32[16,128]{1,0:T(8,128)S(1)}, f32[16,128]{1,0:T(8,128)S(1)}, u32[]{:S(2)}, u32[]{:S(2)}) collective-permute-start(f32[16,128]{1,0:T(8,128)S(1)} %moment.1), channel_id=1, source_target_pairs={{0,2},{1,3},{2,0},{3,1},{4,6},{5,7},{6,4},{7,5},{8,10},{9,11},{10,... | collective-permute-start | bytes 24584 | tf_op jit(solution)/shard_map/ppermute | solution.py:820
  53.0 1.1 %collective-permute-start.32 = (f32[16,128]{1,0:T(8,128)S(1)}, f32[16,128]{1,0:T(8,128)S(1)}, u32[]{:S(2)}, u32[]{:S(2)}) collective-permute-start(f32[16,128]{1,0:T(8,128)S(1)} %moment.1), channel_id=1, source_target_pairs={{0,3},{1,2},{2,1},{3,0},{4,7},{5,6},{6,5},{7,4},{8,11},{9,10},{10,... | collective-permute-start | bytes 24584 | tf_op jit(solution)/shard_map/ppermute | solution.py:820
  54.1 1.2 %last.1.wc = f32[2,16,2048]{2,1,0:T(8,128)S(1)} custom-call(s32[6]{0:T(128)S(4)} %get-tuple-element.104.flags, s32[8,128]{1,0:T(8,128)S(4)} %get-tuple-element.114.tab, bf16[8,256,768]{2,1,0:T(8,128)(2,1)S(1)} %get-tuple-element.115.k12, bf16[8,256,128]{2,1,0:T(8,128)(2,1)S(1)} %get-tuple-element.116.x12, f32[2,24,2048]{2,1,0:T(8,128)S(1)} %get-tuple-element.105.side.w, ...), custom_call_target="tpu_custom_call" | custom-call | flops 1000000000 | bytes 1048576 | tf_op jit(solution)/shard_map/last/pallas_call | solution.py:457
  55.2 0.8 %collective-permute-done.32 = f32[16,128]{1,0:T(8,128)S(1)} collective-permute-done((f32[16,128]{1,0:T(8,128)S(1)}, f32[16,128]{1,0:T(8,128)S(1)}, u32[]{:S(2)}, u32[]{:S(2)}) %collective-permute-start.32) | collective-permute-done | bytes 8224 | tf_op jit(solution)/shard_map/ppermute | solution.py:820
  56.0 4.3 %collective-permute-start.34 = (f32[16,128]{1,0:T(8,128)S(1)}, f32[16,128]{1,0:T(8,128)S(1)}, u32[]{:S(2)}, u32[]{:S(2)}) collective-permute-start(f32[16,128]{1,0:T(8,128)S(1)} %add_add_fusion.7), channel_id=1, source_target_pairs={{0,8},{1,9},{2,10},{3,11},{4,12},{5,13},{6,14},{7,15},{8,0},{9,1},... | collective-permute-start | bytes 24584 | tf_op jit(solution)/shard_map/ppermute | solution.py:820
  60.4 0.7 %collective-permute-start.35 = (f32[16,128]{1,0:T(8,128)S(1)}, f32[16,128]{1,0:T(8,128)S(1)}, u32[]{:S(2)}, u32[]{:S(2)}) collective-permute-start(f32[16,128]{1,0:T(8,128)S(1)} %add_add_fusion.7), channel_id=1, source_target_pairs={{0,12},{1,13},{2,14},{3,15},{4,8},{5,9},{6,10},{7,11},{8,4},{9,5},... | collective-permute-start | bytes 24584 | tf_op jit(solution)/shard_map/ppermute | solution.py:820
  61.1 2.4 %unsort.1 = f32[48,4096]{1,0:T(8,128)S(1)} custom-call(s32[2,1,2048]{2,1,0:T(1,128)S(1)} %get-tuple-element.129.rank, f32[2,16,2048]{2,1,0:T(8,128)S(1)} %get-tuple-element.122.w.wa, f32[2,16,2048]{2,1,0:T(8,128)S(1)} %get-tuple-element.124.w.wb, f32[2,16,2048]{2,1,0:T(8,128)S(1)} %last.1.wc), custom_call_target="tpu_custom_call" | custom-call | flops 1610612736 | bytes 1048576 | tf_op jit(solution)/shard_map/unsort/pallas_call | solution.py:457
  63.6 2.2 %collective-permute-done.35 = f32[16,128]{1,0:T(8,128)S(1)} collective-permute-done((f32[16,128]{1,0:T(8,128)S(1)}, f32[16,128]{1,0:T(8,128)S(1)}, u32[]{:S(2)}, u32[]{:S(2)}) %collective-permute-start.35) | collective-permute-done | bytes 8224 | tf_op jit(solution)/shard_map/ppermute | solution.py:820
  66.0 1.0 %conditional.1 = ((f32[16,4096]{1,0:T(8,128)}, f32[16,4096]{1,0:T(8,128)})) conditional(s32[]{:T(128)} %bitcast.3, (f32[2,24,2048]{2,1,0:T(8,128)S(1)}, s32[6]{0:T(128)S(4)}, f32[24,2048]{1,0:T(8,128)S(1)}, s32[2,1,2048]{2,1,0:T(1,128)S(1)}) %tuple.17, (f32[16,128]{1,0:T(8,128)S(1)}, f32[16,4096]{1,0:T(8,128)S(1)}, f32[48,4096]{1,0:T(8,128)S(1)}) %tuple.18), branch_computations={%region_0.0_spmd, %region_3.0_spmd} | conditional | flops 60036864 | bytes 11600933 | solution.py:959
  66.0 1.0 %combine.1 = (f32[16,4096]{1,0:T(8,128)}, f32[16,4096]{1,0:T(8,128)}) custom-call(f32[16,128]{1,0:T(8,128)S(1)} %get-tuple-element.71.steps, f32[16,4096]{1,0:T(8,128)S(1)} %get-tuple-element.72.probes, f32[48,4096]{1,0:T(8,128)S(1)} %get-tuple-element.73.u), custom_call_target="tpu_custom_call" | custom-call | flops 1000000 | bytes 1048576 | tf_op jit(solution)/shard_map/cond/branch_1_fun/combine/pallas_call | solution.py:457
  (21 shorter events, 1.7 us)
Async XLA Ops:
  10.2 7.0 %collective-permute-start.22 = (f32[24,2048]{1,0:T(8,128)S(1)}, f32[24,2048]{1,0:T(8,128)S(1)}, u32[]{:S(2)}, u32[]{:S(2)}) collective-permute-start(f32[24,2048]{1,0:T(8,128)S(1)} %get-tuple-element.109), channel_id=1, source_target_pairs={{0,1},{1,0},{2,3},{3,2},{4,5},{5,4},{6,7},{7,6},{8,9},{9,8},{10,11... | collective-permute-start | bytes 589832 | tf_op jit(solution)/shard_map/ppermute | solution.py:806
  10.7 6.5 %collective-permute-start.23 = (f32[24,2048]{1,0:T(8,128)S(1)}, f32[24,2048]{1,0:T(8,128)S(1)}, u32[]{:S(2)}, u32[]{:S(2)}) collective-permute-start(f32[24,2048]{1,0:T(8,128)S(1)} %get-tuple-element.109), channel_id=1, source_target_pairs={{0,0},{15,15},{1,2},{2,1},{3,4},{4,3},{5,6},{6,5},{7,8},{8,7},{9,1... | collective-permute-start | bytes 589832 | tf_op jit(solution)/shard_map/ppermute | solution.py:808
  21.9 8.3 %collective-permute-start.24 = (f32[16,2048]{1,0:T(8,128)S(1)}, f32[16,2048]{1,0:T(8,128)S(1)}, u32[]{:S(2)}, u32[]{:S(2)}) collective-permute-start(f32[16,2048]{1,0:T(8,128)S(1)} %get-tuple-element.118), channel_id=1, source_target_pairs={{0,1},{1,0},{2,3},{3,2},{4,5},{5,4},{6,7},{7,6},{8,9},{9,8},{10,11... | collective-permute-start | bytes 393224 | tf_op jit(solution)/shard_map/ppermute | solution.py:806
  25.9 4.3 %collective-permute-start.25 = (f32[16,2048]{1,0:T(8,128)S(1)}, f32[16,2048]{1,0:T(8,128)S(1)}, u32[]{:S(2)}, u32[]{:S(2)}) collective-permute-start(f32[16,2048]{1,0:T(8,128)S(1)} %get-tuple-element.118), channel_id=1, source_target_pairs={{0,0},{15,15},{1,2},{2,1},{3,4},{4,3},{5,6},{6,5},{7,8},{8,7},{9,1... | collective-permute-start | bytes 393224 | tf_op jit(solution)/shard_map/ppermute | solution.py:808
  31.0 7.1 %collective-permute-start.26 = (f32[16,2048]{1,0:T(8,128)S(1)}, f32[16,2048]{1,0:T(8,128)S(1)}, u32[]{:S(2)}, u32[]{:S(2)}) collective-permute-start(f32[16,2048]{1,0:T(8,128)S(1)} %get-tuple-element.120), channel_id=1, source_target_pairs={{0,1},{1,0},{2,3},{3,2},{4,5},{5,4},{6,7},{7,6},{8,9},{9,8},{10,11... | collective-permute-start | bytes 393224 | tf_op jit(solution)/shard_map/ppermute | solution.py:806
  34.4 3.7 %collective-permute-start.27 = (f32[16,2048]{1,0:T(8,128)S(1)}, f32[16,2048]{1,0:T(8,128)S(1)}, u32[]{:S(2)}, u32[]{:S(2)}) collective-permute-start(f32[16,2048]{1,0:T(8,128)S(1)} %get-tuple-element.121), channel_id=1, source_target_pairs={{0,0},{15,15},{1,2},{2,1},{3,4},{4,3},{5,6},{6,5},{7,8},{8,7},{9,1... | collective-permute-start | bytes 393224 | tf_op jit(solution)/shard_map/ppermute | solution.py:808
  39.9 7.1 %collective-permute-start.28 = (f32[16,2048]{1,0:T(8,128)S(1)}, f32[16,2048]{1,0:T(8,128)S(1)}, u32[]{:S(2)}, u32[]{:S(2)}) collective-permute-start(f32[16,2048]{1,0:T(8,128)S(1)} %get-tuple-element.125), channel_id=1, source_target_pairs={{0,1},{1,0},{2,3},{3,2},{4,5},{5,4},{6,7},{7,6},{8,9},{9,8},{10,11... | collective-permute-start | bytes 393224 | tf_op jit(solution)/shard_map/ppermute | solution.py:806
  43.3 3.7 %collective-permute-start.29 = (f32[16,2048]{1,0:T(8,128)S(1)}, f32[16,2048]{1,0:T(8,128)S(1)}, u32[]{:S(2)}, u32[]{:S(2)}) collective-permute-start(f32[16,2048]{1,0:T(8,128)S(1)} %get-tuple-element.126), channel_id=1, source_target_pairs={{0,0},{15,15},{1,2},{2,1},{3,4},{4,3},{5,6},{6,5},{7,8},{8,7},{9,1... | collective-permute-start | bytes 393224 | tf_op jit(solution)/shard_map/ppermute | solution.py:808
  47.1 8.1 %collective-permute-start.31 = (f32[16,128]{1,0:T(8,128)S(1)}, f32[16,128]{1,0:T(8,128)S(1)}, u32[]{:S(2)}, u32[]{:S(2)}) collective-permute-start(f32[16,128]{1,0:T(8,128)S(1)} %moment.1), channel_id=1, source_target_pairs={{0,2},{1,3},{2,0},{3,1},{4,6},{5,7},{6,4},{7,5},{8,10},{9,11},{10,... | collective-permute-start | bytes 24584 | tf_op jit(solution)/shard_map/ppermute | solution.py:820
  53.0 3.1 %collective-permute-start.32 = (f32[16,128]{1,0:T(8,128)S(1)}, f32[16,128]{1,0:T(8,128)S(1)}, u32[]{:S(2)}, u32[]{:S(2)}) collective-permute-start(f32[16,128]{1,0:T(8,128)S(1)} %moment.1), channel_id=1, source_target_pairs={{0,3},{1,2},{2,1},{3,0},{4,7},{5,6},{6,5},{7,4},{8,11},{9,10},{10,... | collective-permute-start | bytes 24584 | tf_op jit(solution)/shard_map/ppermute | solution.py:820
  54.0 2.0 %collective-permute-start.30 = (f32[16,128]{1,0:T(8,128)S(1)}, f32[16,128]{1,0:T(8,128)S(1)}, u32[]{:S(2)}, u32[]{:S(2)}) collective-permute-start(f32[16,128]{1,0:T(8,128)S(1)} %moment.1), channel_id=1, source_target_pairs={{0,1},{1,0},{2,3},{3,2},{4,5},{5,4},{6,7},{7,6},{8,9},{9,8},{10,11... | collective-permute-start | bytes 24584 | tf_op jit(solution)/shard_map/ppermute | solution.py:820
  56.0 7.5 %collective-permute-start.34 = (f32[16,128]{1,0:T(8,128)S(1)}, f32[16,128]{1,0:T(8,128)S(1)}, u32[]{:S(2)}, u32[]{:S(2)}) collective-permute-start(f32[16,128]{1,0:T(8,128)S(1)} %add_add_fusion.7), channel_id=1, source_target_pairs={{0,8},{1,9},{2,10},{3,11},{4,12},{5,13},{6,14},{7,15},{8,0},{9,1},... | collective-permute-start | bytes 24584 | tf_op jit(solution)/shard_map/ppermute | solution.py:820
  60.4 5.4 %collective-permute-start.35 = (f32[16,128]{1,0:T(8,128)S(1)}, f32[16,128]{1,0:T(8,128)S(1)}, u32[]{:S(2)}, u32[]{:S(2)}) collective-permute-start(f32[16,128]{1,0:T(8,128)S(1)} %add_add_fusion.7), channel_id=1, source_target_pairs={{0,12},{1,13},{2,14},{3,15},{4,8},{5,9},{6,10},{7,11},{8,4},{9,5},... | collective-permute-start | bytes 24584 | tf_op jit(solution)/shard_map/ppermute | solution.py:820
  61.1 4.7 %collective-permute-start.33 = (f32[16,128]{1,0:T(8,128)S(1)}, f32[16,128]{1,0:T(8,128)S(1)}, u32[]{:S(2)}, u32[]{:S(2)}) collective-permute-start(f32[16,128]{1,0:T(8,128)S(1)} %add_add_fusion.7), channel_id=1, source_target_pairs={{0,4},{1,5},{2,6},{3,7},{4,0},{5,1},{6,2},{7,3},{8,12},{9,13},{10,... | collective-permute-start | bytes 24584 | tf_op jit(solution)/shard_map/ppermute | solution.py:820

commit v4 on v3

--- a/solution.py
+++ b/solution.py
@@ -414,14 +414,27 @@
                         row_at = pl.multiple_of(i * STRIP + g * SUB, SUB)
                         tile_ref[g * SUB : (g + 1) * SUB, :] = tile_by_difference(row_side, row_at, col_side, col_at)
 
-                if kept is None:
-                    by_difference()
-                elif fill is None:
-                    pl.when(j > first)(by_difference)
+                def multiply(values):
+                    if acc_row is not None:
+                        acc_row[:, here] += halves(nt(v_col[:, there], values))
+                    if acc_col is not None:
+                        acc_col[:, there] += halves(nn(v_row[:, here], values))
+
+                if kept is not None and fill is None:
 
                     @pl.when(j == first)
                     def _():
-                        tile_ref[...] = kept[i]
+                        multiply(kept[i])
+
+                    @pl.when(j > first)
+                    def _():
+                        by_difference()
+                        multiply(tile_ref[...])
+
+                    return carry
+
+                if fill is None:
+                    by_difference()
                 else:
                     near, lhs, rhs = fill
                     pl.when(jnp.logical_not(near))(by_difference)
@@ -434,10 +447,7 @@
                     def _():
                         kept[i] = tile_ref[...]
 
-                if acc_row is not None:
-                    acc_row[:, here] += halves(nt(v_col[:, there], tile_ref[...]))
-                if acc_col is not None:
-                    acc_col[:, there] += halves(nn(v_row[:, here], tile_ref[...]))
+                multiply(tile_ref[...])
                 return carry
 
             return lax.fori_loop(first, tab_ref[base + i, T_END], tile, carry)

time: 66.4 us -> 65.5 us (0.986); the launches traced: 67 us -> 65.2 us
  starting transfers between devices: 26 us -> 21 us
  Pallas kernels: 36.5 us -> 40.4 us
  waiting for transfers between devices: 3.08 us -> 2.26 us
    pallas_call x13, Pallas kernels: 36.5 us -> 40.4 us  [run(): pl.pallas_call(body, out_shape=outs, in_specs=ins, out_specs=out_specs, s...]
    ppermute x4, starting transfers between devices: 11.3 us -> 7.83 us  [swapped_both(): a = lax.ppermute(to_a, 'gx', [(k, k ^ 1) for k in range(count)])]
    ppermute x6, starting transfers between devices: 12 us -> 10.5 us  [sum_over(): lax.ppermute(value, axis, [(k, k ^ m * step) for k in range(count)])]
    ppermute x6, waiting for transfers between devices: 3.04 us -> 2.23 us  [sum_over(): lax.ppermute(value, axis, [(k, k ^ m * step) for k in range(count)])]
  transfers between devices with their start and end apart: 14 -> 14, of which waited for: 2 -> 2; matrix products, arithmetic and copies ran while one was open for 0% -> 0% of each run, Pallas kernels for 28% -> 32%
where the time goes in v4:
time: 65.5 us; the launch traced here: 65.2 us
  Pallas kernels  40.4 us (62%)
  starting transfers between devices  21 us (32%)
  waiting for transfers between devices  2.26 us (3%)
  between operations  1.46 us (2%)
    pallas_call x13, Pallas kernels, run(): pl.pallas_call(body, out_shape=outs, in_specs=ins, out_specs=out_specs, s...  40.4 us
    ppermute x6, starting transfers between devices, sum_over(): lax.ppermute(value, axis, [(k, k ^ m * step) for k in range(count)])  10.5 us
    ppermute x4, starting transfers between devices, swapped_both(): a = lax.ppermute(to_a, 'gx', [(k, k ^ 1) for k in range(count)])  7.83 us
    ppermute x4, starting transfers between devices, swapped_both(): lax.ppermute(to_b, 'gx', ends + [(k, (k + 1 ^ 1) - 1) for k in range(1, c...  2.63 us
    ppermute x6, waiting for transfers between devices, sum_over(): lax.ppermute(value, axis, [(k, k ^ m * step) for k in range(count)])  2.23 us
  transfers between devices with their start and end apart: 14, of which 2 were waited for; matrix products, arithmetic and copies ran while one was open for 0% of the time, Pallas kernels for 32%

profile of v4, /device:TPU:0, one launch (start us, length us, event | category | flops | bytes accessed | tf_op | source)
XLA Modules:
  0.0 65.2 jit_solution(8401070334801864553)
XLA Ops:
  1.3 8.9 %sort_blocks.1 = (f32[2,24,2048]{2,1,0:T(8,128)S(1)}, f32[24,2048]{1,0:T(8,128)S(1)}, bf16[2,2048,64]{2,1,0:T(8,128)(2,1)S(1)}, s32[2,1,2048]{2,1,0:T(1,128)S(1)...) custom-call(f32[3,4096]{1,0:T(4,128)} %pts_hbm.1, f32[1,4096]{1,0:T(1,128)} %bitcast.7, ...), custom_call_target="tpu_custom_call" | custom-call | flops 1000000000 | bytes 1048576 | tf_op jit(solution)/shard_map/sort_blocks/pallas_call | solution.py:467
  10.7 0.7 %collective-permute-start.23 = (f32[24,2048]{1,0:T(8,128)S(1)}, f32[24,2048]{1,0:T(8,128)S(1)}, u32[]{:S(2)}, u32[]{:S(2)}) collective-permute-start(f32[24,2048]{1,0:T(8,128)S(1)} %get-tuple-element.109), channel_id=1, source_target_pairs={{0,0},{15,15},{1,2},{2,1},{3,4},{4,3},{5,6},{6,5},{7,8},{8,7},{9,1... | collective-permute-start | bytes 589832 | tf_op jit(solution)/shard_map/ppermute | solution.py:818
  11.3 5.8 %diag_build.1 = (bf16[2,8,256,512]{3,2,1,0:T(8,128)(2,1)S(1)}, f32[2,16,2048]{2,1,0:T(8,128)S(1)}) custom-call(s32[24,128]{1,0:T(8,128)S(4)} %get-tuple-element.106.tab, f32[2,24,2048]{2,1,0:T(8,128)S(1)} %get-tuple-element.105.side.w, bf16[2,2048,64]{2,1,0:T(8,128)(2,1)S(1)} %get-tuple-element.107.lhs), custom_call_target="tpu_custom_call" | custom-call | flops 3000000000 | bytes 1048576 | tf_op jit(solution)/shard_map/diag_build/pallas_call | solution.py:467
  17.1 5.9 %halo_build.1 = (bf16[8,256,768]{2,1,0:T(8,128)(2,1)S(1)}, bf16[8,256,128]{2,1,0:T(8,128)(2,1)S(1)}, s32[8,128]{1,0:T(8,128)S(4)}, f32[2,16,2048]{2,1,0:T(8,128)...) custom-call(s32[6]{0:T(128)S(4)} %get-tuple-element.104.flags, f32[2,24,2048]{2,1,0:T(8,128)S(1)} %get-tuple-element.105.side.w, ...), custom_call_target="tpu_custom_call" | custom-call | flops 3000000000 | bytes 1048576 | tf_op jit(solution)/shard_map/halo_build/pallas_call | solution.py:467
  23.0 2.8 %collective-permute-start.24 = (f32[16,2048]{1,0:T(8,128)S(1)}, f32[16,2048]{1,0:T(8,128)S(1)}, u32[]{:S(2)}, u32[]{:S(2)}) collective-permute-start(f32[16,2048]{1,0:T(8,128)S(1)} %get-tuple-element.118), channel_id=1, source_target_pairs={{0,1},{1,0},{2,3},{3,2},{4,5},{5,4},{6,7},{7,6},{8,9},{9,8},{10,11... | collective-permute-start | bytes 393224 | tf_op jit(solution)/shard_map/ppermute | solution.py:816
  25.9 0.7 %collective-permute-start.25 = (f32[16,2048]{1,0:T(8,128)S(1)}, f32[16,2048]{1,0:T(8,128)S(1)}, u32[]{:S(2)}, u32[]{:S(2)}) collective-permute-start(f32[16,2048]{1,0:T(8,128)S(1)} %get-tuple-element.118), channel_id=1, source_target_pairs={{0,0},{15,15},{1,2},{2,1},{3,4},{4,3},{5,6},{6,5},{7,8},{8,7},{9,1... | collective-permute-start | bytes 393224 | tf_op jit(solution)/shard_map/ppermute | solution.py:818
  26.5 4.1 %own_build.1 = (bf16[8,256,768]{2,1,0:T(8,128)(2,1)S(1)}, bf16[8,256,128]{2,1,0:T(8,128)(2,1)S(1)}, f32[2,16,2048]{2,1,0:T(8,128)S(1)}) custom-call(s32[24,128]{1,0:T(8,128)S(4)} %get-tuple-element.106.tab, f32[2,24,2048]{2,1,0:T(8,128)S(1)} %get-tuple-element.105.side.w, bf16[2,2048,64]{2,1,0:T(8,128)(2,1)S(1)} %get-tuple-element.107.lhs, ...), custom_call_target="tpu_custom_call" | custom-call | flops 5000000000 | bytes 1048576 | tf_op jit(solution)/shard_map/own_build/pallas_call | solution.py:467
  30.6 1.2 %finish.2 = (f32[2,16,2048]{2,1,0:T(8,128)S(1)}, f32[16,2048]{1,0:T(8,128)S(1)}, f32[16,2048]{1,0:T(8,128)S(1)}, f32[16,128]{1,0:T(8,128)S(1)}) custom-call(s32[6]{0:T(128)S(4)} %get-tuple-element.104.flags, s32[8,128]{1,0:T(8,128)S(4)} %get-tuple-element.114.tab, bf16[8,256,768]{2,1,0:T(8,128)(2,1)S(1)} %get-tuple-element.115.k12, ...), custom_call_target="tpu_custom_call" | custom-call | flops 1000000000 | bytes 1048576 | tf_op jit(solution)/shard_map/finish/pallas_call | solution.py:467
  31.9 2.0 %collective-permute-start.26 = (f32[16,2048]{1,0:T(8,128)S(1)}, f32[16,2048]{1,0:T(8,128)S(1)}, u32[]{:S(2)}, u32[]{:S(2)}) collective-permute-start(f32[16,2048]{1,0:T(8,128)S(1)} %get-tuple-element.120), channel_id=1, source_target_pairs={{0,1},{1,0},{2,3},{3,2},{4,5},{5,4},{6,7},{7,6},{8,9},{9,8},{10,11... | collective-permute-start | bytes 393224 | tf_op jit(solution)/shard_map/ppermute | solution.py:816
  33.9 0.7 %collective-permute-start.27 = (f32[16,2048]{1,0:T(8,128)S(1)}, f32[16,2048]{1,0:T(8,128)S(1)}, u32[]{:S(2)}, u32[]{:S(2)}) collective-permute-start(f32[16,2048]{1,0:T(8,128)S(1)} %get-tuple-element.121), channel_id=1, source_target_pairs={{0,0},{15,15},{1,2},{2,1},{3,4},{4,3},{5,6},{6,5},{7,8},{8,7},{9,1... | collective-permute-start | bytes 393224 | tf_op jit(solution)/shard_map/ppermute | solution.py:818
  34.6 3.3 %own_apply.2.acc_in = f32[2,16,2048]{2,1,0:T(8,128)S(1)} custom-call(s32[24,128]{1,0:T(8,128)S(4)} %get-tuple-element.106.tab, bf16[2,8,256,512]{3,2,1,0:T(8,128)(2,1)S(1)} %get-tuple-element.108.kd, bf16[8,256,768]{2,1,0:T(8,128)(2,1)S(1)} %get-tuple-element.112.k01, bf16[8,256,128]{2,1,0:T(8,128)(2,1)S(1)} %get-tuple-element.113.x01, ...), custom_call_target="tpu_custom_call" | custom-call | flops 2000000000 | bytes 1048576 | tf_op jit(solution)/shard_map/own_apply/pallas_call | solution.py:467
  37.9 2.6 %finish.3 = (f32[2,16,2048]{2,1,0:T(8,128)S(1)}, f32[16,2048]{1,0:T(8,128)S(1)}, f32[16,2048]{1,0:T(8,128)S(1)}, f32[16,128]{1,0:T(8,128)S(1)}) custom-call(s32[6]{0:T(128)S(4)} %get-tuple-element.104.flags, s32[8,128]{1,0:T(8,128)S(4)} %get-tuple-element.114.tab, bf16[8,256,768]{2,1,0:T(8,128)(2,1)S(1)} %get-tuple-element.115.k12, ...), custom_call_target="tpu_custom_call" | custom-call | flops 1000000000 | bytes 1048576 | tf_op jit(solution)/shard_map/finish/pallas_call | solution.py:467
  40.5 2.4 %collective-permute-start.28 = (f32[16,2048]{1,0:T(8,128)S(1)}, f32[16,2048]{1,0:T(8,128)S(1)}, u32[]{:S(2)}, u32[]{:S(2)}) collective-permute-start(f32[16,2048]{1,0:T(8,128)S(1)} %get-tuple-element.125), channel_id=1, source_target_pairs={{0,1},{1,0},{2,3},{3,2},{4,5},{5,4},{6,7},{7,6},{8,9},{9,8},{10,11... | collective-permute-start | bytes 393224 | tf_op jit(solution)/shard_map/ppermute | solution.py:816
  42.9 0.7 %collective-permute-start.29 = (f32[16,2048]{1,0:T(8,128)S(1)}, f32[16,2048]{1,0:T(8,128)S(1)}, u32[]{:S(2)}, u32[]{:S(2)}) collective-permute-start(f32[16,2048]{1,0:T(8,128)S(1)} %get-tuple-element.126), channel_id=1, source_target_pairs={{0,0},{15,15},{1,2},{2,1},{3,4},{4,3},{5,6},{6,5},{7,8},{8,7},{9,1... | collective-permute-start | bytes 393224 | tf_op jit(solution)/shard_map/ppermute | solution.py:818
  43.6 3.3 %own_apply.3.acc = f32[2,16,2048]{2,1,0:T(8,128)S(1)} custom-call(s32[24,128]{1,0:T(8,128)S(4)} %get-tuple-element.106.tab, bf16[2,8,256,512]{3,2,1,0:T(8,128)(2,1)S(1)} %get-tuple-element.108.kd, bf16[8,256,768]{2,1,0:T(8,128)(2,1)S(1)} %get-tuple-element.112.k01, bf16[8,256,128]{2,1,0:T(8,128)(2,1)S(1)} %get-tuple-element.113.x01, ...), custom_call_target="tpu_custom_call" | custom-call | flops 2000000000 | bytes 1048576 | tf_op jit(solution)/shard_map/own_apply/pallas_call | solution.py:467
  47.1 4.9 %collective-permute-start.31 = (f32[16,128]{1,0:T(8,128)S(1)}, f32[16,128]{1,0:T(8,128)S(1)}, u32[]{:S(2)}, u32[]{:S(2)}) collective-permute-start(f32[16,128]{1,0:T(8,128)S(1)} %moment.1), channel_id=1, source_target_pairs={{0,2},{1,3},{2,0},{3,1},{4,6},{5,7},{6,4},{7,5},{8,10},{9,11},{10,... | collective-permute-start | bytes 24584 | tf_op jit(solution)/shard_map/ppermute | solution.py:830
  52.0 1.1 %collective-permute-start.32 = (f32[16,128]{1,0:T(8,128)S(1)}, f32[16,128]{1,0:T(8,128)S(1)}, u32[]{:S(2)}, u32[]{:S(2)}) collective-permute-start(f32[16,128]{1,0:T(8,128)S(1)} %moment.1), channel_id=1, source_target_pairs={{0,3},{1,2},{2,1},{3,0},{4,7},{5,6},{6,5},{7,4},{8,11},{9,10},{10,... | collective-permute-start | bytes 24584 | tf_op jit(solution)/shard_map/ppermute | solution.py:830
  53.1 1.7 %last.1.wc = f32[2,16,2048]{2,1,0:T(8,128)S(1)} custom-call(s32[6]{0:T(128)S(4)} %get-tuple-element.104.flags, s32[8,128]{1,0:T(8,128)S(4)} %get-tuple-element.114.tab, bf16[8,256,768]{2,1,0:T(8,128)(2,1)S(1)} %get-tuple-element.115.k12, bf16[8,256,128]{2,1,0:T(8,128)(2,1)S(1)} %get-tuple-element.116.x12, f32[2,24,2048]{2,1,0:T(8,128)S(1)} %get-tuple-element.105.side.w, ...), custom_call_target="tpu_custom_call" | custom-call | flops 1000000000 | bytes 1048576 | tf_op jit(solution)/shard_map/last/pallas_call | solution.py:467
  55.1 3.4 %collective-permute-start.34 = (f32[16,128]{1,0:T(8,128)S(1)}, f32[16,128]{1,0:T(8,128)S(1)}, u32[]{:S(2)}, u32[]{:S(2)}) collective-permute-start(f32[16,128]{1,0:T(8,128)S(1)} %add_add_fusion.7), channel_id=1, source_target_pairs={{0,8},{1,9},{2,10},{3,11},{4,12},{5,13},{6,14},{7,15},{8,0},{9,1},... | collective-permute-start | bytes 24584 | tf_op jit(solution)/shard_map/ppermute | solution.py:830
  58.5 0.9 %collective-permute-start.35 = (f32[16,128]{1,0:T(8,128)S(1)}, f32[16,128]{1,0:T(8,128)S(1)}, u32[]{:S(2)}, u32[]{:S(2)}) collective-permute-start(f32[16,128]{1,0:T(8,128)S(1)} %add_add_fusion.7), channel_id=1, source_target_pairs={{0,12},{1,13},{2,14},{3,15},{4,8},{5,9},{6,10},{7,11},{8,4},{9,5},... | collective-permute-start | bytes 24584 | tf_op jit(solution)/shard_map/ppermute | solution.py:830
  59.6 2.4 %unsort.1 = f32[48,4096]{1,0:T(8,128)S(1)} custom-call(s32[2,1,2048]{2,1,0:T(1,128)S(1)} %get-tuple-element.129.rank, f32[2,16,2048]{2,1,0:T(8,128)S(1)} %get-tuple-element.122.w.wa, f32[2,16,2048]{2,1,0:T(8,128)S(1)} %get-tuple-element.124.w.wb, f32[2,16,2048]{2,1,0:T(8,128)S(1)} %last.1.wc), custom_call_target="tpu_custom_call" | custom-call | flops 1610612736 | bytes 1048576 | tf_op jit(solution)/shard_map/unsort/pallas_call | solution.py:467
  62.0 1.9 %collective-permute-done.35 = f32[16,128]{1,0:T(8,128)S(1)} collective-permute-done((f32[16,128]{1,0:T(8,128)S(1)}, f32[16,128]{1,0:T(8,128)S(1)}, u32[]{:S(2)}, u32[]{:S(2)}) %collective-permute-start.35) | collective-permute-done | bytes 8224 | tf_op jit(solution)/shard_map/ppermute | solution.py:830
  64.1 1.0 %conditional.1 = ((f32[16,4096]{1,0:T(8,128)}, f32[16,4096]{1,0:T(8,128)})) conditional(s32[]{:T(128)} %bitcast.3, (f32[2,24,2048]{2,1,0:T(8,128)S(1)}, s32[6]{0:T(128)S(4)}, f32[24,2048]{1,0:T(8,128)S(1)}, s32[2,1,2048]{2,1,0:T(1,128)S(1)}) %tuple.17, (f32[16,128]{1,0:T(8,128)S(1)}, f32[16,4096]{1,0:T(8,128)S(1)}, f32[48,4096]{1,0:T(8,128)S(1)}) %tuple.18), branch_computations={%region_0.0_spmd, %region_3.0_spmd} | conditional | flops 60036864 | bytes 11600933 | solution.py:969
  64.2 1.0 %combine.1 = (f32[16,4096]{1,0:T(8,128)}, f32[16,4096]{1,0:T(8,128)}) custom-call(f32[16,128]{1,0:T(8,128)S(1)} %get-tuple-element.71.steps, f32[16,4096]{1,0:T(8,128)S(1)} %get-tuple-element.72.probes, f32[48,4096]{1,0:T(8,128)S(1)} %get-tuple-element.73.u), custom_call_target="tpu_custom_call" | custom-call | flops 1000000 | bytes 1048576 | tf_op jit(solution)/shard_map/cond/branch_1_fun/combine/pallas_call | solution.py:467
  (21 shorter events, 1.4 us)
Async XLA Ops:
  10.2 7.0 %collective-permute-start.22 = (f32[24,2048]{1,0:T(8,128)S(1)}, f32[24,2048]{1,0:T(8,128)S(1)}, u32[]{:S(2)}, u32[]{:S(2)}) collective-permute-start(f32[24,2048]{1,0:T(8,128)S(1)} %get-tuple-element.109), channel_id=1, source_target_pairs={{0,1},{1,0},{2,3},{3,2},{4,5},{5,4},{6,7},{7,6},{8,9},{9,8},{10,11... | collective-permute-start | bytes 589832 | tf_op jit(solution)/shard_map/ppermute | solution.py:816
  10.7 6.5 %collective-permute-start.23 = (f32[24,2048]{1,0:T(8,128)S(1)}, f32[24,2048]{1,0:T(8,128)S(1)}, u32[]{:S(2)}, u32[]{:S(2)}) collective-permute-start(f32[24,2048]{1,0:T(8,128)S(1)} %get-tuple-element.109), channel_id=1, source_target_pairs={{0,0},{15,15},{1,2},{2,1},{3,4},{4,3},{5,6},{6,5},{7,8},{8,7},{9,1... | collective-permute-start | bytes 589832 | tf_op jit(solution)/shard_map/ppermute | solution.py:818
  23.0 7.6 %collective-permute-start.24 = (f32[16,2048]{1,0:T(8,128)S(1)}, f32[16,2048]{1,0:T(8,128)S(1)}, u32[]{:S(2)}, u32[]{:S(2)}) collective-permute-start(f32[16,2048]{1,0:T(8,128)S(1)} %get-tuple-element.118), channel_id=1, source_target_pairs={{0,1},{1,0},{2,3},{3,2},{4,5},{5,4},{6,7},{7,6},{8,9},{9,8},{10,11... | collective-permute-start | bytes 393224 | tf_op jit(solution)/shard_map/ppermute | solution.py:816
  25.9 4.8 %collective-permute-start.25 = (f32[16,2048]{1,0:T(8,128)S(1)}, f32[16,2048]{1,0:T(8,128)S(1)}, u32[]{:S(2)}, u32[]{:S(2)}) collective-permute-start(f32[16,2048]{1,0:T(8,128)S(1)} %get-tuple-element.118), channel_id=1, source_target_pairs={{0,0},{15,15},{1,2},{2,1},{3,4},{4,3},{5,6},{6,5},{7,8},{8,7},{9,1... | collective-permute-start | bytes 393224 | tf_op jit(solution)/shard_map/ppermute | solution.py:818
  31.9 6.0 %collective-permute-start.26 = (f32[16,2048]{1,0:T(8,128)S(1)}, f32[16,2048]{1,0:T(8,128)S(1)}, u32[]{:S(2)}, u32[]{:S(2)}) collective-permute-start(f32[16,2048]{1,0:T(8,128)S(1)} %get-tuple-element.120), channel_id=1, source_target_pairs={{0,1},{1,0},{2,3},{3,2},{4,5},{5,4},{6,7},{7,6},{8,9},{9,8},{10,11... | collective-permute-start | bytes 393224 | tf_op jit(solution)/shard_map/ppermute | solution.py:816
  33.9 4.0 %collective-permute-start.27 = (f32[16,2048]{1,0:T(8,128)S(1)}, f32[16,2048]{1,0:T(8,128)S(1)}, u32[]{:S(2)}, u32[]{:S(2)}) collective-permute-start(f32[16,2048]{1,0:T(8,128)S(1)} %get-tuple-element.121), channel_id=1, source_target_pairs={{0,0},{15,15},{1,2},{2,1},{3,4},{4,3},{5,6},{6,5},{7,8},{8,7},{9,1... | collective-permute-start | bytes 393224 | tf_op jit(solution)/shard_map/ppermute | solution.py:818
  40.5 6.4 %collective-permute-start.28 = (f32[16,2048]{1,0:T(8,128)S(1)}, f32[16,2048]{1,0:T(8,128)S(1)}, u32[]{:S(2)}, u32[]{:S(2)}) collective-permute-start(f32[16,2048]{1,0:T(8,128)S(1)} %get-tuple-element.125), channel_id=1, source_target_pairs={{0,1},{1,0},{2,3},{3,2},{4,5},{5,4},{6,7},{7,6},{8,9},{9,8},{10,11... | collective-permute-start | bytes 393224 | tf_op jit(solution)/shard_map/ppermute | solution.py:816
  42.9 4.0 %collective-permute-start.29 = (f32[16,2048]{1,0:T(8,128)S(1)}, f32[16,2048]{1,0:T(8,128)S(1)}, u32[]{:S(2)}, u32[]{:S(2)}) collective-permute-start(f32[16,2048]{1,0:T(8,128)S(1)} %get-tuple-element.126), channel_id=1, source_target_pairs={{0,0},{15,15},{1,2},{2,1},{3,4},{4,3},{5,6},{6,5},{7,8},{8,7},{9,1... | collective-permute-start | bytes 393224 | tf_op jit(solution)/shard_map/ppermute | solution.py:818
  47.1 7.7 %collective-permute-start.31 = (f32[16,128]{1,0:T(8,128)S(1)}, f32[16,128]{1,0:T(8,128)S(1)}, u32[]{:S(2)}, u32[]{:S(2)}) collective-permute-start(f32[16,128]{1,0:T(8,128)S(1)} %moment.1), channel_id=1, source_target_pairs={{0,2},{1,3},{2,0},{3,1},{4,6},{5,7},{6,4},{7,5},{8,10},{9,11},{10,... | collective-permute-start | bytes 24584 | tf_op jit(solution)/shard_map/ppermute | solution.py:830
  52.0 3.1 %collective-permute-start.32 = (f32[16,128]{1,0:T(8,128)S(1)}, f32[16,128]{1,0:T(8,128)S(1)}, u32[]{:S(2)}, u32[]{:S(2)}) collective-permute-start(f32[16,128]{1,0:T(8,128)S(1)} %moment.1), channel_id=1, source_target_pairs={{0,3},{1,2},{2,1},{3,0},{4,7},{5,6},{6,5},{7,4},{8,11},{9,10},{10,... | collective-permute-start | bytes 24584 | tf_op jit(solution)/shard_map/ppermute | solution.py:830
  53.0 2.0 %collective-permute-start.30 = (f32[16,128]{1,0:T(8,128)S(1)}, f32[16,128]{1,0:T(8,128)S(1)}, u32[]{:S(2)}, u32[]{:S(2)}) collective-permute-start(f32[16,128]{1,0:T(8,128)S(1)} %moment.1), channel_id=1, source_target_pairs={{0,1},{1,0},{2,3},{3,2},{4,5},{5,4},{6,7},{7,6},{8,9},{9,8},{10,11... | collective-permute-start | bytes 24584 | tf_op jit(solution)/shard_map/ppermute | solution.py:830
  55.1 6.9 %collective-permute-start.34 = (f32[16,128]{1,0:T(8,128)S(1)}, f32[16,128]{1,0:T(8,128)S(1)}, u32[]{:S(2)}, u32[]{:S(2)}) collective-permute-start(f32[16,128]{1,0:T(8,128)S(1)} %add_add_fusion.7), channel_id=1, source_target_pairs={{0,8},{1,9},{2,10},{3,11},{4,12},{5,13},{6,14},{7,15},{8,0},{9,1},... | collective-permute-start | bytes 24584 | tf_op jit(solution)/shard_map/ppermute | solution.py:830
  58.5 5.4 %collective-permute-start.35 = (f32[16,128]{1,0:T(8,128)S(1)}, f32[16,128]{1,0:T(8,128)S(1)}, u32[]{:S(2)}, u32[]{:S(2)}) collective-permute-start(f32[16,128]{1,0:T(8,128)S(1)} %add_add_fusion.7), channel_id=1, source_target_pairs={{0,12},{1,13},{2,14},{3,15},{4,8},{5,9},{6,10},{7,11},{8,4},{9,5},... | collective-permute-start | bytes 24584 | tf_op jit(solution)/shard_map/ppermute | solution.py:830
  59.3 4.6 %collective-permute-start.33 = (f32[16,128]{1,0:T(8,128)S(1)}, f32[16,128]{1,0:T(8,128)S(1)}, u32[]{:S(2)}, u32[]{:S(2)}) collective-permute-start(f32[16,128]{1,0:T(8,128)S(1)} %add_add_fusion.7), channel_id=1, source_target_pairs={{0,4},{1,5},{2,6},{3,7},{4,0},{5,1},{6,2},{7,3},{8,12},{9,13},{10,... | collective-permute-start | bytes 24584 | tf_op jit(solution)/shard_map/ppermute | solution.py:830

commit v5 on v2

--- a/solution.py
+++ b/solution.py
@@ -609,7 +609,7 @@
     halo_product(tab, k12, x12, side, halo, halo_w, tile, v2, new.at[1])
 
 
-def unsort(rank, fields, store, repeat):
+def unsort(rank, fields, store, repeat, only=None):
     def block(blk, carry):
         stacked = jnp.concatenate([split2(field[blk]) for field in fields], axis=0)
         place = places()
@@ -621,21 +621,24 @@
                 part = nn(stacked[:, g * STRIP : (g + 1) * STRIP], one_hot(marks(piece, g), place))
                 got = part if got is None else got + part
             size = 2 * N_PROBES
-            store(blk, at(blk * STRIPS + c, STRIP), [halves(got[size * k : size * (k + 1)]) for k in range(len(fields))])
+            store(blk, at(c if only is not None else blk * STRIPS + c, STRIP), [halves(got[size * k : size * (k + 1)]) for k in range(len(fields))])
             return carry
 
         repeat(STRIPS, strip)
         return carry
 
-    repeat(2, block)
-
-
-def unsort_kernel(rank, wa, wb, wc, out):
+    if only is None:
+        repeat(2, block)
+    else:
+        block(only, 0)
+
+
+def unsort_kernel(only, rank, wa, wb, wc, out):
     def store(blk, cols, values):
         for k, value in enumerate(values):
             out[16 * k : 16 * (k + 1), cols] = value
 
-    unsort(rank, (wa, wb, wc), store, each)
+    unsort(rank, (wa, wb, wc), store, each, only)
 
 
 def steps_kernel(mom, out, sound):
@@ -682,12 +685,13 @@
     out[...] = table
 
 
-def combine_kernel(steps, probes, u, sol, res):
+def combine_kernel(steps, probes, u0, u1, sol, res):
     c = [steps[:, k : k + 1] for k in range(7)]
 
     def part(b, carry):
         here = at(b, BLK)
-        w = [probes[:, here], u[0:16, here], u[16:32, here], u[32:48, here]]
+        u = (u0, u1)[b]
+        w = [probes[:, here], u[0:16, :], u[16:32, :], u[32:48, :]]
         sol[:, here] = (c[0] * w[0] + c[1] * w[1]) + c[2] * w[2]
         res[:, here] = ((c[3] * w[0] + c[4] * w[1]) + c[5] * w[2]) + c[6] * w[3]
         return carry
@@ -928,15 +932,18 @@
             flags, tab12, k12, x12, side, halo, *got, acc, w
         )
     )
-    given = call(
-        unsort_kernel,
-        pltpu.VMEM((3 * N_PROBES, 2 * BLK), f32),
-        [VMEM] * 4,
-        VMEM,
-        [],
-        4 * 96 * BLK * BLK,
-        "unsort",
-    )(rank, *kept)
+    given = [
+        call(
+            functools.partial(unsort_kernel, b),
+            pltpu.VMEM((3 * N_PROBES, BLK), f32),
+            [VMEM] * 4,
+            VMEM,
+            [],
+            2 * 96 * BLK * BLK,
+            "unsort",
+        )(rank, *kept)
+        for b in range(2)
+    ]
     steps, sound = call(
         steps_kernel,
         (moments, pltpu.SMEM((1,), jnp.int32)),
@@ -950,7 +957,7 @@
     def from_basis():
         out = jax.ShapeDtypeStruct(shape, f32)
         return tuple(
-            call(combine_kernel, (out, out), [VMEM] * 3, (VMEM, VMEM), [], 10**6, "combine")(steps, probes, given)
+            call(combine_kernel, (out, out), [VMEM] * 4, (VMEM, VMEM), [], 10**6, "combine")(steps, probes, *given)
         )
 
     def from_start():

time: 65.8 us -> 67 us (1.018)
  Pallas kernels: 37.7 us -> 40.4 us
  starting transfers between devices: 23.6 us -> 22 us
    pallas_call x13 -> x14, Pallas kernels: 37.7 us -> 40.4 us  [run(): pl.pallas_call(body, out_shape=outs, in_specs=ins, out_specs=out_specs, s...]
    ppermute x4, starting transfers between devices: 9.86 us -> 8.86 us  [swapped_both(): a = lax.ppermute(to_a, 'gx', [(k, k ^ 1) for k in range(count)])]
  transfers between devices with their start and end apart: 14 -> 14, of which waited for: 2 -> 2; matrix products, arithmetic and copies ran while one was open for 0% -> 0% of each run, Pallas kernels for 30% -> 32%
where the time goes in v5:
time: 67 us; the launch traced here: 65.7 us
  Pallas kernels  40.4 us (60%)
  starting transfers between devices  22 us (33%)
  waiting for transfers between devices  1.78 us (3%)
  between operations  1.46 us (2%)
    pallas_call x14, Pallas kernels, run(): pl.pallas_call(body, out_shape=outs, in_specs=ins, out_specs=out_specs, s...  40.4 us
    ppermute x6, starting transfers between devices, sum_over(): lax.ppermute(value, axis, [(k, k ^ m * step) for k in range(count)])  10.5 us
    ppermute x4, starting transfers between devices, swapped_both(): a = lax.ppermute(to_a, 'gx', [(k, k ^ 1) for k in range(count)])  8.86 us
    ppermute x4, starting transfers between devices, swapped_both(): lax.ppermute(to_b, 'gx', ends + [(k, (k + 1 ^ 1) - 1) for k in range(1, c...  2.63 us
    ppermute x6, waiting for transfers between devices, sum_over(): lax.ppermute(value, axis, [(k, k ^ m * step) for k in range(count)])  1.75 us
  transfers between devices with their start and end apart: 14, of which 2 were waited for; matrix products, arithmetic and copies ran while one was open for 0% of the time, Pallas kernels for 32%

profile of v5, /device:TPU:0, one launch (start us, length us, event | category | flops | bytes accessed | tf_op | source)
XLA Modules:
  0.0 65.7 jit_solution(11262798744584578666)
XLA Ops:
  1.3 8.9 %sort_blocks.1 = (f32[2,24,2048]{2,1,0:T(8,128)S(1)}, f32[24,2048]{1,0:T(8,128)S(1)}, bf16[2,2048,64]{2,1,0:T(8,128)(2,1)S(1)}, s32[2,1,2048]{2,1,0:T(1,128)S(1)...) custom-call(f32[3,4096]{1,0:T(4,128)} %pts_hbm.1, f32[1,4096]{1,0:T(1,128)} %bitcast.7, ...), custom_call_target="tpu_custom_call" | custom-call | flops 1000000000 | bytes 1048576 | tf_op jit(solution)/shard_map/sort_blocks/pallas_call | solution.py:457
  10.7 0.7 %collective-permute-start.23 = (f32[24,2048]{1,0:T(8,128)S(1)}, f32[24,2048]{1,0:T(8,128)S(1)}, u32[]{:S(2)}, u32[]{:S(2)}) collective-permute-start(f32[24,2048]{1,0:T(8,128)S(1)} %get-tuple-element.112), channel_id=1, source_target_pairs={{0,0},{15,15},{1,2},{2,1},{3,4},{4,3},{5,6},{6,5},{7,8},{8,7},{9,1... | collective-permute-start | bytes 589832 | tf_op jit(solution)/shard_map/ppermute | solution.py:812
  11.3 5.8 %diag_build.1 = (bf16[2,8,256,512]{3,2,1,0:T(8,128)(2,1)S(1)}, f32[2,16,2048]{2,1,0:T(8,128)S(1)}) custom-call(s32[24,128]{1,0:T(8,128)S(4)} %get-tuple-element.109.tab, f32[2,24,2048]{2,1,0:T(8,128)S(1)} %get-tuple-element.108.side.w, bf16[2,2048,64]{2,1,0:T(8,128)(2,1)S(1)} %get-tuple-element.110.lhs), custom_call_target="tpu_custom_call" | custom-call | flops 3000000000 | bytes 1048576 | tf_op jit(solution)/shard_map/diag_build/pallas_call | solution.py:457
  17.2 5.6 %halo_build.1 = (bf16[8,256,768]{2,1,0:T(8,128)(2,1)S(1)}, bf16[8,256,128]{2,1,0:T(8,128)(2,1)S(1)}, s32[8,128]{1,0:T(8,128)S(4)}, f32[2,16,2048]{2,1,0:T(8,128)...) custom-call(s32[6]{0:T(128)S(4)} %get-tuple-element.107.flags, f32[2,24,2048]{2,1,0:T(8,128)S(1)} %get-tuple-element.108.side.w, ...), custom_call_target="tpu_custom_call" | custom-call | flops 3000000000 | bytes 1048576 | tf_op jit(solution)/shard_map/halo_build/pallas_call | solution.py:457
  22.7 3.2 %collective-permute-start.24 = (f32[16,2048]{1,0:T(8,128)S(1)}, f32[16,2048]{1,0:T(8,128)S(1)}, u32[]{:S(2)}, u32[]{:S(2)}) collective-permute-start(f32[16,2048]{1,0:T(8,128)S(1)} %get-tuple-element.121), channel_id=1, source_target_pairs={{0,1},{1,0},{2,3},{3,2},{4,5},{5,4},{6,7},{7,6},{8,9},{9,8},{10,11... | collective-permute-start | bytes 393224 | tf_op jit(solution)/shard_map/ppermute | solution.py:810
  25.9 0.7 collective-permute-start.25
  26.6 4.4 %own_build.1 = (bf16[8,256,768]{2,1,0:T(8,128)(2,1)S(1)}, bf16[8,256,128]{2,1,0:T(8,128)(2,1)S(1)}, f32[2,16,2048]{2,1,0:T(8,128)S(1)}) custom-call(s32[24,128]{1,0:T(8,128)S(4)} %get-tuple-element.109.tab, f32[2,24,2048]{2,1,0:T(8,128)S(1)} %get-tuple-element.108.side.w, bf16[2,2048,64]{2,1,0:T(8,128)(2,1)S(1)} %get-tuple-element.110.lhs, ...), custom_call_target="tpu_custom_call" | custom-call | flops 5000000000 | bytes 1048576 | tf_op jit(solution)/shard_map/own_build/pallas_call | solution.py:457
  31.0 1.1 %finish.2 = (f32[2,16,2048]{2,1,0:T(8,128)S(1)}, f32[16,2048]{1,0:T(8,128)S(1)}, f32[16,2048]{1,0:T(8,128)S(1)}, f32[16,128]{1,0:T(8,128)S(1)}) custom-call(s32[6]{0:T(128)S(4)} %get-tuple-element.107.flags, s32[8,128]{1,0:T(8,128)S(4)} %get-tuple-element.117.tab, bf16[8,256,768]{2,1,0:T(8,128)(2,1)S(1)} %get-tuple-element.118.k12, ...), custom_call_target="tpu_custom_call" | custom-call | flops 1000000000 | bytes 1048576 | tf_op jit(solution)/shard_map/finish/pallas_call | solution.py:457
  32.1 2.6 %collective-permute-start.26 = (f32[16,2048]{1,0:T(8,128)S(1)}, f32[16,2048]{1,0:T(8,128)S(1)}, u32[]{:S(2)}, u32[]{:S(2)}) collective-permute-start(f32[16,2048]{1,0:T(8,128)S(1)} %get-tuple-element.123), channel_id=1, source_target_pairs={{0,1},{1,0},{2,3},{3,2},{4,5},{5,4},{6,7},{7,6},{8,9},{9,8},{10,11... | collective-permute-start | bytes 393224 | tf_op jit(solution)/shard_map/ppermute | solution.py:810
  34.7 0.7 collective-permute-start.27
  35.4 3.5 %own_apply.2.acc_in = f32[2,16,2048]{2,1,0:T(8,128)S(1)} custom-call(s32[24,128]{1,0:T(8,128)S(4)} %get-tuple-element.109.tab, bf16[2,8,256,512]{3,2,1,0:T(8,128)(2,1)S(1)} %get-tuple-element.111.kd, bf16[8,256,768]{2,1,0:T(8,128)(2,1)S(1)} %get-tuple-element.115.k01, bf16[8,256,128]{2,1,0:T(8,128)(2,1)S(1)} %get-tuple-element.116.x01, ...), custom_call_target="tpu_custom_call" | custom-call | flops 2000000000 | bytes 1048576 | tf_op jit(solution)/shard_map/own_apply/pallas_call | solution.py:457
  38.9 2.3 %finish.3 = (f32[2,16,2048]{2,1,0:T(8,128)S(1)}, f32[16,2048]{1,0:T(8,128)S(1)}, f32[16,2048]{1,0:T(8,128)S(1)}, f32[16,128]{1,0:T(8,128)S(1)}) custom-call(s32[6]{0:T(128)S(4)} %get-tuple-element.107.flags, s32[8,128]{1,0:T(8,128)S(4)} %get-tuple-element.117.tab, bf16[8,256,768]{2,1,0:T(8,128)(2,1)S(1)} %get-tuple-element.118.k12, ...), custom_call_target="tpu_custom_call" | custom-call | flops 1000000000 | bytes 1048576 | tf_op jit(solution)/shard_map/finish/pallas_call | solution.py:457
  41.2 2.6 %collective-permute-start.28 = (f32[16,2048]{1,0:T(8,128)S(1)}, f32[16,2048]{1,0:T(8,128)S(1)}, u32[]{:S(2)}, u32[]{:S(2)}) collective-permute-start(f32[16,2048]{1,0:T(8,128)S(1)} %get-tuple-element.128), channel_id=1, source_target_pairs={{0,1},{1,0},{2,3},{3,2},{4,5},{5,4},{6,7},{7,6},{8,9},{9,8},{10,11... | collective-permute-start | bytes 393224 | tf_op jit(solution)/shard_map/ppermute | solution.py:810
  44.5 3.5 %own_apply.3.acc = f32[2,16,2048]{2,1,0:T(8,128)S(1)} custom-call(s32[24,128]{1,0:T(8,128)S(4)} %get-tuple-element.109.tab, bf16[2,8,256,512]{3,2,1,0:T(8,128)(2,1)S(1)} %get-tuple-element.111.kd, bf16[8,256,768]{2,1,0:T(8,128)(2,1)S(1)} %get-tuple-element.115.k01, bf16[8,256,128]{2,1,0:T(8,128)(2,1)S(1)} %get-tuple-element.116.x01, ...), custom_call_target="tpu_custom_call" | custom-call | flops 2000000000 | bytes 1048576 | tf_op jit(solution)/shard_map/own_apply/pallas_call | solution.py:457
  48.1 6.8 %collective-permute-start.31 = (f32[16,128]{1,0:T(8,128)S(1)}, f32[16,128]{1,0:T(8,128)S(1)}, u32[]{:S(2)}, u32[]{:S(2)}) collective-permute-start(f32[16,128]{1,0:T(8,128)S(1)} %moment.1), channel_id=1, source_target_pairs={{0,2},{1,3},{2,0},{3,1},{4,6},{5,7},{6,4},{7,5},{8,10},{9,11},{10,... | collective-permute-start | bytes 24584 | tf_op jit(solution)/shard_map/ppermute | solution.py:824
  55.0 1.5 %last.1.wc = f32[2,16,2048]{2,1,0:T(8,128)S(1)} custom-call(s32[6]{0:T(128)S(4)} %get-tuple-element.107.flags, s32[8,128]{1,0:T(8,128)S(4)} %get-tuple-element.117.tab, bf16[8,256,768]{2,1,0:T(8,128)(2,1)S(1)} %get-tuple-element.118.k12, bf16[8,256,128]{2,1,0:T(8,128)(2,1)S(1)} %get-tuple-element.119.x12, f32[2,24,2048]{2,1,0:T(8,128)S(1)} %get-tuple-element.108.side.w, ...), custom_call_target="tpu_custom_call" | custom-call | flops 1000000000 | bytes 1048576 | tf_op jit(solution)/shard_map/last/pallas_call | solution.py:457
  56.6 1.3 %unsort.2 = f32[48,2048]{1,0:T(8,128)S(1)} custom-call(s32[2,1,2048]{2,1,0:T(1,128)S(1)} %get-tuple-element.132.rank, f32[2,16,2048]{2,1,0:T(8,128)S(1)} %get-tuple-element.125.w.wa, f32[2,16,2048]{2,1,0:T(8,128)S(1)} %get-tuple-element.127.w.wb, f32[2,16,2048]{2,1,0:T(8,128)S(1)} %last.1.wc), custom_call_target="tpu_custom_call" | custom-call | flops 805306368 | bytes 1048576 | tf_op jit(solution)/shard_map/unsort/pallas_call | solution.py:457
  57.9 1.1 %collective-permute-start.34 = (f32[16,128]{1,0:T(8,128)S(1)}, f32[16,128]{1,0:T(8,128)S(1)}, u32[]{:S(2)}, u32[]{:S(2)}) collective-permute-start(f32[16,128]{1,0:T(8,128)S(1)} %add_add_fusion.7), channel_id=1, source_target_pairs={{0,8},{1,9},{2,10},{3,11},{4,12},{5,13},{6,14},{7,15},{8,0},{9,1},... | collective-permute-start | bytes 24584 | tf_op jit(solution)/shard_map/ppermute | solution.py:824
  59.0 1.6 %collective-permute-start.35 = (f32[16,128]{1,0:T(8,128)S(1)}, f32[16,128]{1,0:T(8,128)S(1)}, u32[]{:S(2)}, u32[]{:S(2)}) collective-permute-start(f32[16,128]{1,0:T(8,128)S(1)} %add_add_fusion.7), channel_id=1, source_target_pairs={{0,12},{1,13},{2,14},{3,15},{4,8},{5,9},{6,10},{7,11},{8,4},{9,5},... | collective-permute-start | bytes 24584 | tf_op jit(solution)/shard_map/ppermute | solution.py:824
  60.6 0.9 %collective-permute-start.33 = (f32[16,128]{1,0:T(8,128)S(1)}, f32[16,128]{1,0:T(8,128)S(1)}, u32[]{:S(2)}, u32[]{:S(2)}) collective-permute-start(f32[16,128]{1,0:T(8,128)S(1)} %add_add_fusion.7), channel_id=1, source_target_pairs={{0,4},{1,5},{2,6},{3,7},{4,0},{5,1},{6,2},{7,3},{8,12},{9,13},{10,... | collective-permute-start | bytes 24584 | tf_op jit(solution)/shard_map/ppermute | solution.py:824
  61.5 1.3 %unsort.3 = f32[48,2048]{1,0:T(8,128)S(1)} custom-call(s32[2,1,2048]{2,1,0:T(1,128)S(1)} %get-tuple-element.132.rank, f32[2,16,2048]{2,1,0:T(8,128)S(1)} %get-tuple-element.125.w.wa, f32[2,16,2048]{2,1,0:T(8,128)S(1)} %get-tuple-element.127.w.wb, f32[2,16,2048]{2,1,0:T(8,128)S(1)} %last.1.wc), custom_call_target="tpu_custom_call" | custom-call | flops 805306368 | bytes 1048576 | tf_op jit(solution)/shard_map/unsort/pallas_call | solution.py:457
  62.8 1.7 %collective-permute-done.35 = f32[16,128]{1,0:T(8,128)S(1)} collective-permute-done((f32[16,128]{1,0:T(8,128)S(1)}, f32[16,128]{1,0:T(8,128)S(1)}, u32[]{:S(2)}, u32[]{:S(2)}) %collective-permute-start.35) | collective-permute-done | bytes 8224 | tf_op jit(solution)/shard_map/ppermute | solution.py:824
  64.7 1.0 %conditional.1 = ((f32[16,4096]{1,0:T(8,128)}, f32[16,4096]{1,0:T(8,128)})) conditional(s32[]{:T(128)} %bitcast.3, (f32[2,24,2048]{2,1,0:T(8,128)S(1)}, s32[6]{0:T(128)S(4)}, f32[24,2048]{1,0:T(8,128)S(1)}, s32[2,1,2048]{2,1,0:T(1,128)S(1)}) %tuple.17, (f32[16,128]{1,0:T(8,128)S(1)}, f32[16,4096]{1,0:T(8,128)S(1)}, f32[48,2048]{1,0:T(8,128)S(1)}, ...), branch_computations={%region_0.0_spmd, %region_3.0_spmd} | conditional | flops 60036864 | bytes 11600933 | solution.py:966
  64.7 1.0 %combine.1 = (f32[16,4096]{1,0:T(8,128)}, f32[16,4096]{1,0:T(8,128)}) custom-call(f32[16,128]{1,0:T(8,128)S(1)} %get-tuple-element.73.steps, f32[16,4096]{1,0:T(8,128)S(1)} %get-tuple-element.74.probes, f32[48,2048]{1,0:T(8,128)S(1)} %get-tuple-element.75.u0, f32[48,2048]{1,0:T(8,128)S(1)} %get-tuple-element.76.u1), custom_call_target="tpu_custom_call" | custom-call | flops 1000000 | bytes 1048576 | tf_op jit(solution)/shard_map/cond/branch_1_fun/combine/pallas_call | solution.py:457
  (22 shorter events, 1.8 us)
Async XLA Ops:
  10.2 7.0 %collective-permute-start.22 = (f32[24,2048]{1,0:T(8,128)S(1)}, f32[24,2048]{1,0:T(8,128)S(1)}, u32[]{:S(2)}, u32[]{:S(2)}) collective-permute-start(f32[24,2048]{1,0:T(8,128)S(1)} %get-tuple-element.112), channel_id=1, source_target_pairs={{0,1},{1,0},{2,3},{3,2},{4,5},{5,4},{6,7},{7,6},{8,9},{9,8},{10,11... | collective-permute-start | bytes 589832 | tf_op jit(solution)/shard_map/ppermute | solution.py:810
  10.7 6.5 %collective-permute-start.23 = (f32[24,2048]{1,0:T(8,128)S(1)}, f32[24,2048]{1,0:T(8,128)S(1)}, u32[]{:S(2)}, u32[]{:S(2)}) collective-permute-start(f32[24,2048]{1,0:T(8,128)S(1)} %get-tuple-element.112), channel_id=1, source_target_pairs={{0,0},{15,15},{1,2},{2,1},{3,4},{4,3},{5,6},{6,5},{7,8},{8,7},{9,1... | collective-permute-start | bytes 589832 | tf_op jit(solution)/shard_map/ppermute | solution.py:812
  22.7 8.3 %collective-permute-start.24 = (f32[16,2048]{1,0:T(8,128)S(1)}, f32[16,2048]{1,0:T(8,128)S(1)}, u32[]{:S(2)}, u32[]{:S(2)}) collective-permute-start(f32[16,2048]{1,0:T(8,128)S(1)} %get-tuple-element.121), channel_id=1, source_target_pairs={{0,1},{1,0},{2,3},{3,2},{4,5},{5,4},{6,7},{7,6},{8,9},{9,8},{10,11... | collective-permute-start | bytes 393224 | tf_op jit(solution)/shard_map/ppermute | solution.py:810
  25.9 5.1 %collective-permute-start.25 = (f32[16,2048]{1,0:T(8,128)S(1)}, f32[16,2048]{1,0:T(8,128)S(1)}, u32[]{:S(2)}, u32[]{:S(2)}) collective-permute-start(f32[16,2048]{1,0:T(8,128)S(1)} %get-tuple-element.121), channel_id=1, source_target_pairs={{0,0},{15,15},{1,2},{2,1},{3,4},{4,3},{5,6},{6,5},{7,8},{8,7},{9,1... | collective-permute-start | bytes 393224 | tf_op jit(solution)/shard_map/ppermute | solution.py:812
  32.1 6.7 %collective-permute-start.26 = (f32[16,2048]{1,0:T(8,128)S(1)}, f32[16,2048]{1,0:T(8,128)S(1)}, u32[]{:S(2)}, u32[]{:S(2)}) collective-permute-start(f32[16,2048]{1,0:T(8,128)S(1)} %get-tuple-element.123), channel_id=1, source_target_pairs={{0,1},{1,0},{2,3},{3,2},{4,5},{5,4},{6,7},{7,6},{8,9},{9,8},{10,11... | collective-permute-start | bytes 393224 | tf_op jit(solution)/shard_map/ppermute | solution.py:810
  34.7 4.1 %collective-permute-start.27 = (f32[16,2048]{1,0:T(8,128)S(1)}, f32[16,2048]{1,0:T(8,128)S(1)}, u32[]{:S(2)}, u32[]{:S(2)}) collective-permute-start(f32[16,2048]{1,0:T(8,128)S(1)} %get-tuple-element.124), channel_id=1, source_target_pairs={{0,0},{15,15},{1,2},{2,1},{3,4},{4,3},{5,6},{6,5},{7,8},{8,7},{9,1... | collective-permute-start | bytes 393224 | tf_op jit(solution)/shard_map/ppermute | solution.py:812
  41.2 6.7 %collective-permute-start.28 = (f32[16,2048]{1,0:T(8,128)S(1)}, f32[16,2048]{1,0:T(8,128)S(1)}, u32[]{:S(2)}, u32[]{:S(2)}) collective-permute-start(f32[16,2048]{1,0:T(8,128)S(1)} %get-tuple-element.128), channel_id=1, source_target_pairs={{0,1},{1,0},{2,3},{3,2},{4,5},{5,4},{6,7},{7,6},{8,9},{9,8},{10,11... | collective-permute-start | bytes 393224 | tf_op jit(solution)/shard_map/ppermute | solution.py:810
  43.8 4.1 %collective-permute-start.29 = (f32[16,2048]{1,0:T(8,128)S(1)}, f32[16,2048]{1,0:T(8,128)S(1)}, u32[]{:S(2)}, u32[]{:S(2)}) collective-permute-start(f32[16,2048]{1,0:T(8,128)S(1)} %get-tuple-element.129), channel_id=1, source_target_pairs={{0,0},{15,15},{1,2},{2,1},{3,4},{4,3},{5,6},{6,5},{7,8},{8,7},{9,1... | collective-permute-start | bytes 393224 | tf_op jit(solution)/shard_map/ppermute | solution.py:812
  48.1 9.8 %collective-permute-start.31 = (f32[16,128]{1,0:T(8,128)S(1)}, f32[16,128]{1,0:T(8,128)S(1)}, u32[]{:S(2)}, u32[]{:S(2)}) collective-permute-start(f32[16,128]{1,0:T(8,128)S(1)} %moment.1), channel_id=1, source_target_pairs={{0,2},{1,3},{2,0},{3,1},{4,6},{5,7},{6,4},{7,5},{8,10},{9,11},{10,... | collective-permute-start | bytes 24584 | tf_op jit(solution)/shard_map/ppermute | solution.py:824
  54.9 3.1 %collective-permute-start.32 = (f32[16,128]{1,0:T(8,128)S(1)}, f32[16,128]{1,0:T(8,128)S(1)}, u32[]{:S(2)}, u32[]{:S(2)}) collective-permute-start(f32[16,128]{1,0:T(8,128)S(1)} %moment.1), channel_id=1, source_target_pairs={{0,3},{1,2},{2,1},{3,0},{4,7},{5,6},{6,5},{7,4},{8,11},{9,10},{10,... | collective-permute-start | bytes 24584 | tf_op jit(solution)/shard_map/ppermute | solution.py:824
  54.9 3.1 %collective-permute-start.30 = (f32[16,128]{1,0:T(8,128)S(1)}, f32[16,128]{1,0:T(8,128)S(1)}, u32[]{:S(2)}, u32[]{:S(2)}) collective-permute-start(f32[16,128]{1,0:T(8,128)S(1)} %moment.1), channel_id=1, source_target_pairs={{0,1},{1,0},{2,3},{3,2},{4,5},{5,4},{6,7},{7,6},{8,9},{9,8},{10,11... | collective-permute-start | bytes 24584 | tf_op jit(solution)/shard_map/ppermute | solution.py:824
  57.9 4.8 %collective-permute-start.34 = (f32[16,128]{1,0:T(8,128)S(1)}, f32[16,128]{1,0:T(8,128)S(1)}, u32[]{:S(2)}, u32[]{:S(2)}) collective-permute-start(f32[16,128]{1,0:T(8,128)S(1)} %add_add_fusion.7), channel_id=1, source_target_pairs={{0,8},{1,9},{2,10},{3,11},{4,12},{5,13},{6,14},{7,15},{8,0},{9,1},... | collective-permute-start | bytes 24584 | tf_op jit(solution)/shard_map/ppermute | solution.py:824
  59.0 5.4 %collective-permute-start.35 = (f32[16,128]{1,0:T(8,128)S(1)}, f32[16,128]{1,0:T(8,128)S(1)}, u32[]{:S(2)}, u32[]{:S(2)}) collective-permute-start(f32[16,128]{1,0:T(8,128)S(1)} %add_add_fusion.7), channel_id=1, source_target_pairs={{0,12},{1,13},{2,14},{3,15},{4,8},{5,9},{6,10},{7,11},{8,4},{9,5},... | collective-permute-start | bytes 24584 | tf_op jit(solution)/shard_map/ppermute | solution.py:824
  60.6 3.8 %collective-permute-start.33 = (f32[16,128]{1,0:T(8,128)S(1)}, f32[16,128]{1,0:T(8,128)S(1)}, u32[]{:S(2)}, u32[]{:S(2)}) collective-permute-start(f32[16,128]{1,0:T(8,128)S(1)} %add_add_fusion.7), channel_id=1, source_target_pairs={{0,4},{1,5},{2,6},{3,7},{4,0},{5,1},{6,2},{7,3},{8,12},{9,13},{10,... | collective-permute-start | bytes 24584 | tf_op jit(solution)/shard_map/ppermute | solution.py:824
